TPU v7x, 32 devices: a whole 2x2x4 slice. The times are simulated.
32 devices in a mesh: req: 8 (over z, core), mlp: 4 (over y, x).
Axes of the slice: x: 2, y: 2, z: 4, core: 2. Of those that a mesh axis runs over, the one named last changes fastest.
Arguments:
- hidden_input: bfloat16 [3072, 4096], P('req', 'mlp'), may hold values from -6 to 6
- input_norm_gain: bfloat16 [4096], replicated, may hold values from 0.099609375 to 1.8984375
- query_norm_gain: bfloat16 [128], replicated, may hold values from 0.099609375 to 1.8984375
- key_norm_gain: bfloat16 [128], replicated, may hold values from 0.099609375 to 1.8984375
- query_weight: bfloat16 [4096, 4096], P('req', 'mlp'), may hold values from -0.09375 to 0.09375
- key_value_weight: bfloat16 [4096, 2, 1024], P('req'), may hold values from -0.09375 to 0.09375
- output_weight: bfloat16 [4096, 4, 1024], P('mlp', None, 'req'), may hold values from -0.09375 to 0.09375
- adapter_down_qkv: bfloat16 [16, 48, 4096], P('req', None, 'mlp'), may hold values from -0.09375 to 0.09375
- adapter_down_output: bfloat16 [16, 16, 4096], P('req', None, 'mlp'), may hold values from -0.09375 to 0.09375
- adapter_up_query: bfloat16 [16, 16, 4096], P('req', None, 'mlp'), may hold values from -1.5 to 1.5
- adapter_up_key_value: bfloat16 [16, 16, 2, 1024], P('req'), may hold values from -1.5 to 1.5
- adapter_up_output: bfloat16 [16, 16, 4096], P('req', None, 'mlp'), may hold values from -1.5 to 1.5
- pool: bfloat16 [4096, 2, 1024], P('req'), may hold values from -6 to 6
- lengths: int32 [8, 4], P('req'), may hold values from 1 to 192, 384 in all within a row
- cached_prefix_pages: int32 [8, 4], P('req'), may hold values from 0 to 8
- prefix_page_table: int32 [8, 4, 8], P('req'), may hold values from 0 to 7, each once within a row
- adapter_of_request: int32 [8, 4, 1], P('req'), may hold values from 0 to 15
- adapter_storage: int32 [16], replicated, may hold values from 0 to 15, each once
Outputs:
- attention_update: bfloat16 [3072, 4096], P('req', 'mlp')
- new_cache: bfloat16 [3072, 2, 1024], P('req', None, 'mlp')
Inputs may be any that keep to these rules, and one draw needn't show every extreme that they name: The lengths of one index of req sum to 384, and the longest of them is 192. `prefix_page_table`: each row lists every page of its pool once. `adapter_of_request`: every adapter is used by some request. `adapter_storage`: each slot holds one adapter.
All inputs are finite; a program needn't handle non-finite values.
Results may differ from a plain program's by a relative error of at most 0.035.
Values may be sent and summed in bfloat16 or wider, within the bound.
No kernel may reach another device: no remote copies, remote signals or barrier semaphores. Data moves between devices by JAX's collectives and lax.ppermute only.
A program may use at most 128 MiB of HBM per device.

v0:
```python
import math

import jax
import jax.numpy as jnp
from jax import lax
from jax.sharding import PartitionSpec as P

QUERY_HEADS = 32
KEY_VALUE_HEADS = 8
HEAD_SIZE = 128
ADAPTER_RANK = 16
PAGE = 64


epsilon = 1e-06
rope_base = 1000000.0


def root_mean_scale(values, gain_vec):
    mean_sq = jnp.mean(values * values, axis=-1, keepdims=True)
    return values * lax.rsqrt(mean_sq + epsilon) * gain_vec.astype(jnp.float32)


def rotary_embed(values, token_positions):
    half_width = values.shape[-1] // 2
    inverse_freq = jnp.exp(
        jnp.arange(half_width, dtype=jnp.float32) * (-2.0 / values.shape[-1]) * math.log(rope_base)
    )
    angles = token_positions.astype(jnp.float32)[:, None] * inverse_freq[None, :]
    cosine = jnp.cos(angles)[:, None, :]
    sine_part = jnp.sin(angles)[:, None, :]
    front = values[..., :half_width]
    back = values[..., half_width:]
    return jnp.concatenate(
        [front * cosine - back * sine_part, back * cosine + front * sine_part], axis=-1
    )


def row_tables(lengths_row, prefix_row, page_rows, row_count):
    ends_at = jnp.cumsum(lengths_row)
    starts_at = ends_at - lengths_row
    row_ids = jnp.arange(row_count, dtype=jnp.int32)
    owners = jnp.sum((row_ids[:, None] >= ends_at[None, :]).astype(jnp.int32), axis=1)
    group_members = owners[:, None] == jnp.arange(lengths_row.shape[0], dtype=jnp.int32)[None, :]
    offsets = PAGE * prefix_row[None, :] + row_ids[:, None] - starts_at[None, :]
    token_positions = jnp.sum(jnp.where(group_members, offsets, 0), axis=1)
    page_ids = jnp.arange(page_rows.shape[1], dtype=jnp.int32)
    listed = (page_rows[:, :, None] == page_ids[None, None, :]) & (
        page_ids[None, :, None] < prefix_row[:, None, None]
    )
    page_used = jnp.sum(listed.astype(jnp.float32), axis=1)
    return (owners, group_members, token_positions, page_used)


def apply_adapter(lowrank_inner, group_members, chosen_up):
    masked = lowrank_inner[:, None, :] * group_members.astype(lowrank_inner.dtype)[:, :, None]
    return jnp.einsum("gjr,jrc->gc", masked, chosen_up, preferred_element_type=jnp.float32)


def select_rows(terms, group_members):
    return jnp.sum(terms * group_members.astype(jnp.float32)[:, :, None], axis=1)


def shards(
    hidden_input,
    input_norm_gain,
    query_norm_gain,
    key_norm_gain,
    query_weight,
    key_value_weight,
    output_weight,
    adapter_down_qkv,
    adapter_down_output,
    adapter_up_query,
    adapter_up_key_value,
    adapter_up_output,
    pool,
    lengths,
    cached_prefix_pages,
    prefix_page_table,
    adapter_of_request,
    adapter_storage,
):
    feature_group_count = lax.axis_size("mlp")
    feature_group_index = lax.axis_index("mlp")
    whole = lax.all_gather(hidden_input, "mlp", axis=1, tiled=True)
    row_count, full_width = whole.shape
    normalized_input = root_mean_scale(whole.astype(jnp.float32), input_norm_gain).astype(
        jnp.bfloat16
    )
    owners, group_members, token_positions, page_used = row_tables(
        lengths[0], cached_prefix_pages[0], prefix_page_table[0], row_count
    )
    q_width = query_weight.shape[1]
    query_head_rows = q_width // HEAD_SIZE
    key_value_local = max(1, KEY_VALUE_HEADS // feature_group_count)
    key_value_width = key_value_local * HEAD_SIZE
    key_value_begin = (
        feature_group_index * query_head_rows // (QUERY_HEADS // KEY_VALUE_HEADS) * HEAD_SIZE
    )
    own_wkv = lax.dynamic_slice_in_dim(key_value_weight, key_value_begin, key_value_width, 2)
    request_key_value_up = lax.dynamic_slice_in_dim(
        adapter_up_key_value, key_value_begin, key_value_width, 3
    )
    gathered = (
        lax.all_gather(adapter_down_qkv, "req", axis=0, tiled=True),
        lax.all_gather(adapter_down_output, "req", axis=0, tiled=True),
        lax.all_gather(adapter_up_query, "req", axis=0, tiled=True),
        lax.all_gather(request_key_value_up, "req", axis=0, tiled=True),
        lax.all_gather(adapter_up_output, "req", axis=0, tiled=True),
    )
    slot_indices = jnp.take(adapter_storage, adapter_of_request[0, :, 0], axis=0)
    chosen_down = jnp.take(gathered[0], slot_indices, axis=0)
    output_down = jnp.take(gathered[1], slot_indices, axis=0)
    query_up_part = jnp.take(gathered[2], slot_indices, axis=0)
    key_value_up = jnp.take(gathered[3], slot_indices, axis=0)
    output_up = jnp.take(gathered[4], slot_indices, axis=0)
    feature_cols = full_width // feature_group_count
    own_normed = lax.dynamic_slice_in_dim(
        normalized_input, feature_group_index * feature_cols, feature_cols, 1
    )
    low_terms = jnp.einsum(
        "gd,jkd->gjk", own_normed, chosen_down, preferred_element_type=jnp.float32
    )
    lowrank_inner = lax.psum(select_rows(low_terms, group_members).astype(jnp.bfloat16), "mlp")
    q_part = lax.all_gather(query_weight, "req", axis=0, tiled=True)
    kv_part = lax.all_gather(own_wkv, "req", axis=0, tiled=True)
    query_width_total = jnp.dot(normalized_input, q_part, preferred_element_type=jnp.float32)
    kv_total = jnp.dot(
        normalized_input,
        kv_part.reshape(kv_part.shape[0], 2 * key_value_width),
        preferred_element_type=jnp.float32,
    )
    query_width_total, kv_total = (query_width_total, kv_total)
    query_plain = (
        query_width_total
        + apply_adapter(lowrank_inner[:, 0:ADAPTER_RANK], group_members, query_up_part)
    ).astype(jnp.bfloat16)
    key_lowrank_part = apply_adapter(
        lowrank_inner[:, ADAPTER_RANK : 2 * ADAPTER_RANK], group_members, key_value_up[:, :, 0]
    )
    value_lowrank_part = apply_adapter(
        lowrank_inner[:, 2 * ADAPTER_RANK : 3 * ADAPTER_RANK], group_members, key_value_up[:, :, 1]
    )
    key_value_plain = (
        kv_total.reshape(row_count, 2, key_value_width)
        + jnp.stack([key_lowrank_part, value_lowrank_part], axis=1)
    ).astype(jnp.bfloat16)
    cached = lax.dynamic_slice_in_dim(pool, key_value_begin, key_value_width, 2)
    pool_token_rows = cached.shape[0]
    query_rotated = rotary_embed(
        root_mean_scale(
            query_plain.astype(jnp.float32).reshape(row_count, query_head_rows, HEAD_SIZE),
            query_norm_gain,
        ),
        token_positions,
    ).astype(jnp.bfloat16)
    key_rotated = rotary_embed(
        root_mean_scale(
            key_value_plain[:, 0]
            .astype(jnp.float32)
            .reshape(row_count, key_value_local, HEAD_SIZE),
            key_norm_gain,
        ),
        token_positions,
    ).astype(jnp.bfloat16)
    cache_columns = KEY_VALUE_HEADS * HEAD_SIZE // feature_group_count
    own_offset = feature_group_index * cache_columns - key_value_begin
    local_cache = jnp.stack(
        [key_rotated.reshape(row_count, key_value_width), key_value_plain[:, 1]], axis=1
    )
    new_cache = lax.dynamic_slice_in_dim(local_cache, own_offset, cache_columns, 2)
    key_matrix = jnp.concatenate(
        [cached[:, 0].reshape(pool_token_rows, key_value_local, HEAD_SIZE), key_rotated], axis=0
    )
    value_matrix = jnp.concatenate(
        [
            cached[:, 1].reshape(pool_token_rows, key_value_local, HEAD_SIZE),
            key_value_plain[:, 1].reshape(row_count, key_value_local, HEAD_SIZE),
        ],
        axis=0,
    )
    pool_ok = jnp.dot(group_members.astype(jnp.float32), page_used, precision=lax.Precision.HIGHEST)
    pool_ok = jnp.repeat(pool_ok, PAGE, axis=1) > 0.5
    row_ids = jnp.arange(row_count, dtype=jnp.int32)
    causal = (owners[:, None] == owners[None, :]) & (row_ids[None, :] <= row_ids[:, None])
    allowed = jnp.concatenate([pool_ok, causal], axis=1)
    query_rows = query_rotated.reshape(
        row_count, key_value_local, query_head_rows // key_value_local, HEAD_SIZE
    )
    scores = jnp.einsum(
        "gkhd,skd->khgs", query_rows, key_matrix, preferred_element_type=jnp.float32
    ) / math.sqrt(HEAD_SIZE)
    exp_scores = jnp.where(allowed[None, None], jnp.exp(scores), 0.0)
    softmax = (exp_scores / jnp.sum(exp_scores, axis=-1, keepdims=True)).astype(jnp.bfloat16)
    attended = jnp.einsum(
        "khgs,skd->gkhd", softmax, value_matrix, preferred_element_type=jnp.float32
    )
    attended = attended.astype(jnp.bfloat16).reshape(row_count, q_width)
    out_terms = jnp.einsum("gc,jrc->gjr", attended, output_down, preferred_element_type=jnp.float32)
    lowrank_result = lax.psum(select_rows(out_terms, group_members), "mlp").astype(jnp.bfloat16)
    partial_value = jnp.einsum(
        "gc,cnk->gnk",
        attended,
        lax.all_gather(output_weight, "req", axis=2, tiled=True),
        preferred_element_type=jnp.float32,
    )
    summed_output = lax.psum_scatter(
        partial_value.reshape(row_count, full_width).astype(jnp.bfloat16),
        "mlp",
        scatter_dimension=1,
        tiled=True,
    ).astype(jnp.float32)
    attention_update = (
        summed_output + apply_adapter(lowrank_result, group_members, output_up)
    ).astype(jnp.bfloat16)
    return (attention_update, new_cache)


def solution(mesh):
    return jax.shard_map(
        shards,
        mesh=mesh,
        in_specs=(
            P("req", "mlp"),
            P(),
            P(),
            P(),
            P("req", "mlp"),
            P("req", None, None),
            P("mlp", None, "req"),
            P("req", None, "mlp"),
            P("req", None, "mlp"),
            P("req", None, "mlp"),
            P("req", None, None, None),
            P("req", None, "mlp"),
            P("req", None, None),
            P("req", None),
            P("req", None),
            P("req", None, None),
            P("req", None, None),
            P(),
        ),
        out_specs=(P("req", "mlp"), P("req", None, "mlp")),
        check_vma=False,
    )
```

profile of v0, /device:TPU:0, one launch (start us, length us, event | category | flops | bytes accessed | tf_op | source)
XLA Modules:
  0.0 383.0 jit_solution(2718881708258280493)
XLA Ops:
  8.8 1.2 constant_dynamic-slice_fusion.2
  12.4 2.6 constant_dynamic-slice_fusion
  17.9 16.6 %all_gather.30 = bf16[16,16,2,256]{3,1,2,0:T(8,128)(2,1)S(1)} all-gather(bf16[2,16,2,256]{3,1,2,0:T(8,128)(2,1)S(1)} %copy.100), channel_id=1, replica_groups=mesh['req'=8,'mlp'=4] {'req'}, dimensions={0}, use_global_device_ids=true | all-gather | bytes 294912 | tf_op jit(solution)/shard_map/all_gather | solution.py:109
  35.1 15.0 %all_gather.32 = bf16[16,16,1024]{2,1,0:T(8,128)(2,1)S(1)} all-gather(bf16[2,16,1024]{2,1,0:T(8,128)(2,1)S(1)} %copy-done.7), channel_id=1, replica_groups=mesh['req'=8,'mlp'=4] {'req'}, dimensions={0}, use_global_device_ids=true | all-gather | bytes 589824 | tf_op jit(solution)/shard_map/all_gather | solution.py:108
  52.9 2.0 gather_fusion.1
  54.9 29.8 %all-gather.6.cloned.1.call-done = bf16[384,4096]{1,0:T(8,128)(2,1)} async-done(((bf16[384,1024]{1,0:T(8,128)(2,1)}), bf16[384,4096]{1,0:T(8,128)(2,1)}) %all-gather.6.cloned.1.call-update) | async-done | bytes 3145744 | tf_op jit(solution)/shard_map/all_gather | solution.py:86
  84.7 2.7 fusion.1
  88.7 1.7 copy-done.4
  90.8 15.7 %psum.14 = bf16[384,48]{0,1:T(8,128)(2,1)S(1)} all-reduce(bf16[384,48]{0,1:T(8,128)(2,1)S(1)} %fusion.21), channel_id=1, replica_groups=mesh['req'=8,'mlp'=4] {'mlp'}, use_global_device_ids=true, to_apply=%region_4.5 | all-reduce | flops 18432 | bytes 73728 | tf_op jit(solution)/shard_map/psum | solution.py:125
  107.1 27.0 %all-gather.8.cloned.1.call-done = bf16[4096,2,256]{2,1,0:T(2,128)(2,1)} async-done(((bf16[512,2,256]{2,1,0:T(2,128)(2,1)}), bf16[4096,2,256]{2,1,0:T(2,128)(2,1)}) %all-gather.8.cloned.1.call-update) | async-done | bytes 4194320 | tf_op jit(solution)/shard_map/all_gather | solution.py:127
  134.1 11.4 %copy.96 = bf16[4096,2,256]{0,2,1:T(8,128)(2,1)} copy(bf16[4096,2,256]{2,1,0:T(2,128)(2,1)} %all-gather.8.cloned.1.call-done) | data formatting | bytes 8388608 | tf_op jit(solution)/shard_map/reshape | solution.py:131
  145.4 5.5 %fusion.16 = bf16[384,2,256]{0,2,1:T(8,128)(2,1)S(1)} fusion(bf16[4096,2,256]{0,2,1:T(8,128)(2,1)} %copy.96, bf16[384,4096]{1,0:T(8,128)(2,1)} %copy-done.4, f32[384,1,256]{0,2,1:T(8,128)S(1)} %convolution_bitcast_fusion, f32[384,1,256]{0,2,1:T(8,128)S(1)} %convolution_bitcast_fusion.1), kind=kOutput, calls=%fused_computation.31 | convolution fusion | flops 1611202560 | bytes 8519680 | tf_op jit(solution)/shard_map/dot_general | solution.py:129
  151.8 64.6 %all-gather.12.cloned.1.call-done = bf16[4096,1024]{1,0:T(8,128)(2,1)} async-done(((bf16[512,1024]{1,0:T(8,128)(2,1)}), bf16[4096,1024]{1,0:T(8,128)(2,1)}) %all-gather.12.cloned.1.call-update) | async-done | bytes 8388624 | tf_op jit(solution)/shard_map/all_gather | solution.py:126
  216.4 6.8 %fusion.76 = f32[384,1024]{1,0:T(8,128)S(1)} fusion(bf16[384,4096]{1,0:T(8,128)(2,1)} %copy-done.4, bf16[4096,1024]{1,0:T(8,128)(2,1)} %all-gather.12.cloned.1.call-done), kind=kOutput, calls=%fused_computation.133 | convolution fusion | flops 3221225472 | bytes 13107200 | tf_op jit(solution)/shard_map/dot_general | solution.py:128
  226.0 72.8 %all-gather.14.cloned.1.call-done = bf16[1024,4,1024]{2,1,0:T(4,128)(2,1)} async-done(((bf16[1024,4,128]{2,1,0:T(4,128)(2,1)}), bf16[1024,4,1024]{2,1,0:T(4,128)(2,1)}) %all-gather.14.cloned.1.call-update) | async-done | bytes 8388624 | tf_op jit(solution)/shard_map/all_gather | solution.py:205
  298.9 12.2 %copy.103 = bf16[128,8,4,1024]{3,1,2,0:T(8,128)(2,1)} copy(bf16[128,8,4,1024]{3,2,1,0:T(4,128)(2,1)} %bitcast.125) | data formatting | bytes 16777216
  311.1 3.1 fusion
  314.2 3.7 fusion.10
  317.9 5.0 %convolution_convert_fusion = bf16[384,4096]{1,0:T(8,128)(2,1)} fusion(bf16[384,1024]{0,1:T(8,128)(2,1)S(1)} %bitcast.142, bf16[4096,1024]{0,1:T(8,128)(2,1)S(1)} %bitcast.128), kind=kOutput, calls=%fused_computation.14 | convolution fusion | flops 3222798336 | bytes 12320768 | tf_op jit(solution)/shard_map/gc,cnk->gnk/dot_general | solution.py:202
  323.7 14.9 %all_gather.34 = bf16[16,16,1024]{2,1,0:T(8,128)(2,1)S(1)} all-gather(bf16[2,16,1024]{2,1,0:T(8,128)(2,1)S(1)} %copy-done.8), channel_id=1, replica_groups=mesh['req'=8,'mlp'=4] {'req'}, dimensions={0}, use_global_device_ids=true | all-gather | bytes 589824 | tf_op jit(solution)/shard_map/all_gather | solution.py:107
  339.1 14.9 %all_gather.35 = bf16[16,16,1024]{2,1,0:T(8,128)(2,1)S(1)} all-gather(bf16[2,16,1024]{2,1,0:T(8,128)(2,1)S(1)} %copy-done.9), channel_id=1, replica_groups=mesh['req'=8,'mlp'=4] {'req'}, dimensions={0}, use_global_device_ids=true | all-gather | bytes 589824 | tf_op jit(solution)/shard_map/all_gather | solution.py:110
  355.9 1.4 fusion.22
  357.4 16.4 %psum.15 = bf16[384,16]{0,1:T(8,128)(2,1)S(1)} all-reduce(f32[384,16]{0,1:T(8,128)S(1)} %fusion.22), channel_id=1, replica_groups=mesh['req'=8,'mlp'=4] {'mlp'}, use_global_device_ids=true, to_apply=%region_12.14 | all-reduce | flops 6144 | bytes 36864 | tf_op jit(solution)/shard_map/psum | solution.py:201
  373.8 2.4 fusion.8
  (119 shorter events, 19.2 us)
Async XLA Ops:
  7.2 4.9 %copy-start.16 = (s32[1,4]{1,0:T(1,128)S(1)}, s32[1,4]{1,0:T(1,128)}, u32[]{:S(2)}) copy-start(s32[1,4]{1,0:T(1,128)} %param.33) | copy-start | bytes 52
  7.2 5.0 %copy-start.10 = (bf16[4096]{0:T(1024)(128)(2,1)S(1)}, bf16[4096]{0:T(1024)(128)(2,1)}, u32[]{:S(2)}) copy-start(bf16[4096]{0:T(1024)(128)(2,1)} %param.21) | copy-start | bytes 24580
  7.2 5.0 %copy-start.15 = (bf16[128]{0:T(256)(128)(2,1)S(1)}, bf16[128]{0:T(256)(128)(2,1)}, u32[]{:S(2)}) copy-start(bf16[128]{0:T(256)(128)(2,1)} %param.23) | copy-start | bytes 772
  7.2 5.1 %copy-start.18 = (s32[1,4]{1,0:T(1,128)S(1)}, s32[1,4]{1,0:T(1,128)}, u32[]{:S(2)}) copy-start(s32[1,4]{1,0:T(1,128)} %param.34) | copy-start | bytes 52
  7.2 45.7 %all-gather.10.cloned.1.call-start = ((), (), s32[]{:S(2)}) async-start(), calls=%async_computation.3 | async-start | bytes 1769472 | tf_op jit(solution)/shard_map/all_gather | solution.py:106
  8.0 76.8 %all-gather.6.cloned.1.call-start = ((), (), s32[]{:S(2)}) async-start(), calls=%async_computation.1 | async-start | bytes 3932160 | tf_op jit(solution)/shard_map/all_gather | solution.py:86
  8.7 125.4 %all-gather.8.cloned.1.call-start = ((), (), s32[]{:S(2)}) async-start(), calls=%async_computation.2 | async-start | bytes 4718592 | tf_op jit(solution)/shard_map/all_gather | solution.py:127
  9.9 6.6 %copy-start.17 = (bf16[128]{0:T(256)(128)(2,1)S(1)}, bf16[128]{0:T(256)(128)(2,1)}, u32[]{:S(2)}) copy-start(bf16[128]{0:T(256)(128)(2,1)} %param.22) | copy-start | bytes 772
  10.0 7.3 %copy-start.14 = (s32[1,4,1]{1,2,0:T(1,128)S(1)}, s32[1,4,1]{1,2,0:T(1,128)}, u32[]{:S(2)}) copy-start(s32[1,4,1]{1,2,0:T(1,128)} %param.36) | copy-start | bytes 52
  10.0 7.3 %copy-start.2 = (s32[16]{0:T(128)S(1)}, s32[16]{0:T(128)}, u32[]{:S(2)}) copy-start(s32[16]{0:T(128)} %param.37) | copy-start | bytes 196
  10.0 206.4 %all-gather.12.cloned.1.call-start = ((), (), s32[]{:S(2)}) async-start(), calls=%async_computation.4 | async-start | bytes 9437184 | tf_op jit(solution)/shard_map/all_gather | solution.py:126
  10.6 24.6 %copy-start.7 = (bf16[2,16,1024]{2,1,0:T(8,128)(2,1)S(1)}, bf16[2,16,1024]{2,1,0:T(8,128)(2,1)}, u32[]{:S(2)}) copy-start(bf16[2,16,1024]{2,1,0:T(8,128)(2,1)} %param.29) | copy-start | bytes 196612
  10.6 288.3 %all-gather.14.cloned.1.call-start = ((), (), s32[]{:S(2)}) async-start(), calls=%async_computation.5 | async-start | bytes 9437184 | tf_op jit(solution)/shard_map/all_gather | solution.py:205
  11.2 39.6 %copy-start.13 = (s32[1,4,8]{2,1,0:T(4,128)S(1)}, s32[1,4,8]{2,1,0:T(4,128)}, u32[]{:S(2)}) copy-start(s32[1,4,8]{2,1,0:T(4,128)} %param.35) | copy-start | bytes 388
  11.2 362.6 %reduce-scatter.2.cloned.1.call-start = ((), (), s32[]{:S(2)}) async-start(), calls=%async_computation.6 | async-start | bytes 3932160 | tf_op jit(solution)/shard_map/reduce_scatter | solution.py:208
  35.1 188.0 %copy-start.11 = (pred[4]{0:T(512)(128)(4,1)}, pred[4]{0:T(512)(128)(4,1)S(1)}, u32[]{:S(2)}) copy-start(pred[4]{0:T(512)(128)(4,1)S(1)} %get-tuple-element.15) | copy-start | bytes 16
  298.9 12.2 %copy-start.5 = (pred[384,896]{0,1:T(8,128)(4,1)S(1)}, pred[384,896]{0,1:T(8,128)(4,1)}, u32[]{:S(2)}) copy-start(pred[384,896]{0,1:T(8,128)(4,1)} %pad_add_fusion) | copy-start | bytes 1032196
  298.9 12.2 %copy-start.6 = (bf16[512,2,128]{2,0,1:T(8,128)(2,1)S(1)}, bf16[512,2,128]{2,0,1:T(8,128)(2,1)}, u32[]{:S(2)}) copy-start(bf16[512,2,128]{2,0,1:T(8,128)(2,1)} %copy.83) | copy-start | bytes 786436
  311.1 6.8 %slice-start = ((s8[8388608]{0:T(1024)(128)(4,1)}), s8[4194304]{0:T(1024)(128)(4,1)S(1)}, s32[]{:S(2)}) async-start(s8[8388608]{0:T(1024)(128)(4,1)} %bitcast.126), calls=%async_computation.7 | async-start | bytes 8388608
  314.2 3.7 slice-start.1
  317.9 5.0 %copy-start.19 = (bf16[2,128,4,384]{3,1,2,0:T(8,128)(2,1)}, bf16[2,128,4,384]{3,1,2,0:T(8,128)(2,1)S(1)}, u32[]{:S(2)}) copy-start(bf16[2,128,4,384]{3,1,2,0:T(8,128)(2,1)S(1)} %fusion.10) | copy-start | bytes 2359300
  322.9 16.3 %copy-start.9 = (bf16[2,16,1024]{2,1,0:T(8,128)(2,1)S(1)}, bf16[2,16,1024]{2,1,0:T(8,128)(2,1)}, u32[]{:S(2)}) copy-start(bf16[2,16,1024]{2,1,0:T(8,128)(2,1)} %param.31) | copy-start | bytes 196612
  322.9 33.1 %copy-start.12 = (pred[4]{0:T(512)(128)(4,1)S(1)}, pred[4]{0:T(512)(128)(4,1)}, u32[]{:S(2)}) copy-start(pred[4]{0:T(512)(128)(4,1)} %copy-done.11) | copy-start | bytes 16
  354.0 22.1 %copy-start.1 = (bf16[512,2,1024]{2,1,0:T(2,128)(2,1)S(1)}, bf16[512,2,1024]{2,1,0:T(2,128)(2,1)}, u32[]{:S(2)}) copy-start(bf16[512,2,1024]{2,1,0:T(2,128)(2,1)} %param.25) | copy-start | bytes 6291460
  (4 other events, 7.0 us)
Sparse Core Ops, SparseCore 0:
  9.7 29.8 all-gather.9
  41.4 43.2 all-gather.5
  86.9 47.1 all-gather.7
  135.5 80.7 all-gather.11
  217.8 81.0 all-gather.13
  323.0 42.3 reduce-scatter.1
where the time goes:
time: 384 us; the launch traced here: 383 us
  waiting for transfers between devices  197 us (51%)
  blocking collectives  93.4 us (24%)
  local copies, waits for them, and re-layouts  40.1 us (10%)
  matrix products  29.5 us (8%)
  between operations  14.7 us (4%)
  other arithmetic  8.47 us (2%)
    all_gather x1, waiting for transfers between devices, shards(): lax.all_gather(output_weight, 'req', axis=2, tiled=True)  72.8 us
    all_gather x1, waiting for transfers between devices, shards(): q_part = lax.all_gather(query_weight, 'req', axis=0, tiled=True)  64.6 us
    all_gather x1, waiting for transfers between devices, shards(): whole = lax.all_gather(hidden_input, 'mlp', axis=1, tiled=True)  29.8 us
    all_gather x1, waiting for transfers between devices, shards(): kv_part = lax.all_gather(own_wkv, 'req', axis=0, tiled=True)  27 us
    unnamed x50, local copies, waits for them, and re-layouts  17.7 us
    all_gather x1, blocking collectives, shards(): lax.all_gather(request_key_value_up, 'req', axis=0, tiled=True)  16.6 us
    psum x1, blocking collectives, shards(): lax.psum(select_rows(out_terms, group_members), 'mlp').astype(jnp.bfloat16)  16.4 us
    psum x1, blocking collectives, shards(): lax.psum(select_rows(low_terms, group_members).astype(jnp.bfloat16), 'mlp')  15.7 us
  transfers between devices with their start and end apart: 6, of which 4 were waited for; matrix products, arithmetic and copies ran while one was open for 13% of the time, Pallas kernels for 0%

commit v1 on v0

--- a/solution.py
+++ b/solution.py
@@ -1,8 +1,11 @@
+import functools
 import math
 
 import jax
 import jax.numpy as jnp
 from jax import lax
+from jax.experimental import pallas as pl
+from jax.experimental.pallas import tpu as pltpu
 from jax.sharding import PartitionSpec as P
 
 QUERY_HEADS = 32
@@ -217,9 +220,733 @@
     return (attention_update, new_cache)
 
 
+PLANES = 4
+BLOCKS = 4
+GROUPS = 2
+WIDE = 256
+
+
+def planes_fit(mesh):
+    return mesh.shape["req"] == 2 * PLANES and mesh.shape["mlp"] == BLOCKS
+
+
+def plane_pairs(pairs):
+    return [(2 * a + core, 2 * b + core) for a, b in pairs for core in range(2)]
+
+
+INWARD = plane_pairs([(0, 1), (3, 2)])
+MIDDLE = plane_pairs([(1, 2), (2, 1)])
+OUTWARD = plane_pairs([(1, 0), (2, 3)])
+NEAR = plane_pairs([(0, 1), (1, 0), (2, 3), (3, 2)])
+CORES = [(r, r ^ 1) for r in range(2 * PLANES)]
+
+
+def along(value, pairs):
+    return lax.ppermute(value, "req", pairs)
+
+
+def swap_blocks(value, k):
+    return lax.ppermute(value, "mlp", [(b, b ^ k) for b in range(BLOCKS)])
+
+
+def to_blocks(pieces):
+    return [
+        lax.ppermute(piece, "mlp", [(b, b ^ k) for b in range(BLOCKS)])
+        for k, piece in enumerate(pieces)
+        if k > 0
+    ]
+
+
+def gate_kernel(*refs):
+    del refs
+
+
+def gate(values, earlier):
+    return pl.pallas_call(
+        gate_kernel,
+        in_specs=[pl.BlockSpec(memory_space=pl.ANY)] * (len(values) + len(earlier)),
+        out_specs=[pl.BlockSpec(memory_space=pl.ANY)] * len(values),
+        out_shape=[jax.ShapeDtypeStruct(v.shape, v.dtype) for v in values],
+        input_output_aliases={i: i for i in range(len(values))},
+        name="gate",
+    )(*values, *earlier)
+
+
+def in_vmem():
+    return pl.BlockSpec(memory_space=pltpu.VMEM)
+
+
+def in_smem():
+    return pl.BlockSpec(memory_space=pltpu.SMEM)
+
+
+def cost(flops, bytes_accessed, transcendentals=0):
+    return pl.CostEstimate(
+        flops=flops, bytes_accessed=bytes_accessed, transcendentals=transcendentals
+    )
+
+
+def kernel_params():
+    return pltpu.CompilerParams(vmem_limit_bytes=56 * 1024 * 1024)
+
+
+def request_of_rows(table, shape, axis):
+    row = lax.broadcasted_iota(jnp.int32, shape, axis)
+    end, owner = table[0], jnp.zeros(shape, jnp.int32)
+    for j in range(1, 4):
+        owner = jnp.where(row >= end, j, owner)
+        end = end + table[j]
+    return owner
+
+
+def slots_of_rows(table, storage, row_count):
+    owner = request_of_rows(table, (1, row_count), 1)
+    slots = jnp.zeros((1, row_count), jnp.int32) + storage[table[4]]
+    for j in range(1, 4):
+        slots = jnp.where(owner == j, storage[table[4 + j]], slots)
+    return slots
+
+
+def slot_list(place):
+    core = place[0]
+    return [4 * place[2 + i] + 2 * c + s for c in (core, 1 - core) for i in range(4) for s in range(2)]
+
+
+def dot(a, b):
+    return jnp.dot(a, b, preferred_element_type=jnp.float32)
+
+
+def core_columns(c, half):
+    return pl.ds(pl.multiple_of(c * half, half), half)
+
+
+def norm_kernel(place, gain, p0, p1, p2, p3, p4, *refs):
+    out, done = refs[-2:]
+    pieces = [p[...].astype(jnp.float32) for p in (p0, p1, p2)]
+    late = pl.program_id(0) >= pl.num_programs(0) // 2
+    pieces.append(jnp.where(late, p4[...], p3[...]).astype(jnp.float32))
+    total = sum(jnp.sum(v * v, axis=1, keepdims=True) for v in pieces)
+    half = pieces[0].shape[1] // 2
+    scale = lax.rsqrt(total / (BLOCKS * 2 * half) + epsilon)
+    core = place[0]
+    for k, v in enumerate(pieces):
+        normed = (v * scale * gain[pl.ds(place[1] ^ k, 1), :]).astype(jnp.bfloat16)
+        out[k, :, core_columns(core, half)] = normed[:, :half]
+        out[k, :, core_columns(1 - core, half)] = normed[:, half:]
+    done[...] = jnp.zeros(done.shape, jnp.float32)
+
+
+def norm_rows(place, gain, pieces, group, given):
+    rows, width = pieces[0].shape
+    tiles = 4
+    tile = rows // tiles
+    more = [] if given is None else [given]
+    whole = pl.BlockSpec((tile, width), lambda i, place: (i, 0))
+    front = pl.BlockSpec((tile, width), lambda i, place: (jnp.minimum(i, tiles // 2 - 1), 0))
+    back = pl.BlockSpec((tile, width), lambda i, place: (jnp.maximum(i - tiles // 2, 0), 0))
+    return pl.pallas_call(
+        norm_kernel,
+        grid_spec=pltpu.PrefetchScalarGridSpec(
+            num_scalar_prefetch=1,
+            grid=(tiles,),
+            in_specs=[pl.BlockSpec((BLOCKS, width), lambda i, place: (0, 0))]
+            + [whole] * 3
+            + [front, back]
+            + [pl.BlockSpec(memory_space=pl.ANY)] * len(more),
+            out_specs=[
+                pl.BlockSpec((BLOCKS, tile, width), lambda i, place: (0, tiles * group + i, 0)),
+                pl.BlockSpec((8, 128), lambda i, place: (0, 0)),
+            ],
+        ),
+        out_shape=[
+            jax.ShapeDtypeStruct((BLOCKS, GROUPS * rows, width), jnp.bfloat16),
+            jax.ShapeDtypeStruct((8, 128), jnp.float32),
+        ],
+        input_output_aliases={7: 0} if more else {},
+        compiler_params=kernel_params(),
+        cost_estimate=cost(16 * rows * width, 4 * BLOCKS * rows * width),
+        name="norm_rows",
+    )(place, gain, *pieces, *more)
+
+
+SLOT_ROWS = 128
+
+
+def pack_kernel(table, kv, down_qkv, up_query, up_kv, down_out, up_out, out):
+    depth, kv_columns = kv.shape
+    rank = ADAPTER_RANK
+    out[2 * SLOT_ROWS :, :kv_columns] = kv[: depth // 2]
+    out[2 * SLOT_ROWS :, kv_columns:] = kv[depth // 2 :]
+    for s in range(2):
+        first = s * SLOT_ROWS
+        out[first : first + 3 * rank] = down_qkv[s]
+        out[first + 3 * rank : first + 4 * rank] = up_query[s]
+        out[first + 4 * rank : first + 5 * rank, :kv_columns] = up_kv[s]
+        out[first + 4 * rank : first + 5 * rank, kv_columns:] = jnp.zeros(
+            (rank, out.shape[1] - kv_columns), jnp.bfloat16
+        )
+        out[first + 5 * rank : first + 6 * rank] = down_out[s]
+        out[first + 6 * rank : first + 7 * rank] = up_out[s]
+    shape = (rank, out.shape[1])
+    lane = lax.broadcasted_iota(jnp.int32, shape, 1)
+    numbers = jnp.zeros(shape, jnp.float32)
+    for i in range(8):
+        numbers = jnp.where(lane == i, table[i].astype(jnp.float32), numbers)
+    for s in range(2):
+        out[s * SLOT_ROWS + 7 * rank : (s + 1) * SLOT_ROWS] = numbers.astype(jnp.bfloat16)
+
+
+def pack_rows(table, kv, *adapters):
+    width = adapters[0].shape[2]
+    return pl.pallas_call(
+        pack_kernel,
+        in_specs=[in_smem()] + [in_vmem()] * 6,
+        out_specs=in_vmem(),
+        out_shape=jax.ShapeDtypeStruct((2 * SLOT_ROWS + kv.shape[0] // 2, width), jnp.bfloat16),
+        compiler_params=kernel_params(),
+        cost_estimate=cost(0, 4 * width * (2 * SLOT_ROWS + kv.shape[0] // 2), 0),
+        name="pack_rows",
+    )(table, kv, *adapters)
+
+
+def rank_kernel(place, own_table, end_table, storage, x, *refs):
+    packed, (low, chosen_own, chosen_end, up, down) = refs[:8], refs[8:]
+    slots = slot_list(place)
+    rank, rows, q_width = ADAPTER_RANK, x.shape[1] // GROUPS, x.shape[2]
+    kv_columns, half, core = up.shape[1] - q_width, q_width // 2, place[0]
+    for t, ref in enumerate(packed):
+        for s in range(2):
+            i, first = 2 * t + s, s * SLOT_ROWS
+            for c, columns in ((core, slice(0, half)), (1 - core, slice(half, q_width))):
+                down[3 * rank * i : 3 * rank * (i + 1), columns] = ref[
+                    first : first + 3 * rank, core_columns(c, half)
+                ]
+            up[rank * i : rank * (i + 1), :q_width] = ref[first + 3 * rank : first + 4 * rank, :]
+            up[rank * i : rank * (i + 1), q_width:] = ref[
+                first + 4 * rank : first + 5 * rank, :kv_columns
+            ]
+    for g, (table, chosen) in enumerate(((own_table, chosen_own), (end_table, chosen_end))):
+        terms = lax.dot_general(
+            down[...],
+            x[0, g * rows : (g + 1) * rows, :],
+            (((1,), (1,)), ((), ())),
+            preferred_element_type=jnp.float32,
+        )
+        row_slots = slots_of_rows(table, storage, rows)
+        total = jnp.zeros((3 * rank, rows), jnp.float32)
+        for i, slot in enumerate(slots):
+            total += jnp.where(row_slots == slot, terms[3 * rank * i : 3 * rank * (i + 1)], 0.0)
+        low[:, g * rows : (g + 1) * rows] = total.astype(jnp.bfloat16)
+        for j in range(4):
+            wanted = storage[table[4 + j]]
+            for i, slot in enumerate(slots):
+
+                @pl.when(wanted == slot)
+                def _(j=j, i=i, chosen=chosen):
+                    first = (i % 2) * SLOT_ROWS
+                    chosen[j] = packed[i // 2][first + 5 * rank : first + 7 * rank, :]
+
+
+def rank_terms(place, own_table, end_table, storage, x, packed, kv_columns):
+    _, rows, width = x.shape
+    chosen = jax.ShapeDtypeStruct((4, 2 * ADAPTER_RANK, width), jnp.bfloat16)
+    up = jax.ShapeDtypeStruct((16 * ADAPTER_RANK, width + kv_columns), jnp.bfloat16)
+    low = jax.ShapeDtypeStruct((3 * ADAPTER_RANK, rows), jnp.bfloat16)
+    first = pl.BlockSpec((1, rows, width), lambda i: (0, 0, 0))
+    slots = pl.BlockSpec((2 * SLOT_ROWS, width), lambda i: (0, 0))
+    whole = lambda shape: pl.BlockSpec(shape, lambda i: (0,) * len(shape))
+    return pl.pallas_call(
+        rank_kernel,
+        grid=(1,),
+        in_specs=[in_smem()] * 4 + [first] + [slots] * 8,
+        out_specs=[whole(v.shape) for v in (low, chosen, chosen, up)],
+        out_shape=[low, chosen, chosen, up],
+        scratch_shapes=[pltpu.VMEM((16 * 3 * ADAPTER_RANK, width), jnp.bfloat16)],
+        compiler_params=kernel_params(),
+        cost_estimate=cost(2 * 16 * 3 * ADAPTER_RANK * rows * width, 2 * width * (rows + 18 * SLOT_ROWS + 256), 0),
+        name="rank_terms",
+    )(place, own_table, end_table, storage, x, *packed)
+
+
+def first_kernel(place, x, *refs):
+    weights, packed, (out, done) = refs[:6], refs[6:22], refs[22:]
+    half, depth = x.shape[2] // 2, packed[0].shape[0]
+    step = pl.program_id(0)
+
+    @pl.when(step < 4)
+    def _():
+        total = None
+        for i, w in enumerate(weights):
+            k, c = place[2 + i // 2] ^ place[1], i % 2
+            term = dot(x[k, :, c * half : (c + 1) * half], w[...])
+            total = term if total is None else total + term
+        out[...] = total
+
+    @pl.when(step >= 4)
+    def _():
+        total = None
+        for i, w in enumerate(packed):
+            k, c = place[2 + i // 4] ^ place[1], i % 4
+            term = dot(x[k, :, c * depth : (c + 1) * depth], w[...])
+            total = term if total is None else total + term
+        out[...] = total
+
+    done[...] = jnp.zeros(done.shape, jnp.float32)
+
+
+def project_first(place, x, queries, packed):
+    _, rows, width = x.shape
+    depth = queries[0].shape[0]
+    tile = pl.BlockSpec((rows, WIDE), lambda n: (0, n))
+    query = pl.BlockSpec((depth, WIDE), lambda n: (0, jnp.minimum(n, 3)))
+    key_values = [
+        pl.BlockSpec((depth // 2, WIDE), lambda n, b=b: (1, b + jnp.maximum(n - 4, 0)))
+        for b in (0, 2)
+    ]
+    return pl.pallas_call(
+        first_kernel,
+        grid=(6,),
+        in_specs=[in_smem(), pl.BlockSpec(x.shape, lambda n: (0, 0, 0))]
+        + [query] * 6
+        + key_values * 8,
+        out_specs=[tile, pl.BlockSpec((8, 128), lambda n: (0, 0))],
+        out_shape=[
+            jax.ShapeDtypeStruct((rows, 6 * WIDE), jnp.float32),
+            jax.ShapeDtypeStruct((8, 128), jnp.float32),
+        ],
+        compiler_params=kernel_params(),
+        cost_estimate=cost(2 * rows * width * (3 * width + 2 * width), 8 * rows * width + 2 * width * (3 * width + 2 * width) + 24 * rows * WIDE, 0),
+        name="project_first",
+    )(place, x, *queries, *[p for p in packed for _ in range(2)])
+
+
+def last_kernel(place, x, q_core, q_other, up, given, *refs):
+    own_table, end_table, storage = refs[:3]
+    lows, (own, end, spread) = refs[3:7], refs[7:]
+    rank, rows, half = ADAPTER_RANK, x.shape[1] // GROUPS, x.shape[2] // 2
+    step = pl.program_id(0)
+    for part, at in enumerate((0, 4, 5)):
+
+        @pl.when(step == at)
+        def _(part=part):
+            slots = slot_list(place)
+            low = sum(v[part * rank : (part + 1) * rank].astype(jnp.float32) for v in lows)
+            low = low.astype(jnp.bfloat16).astype(jnp.float32)
+            for g, table in enumerate((own_table, end_table)):
+                row_slots = slots_of_rows(table, storage, rows)
+                mine = low[:, g * rows : (g + 1) * rows]
+                wide = jnp.concatenate([jnp.where(row_slots == s, mine, 0.0) for s in slots], axis=0)
+                spread[g * rows : (g + 1) * rows, :] = wide.T.astype(jnp.bfloat16)
+
+    @pl.when(step < 4)
+    def _():
+        total = (
+            given[...]
+            + dot(spread[...], up[...])
+            + dot(x[0, :, :half], q_core[...])
+            + dot(x[0, :, half:], q_other[...])
+        ).astype(jnp.bfloat16)
+        own[...] = total[:rows]
+        end[...] = total[rows:]
+
+    @pl.when(step >= 4)
+    def _():
+        total = (given[...] + dot(spread[...], up[...])).astype(jnp.bfloat16)
+        own[...] = total[:rows]
+        end[...] = total[rows:]
+
+
+def project_last(place, own_table, end_table, storage, x, queries, up, lows, sums):
+    _, rows, width = x.shape
+    depth = queries[0].shape[0]
+    features = pl.BlockSpec((1, rows, width), lambda n, place: (place[5] ^ place[1], 0, 0))
+    tile = pl.BlockSpec((rows // GROUPS, WIDE), lambda n, place: (0, n))
+    query = pl.BlockSpec((depth, WIDE), lambda n, place: (0, jnp.minimum(n, 3)))
+    low = pl.BlockSpec(lows[0].shape, lambda n, place: (0, 0))
+    return pl.pallas_call(
+        last_kernel,
+        grid_spec=pltpu.PrefetchScalarGridSpec(
+            num_scalar_prefetch=1,
+            grid=(6,),
+            in_specs=[features]
+            + [query] * 2
+            + [pl.BlockSpec((up.shape[0], WIDE), lambda n, place: (0, n))]
+            + [pl.BlockSpec((rows, WIDE), lambda n, place: (0, n))]
+            + [in_smem()] * 3
+            + [low] * 4,
+            out_specs=[tile, tile],
+            scratch_shapes=[pltpu.VMEM((rows, 16 * ADAPTER_RANK), jnp.bfloat16)],
+        ),
+        out_shape=[jax.ShapeDtypeStruct((rows // GROUPS, 6 * WIDE), jnp.bfloat16)] * 2,
+        compiler_params=kernel_params(),
+        cost_estimate=cost(2 * rows * (width + 256) * 6 * WIDE, 2 * rows * width + 2 * width * width + 36 * rows * WIDE, 0),
+        name="project_last",
+    )(place, x, *queries, up, sums, own_table, end_table, storage, *lows)
+
+
+def attention_kernel(
+    place, table, prefix, pages, own, back, k_pool, v_pool, q_gain, k_gain, cosine, sine,
+    chosen_own, chosen_back, out, cache, low, raw, keys, values, allowed, down,
+):
+    rows, pool_rows = own.shape[0], k_pool.shape[0]
+    page_count = pool_rows // PAGE
+
+    @pl.when(place[6] == 1)
+    def _():
+        raw[...] = back[...]
+        down[...] = chosen_back[:, :ADAPTER_RANK, :].reshape(down.shape)
+
+    @pl.when(place[6] == 0)
+    def _():
+        raw[...] = own[...]
+        down[...] = chosen_own[:, :ADAPTER_RANK, :].reshape(down.shape)
+
+    owner = request_of_rows(table, (rows, 1), 0)
+    page = lax.broadcasted_iota(jnp.int32, (1, pool_rows), 1) // PAGE
+    seen = jnp.zeros((rows, pool_rows), jnp.int32)
+    for j in range(4):
+        mine = jnp.zeros((1, pool_rows), jnp.int32)
+        for i in range(page_count):
+            mine = jnp.where((page == pages[8 * j + i]) & (i < prefix[j]), 1, mine)
+        seen = jnp.where(owner == j, mine, seen)
+    allowed[:, :pool_rows] = seen
+    row = lax.broadcasted_iota(jnp.int32, (rows, rows), 0)
+    column = lax.broadcasted_iota(jnp.int32, (rows, rows), 1)
+    same = owner == request_of_rows(table, (1, rows), 1)
+    allowed[:, pool_rows:] = (same & (column <= row)).astype(jnp.int32)
+
+    def turned(value, gain):
+        value = value.astype(jnp.float32)
+        mean_sq = jnp.mean(value * value, axis=1, keepdims=True)
+        value = value * lax.rsqrt(mean_sq + epsilon) * gain[...]
+        other = pltpu.roll(value, HEAD_SIZE // 2, 1)
+        return (value * cosine[...] + other * sine[...]).astype(jnp.bfloat16)
+
+    kv_heads = k_pool.shape[1] // HEAD_SIZE
+    q_width = out.shape[1]
+    per_key = q_width // HEAD_SIZE // kv_heads
+    kv_width = kv_heads * HEAD_SIZE
+    cache[:, kv_width:] = raw[:, q_width + kv_width :]
+    for h in range(kv_heads):
+        head = slice(h * HEAD_SIZE, (h + 1) * HEAD_SIZE)
+        keys[:pool_rows] = k_pool[:, head]
+        values[:pool_rows] = v_pool[:, head]
+        k_new = turned(raw[:, q_width + h * HEAD_SIZE : q_width + (h + 1) * HEAD_SIZE], k_gain)
+        keys[pool_rows:] = k_new
+        cache[:, head] = k_new
+        values[pool_rows:] = raw[
+            :, q_width + kv_width + h * HEAD_SIZE : q_width + kv_width + (h + 1) * HEAD_SIZE
+        ]
+        for g in range(per_key):
+            place_q = slice((h * per_key + g) * HEAD_SIZE, (h * per_key + g + 1) * HEAD_SIZE)
+            query = turned(raw[:, place_q], q_gain)
+            scores = lax.dot_general(
+                query, keys[...], (((1,), (1,)), ((), ())), preferred_element_type=jnp.float32
+            ) * (1.0 / math.sqrt(HEAD_SIZE))
+            grown = jnp.where(allowed[...] > 0, jnp.exp(scores), 0.0)
+            weights = (grown / jnp.sum(grown, axis=1, keepdims=True)).astype(jnp.bfloat16)
+            out[:, place_q] = jnp.dot(
+                weights, values[...], preferred_element_type=jnp.float32
+            ).astype(jnp.bfloat16)
+    terms = lax.dot_general(
+        down[...], out[...], (((1,), (1,)), ((), ())), preferred_element_type=jnp.float32
+    )
+    owner_lane = request_of_rows(table, (1, rows), 1)
+    low[...] = sum(
+        jnp.where(owner_lane == j, terms[j * ADAPTER_RANK : (j + 1) * ADAPTER_RANK], 0.0)
+        for j in range(4)
+    )
+
+
+def attend(place, table, prefix, pages, own, back, k_pool, v_pool, q_gain, k_gain, cosine, sine,
+           chosen_own, chosen_back):
+    rows = own.shape[0]
+    kv_width = k_pool.shape[1]
+    q_width = own.shape[1] - 2 * kv_width
+    keys = k_pool.shape[0] + rows
+    return pl.pallas_call(
+        attention_kernel,
+        in_specs=[in_smem()] * 4 + [in_vmem()] * 10,
+        out_specs=[in_vmem()] * 3,
+        out_shape=[
+            jax.ShapeDtypeStruct((rows, q_width), jnp.bfloat16),
+            jax.ShapeDtypeStruct((rows, 2 * kv_width), jnp.bfloat16),
+            jax.ShapeDtypeStruct((ADAPTER_RANK, rows), jnp.float32),
+        ],
+        scratch_shapes=[
+            pltpu.VMEM(own.shape, jnp.bfloat16),
+            pltpu.VMEM((keys, HEAD_SIZE), jnp.bfloat16),
+            pltpu.VMEM((keys, HEAD_SIZE), jnp.bfloat16),
+            pltpu.VMEM((rows, keys), jnp.int32),
+            pltpu.VMEM((4 * ADAPTER_RANK, chosen_own.shape[2]), jnp.bfloat16),
+        ],
+        compiler_params=kernel_params(),
+        cost_estimate=cost(4 * rows * keys * q_width, 6 * rows * q_width, rows * keys * (q_width // HEAD_SIZE)),
+        name="attend",
+    )(place, table, prefix, pages, own, back, k_pool, v_pool, q_gain, k_gain, cosine, sine,
+      chosen_own, chosen_back)
+
+
+def columns_kernel(count, place, attended, *refs):
+    sources, outs, (held, sems) = refs[: 4 * count], refs[-2 - BLOCKS : -2], refs[-2:]
+    rows = attended.shape[0]
+    if len(refs) > 4 * count + BLOCKS + 2:
+        low = refs[4 * count]
+        for out in outs:
+            out[rows:, :rows] = low[...].astype(jnp.bfloat16)
+            out[rows:, rows:] = jnp.zeros((low.shape[0], out.shape[1] - rows), jnp.bfloat16)
+    at_end = place[6] == 1
+
+    def copies(chunk, end, k):
+        pair = sources[4 * chunk + (0 if end else 2) :][:2]
+        return [
+            pltpu.make_async_copy(
+                pair[c].at[place[1] ^ k],
+                held.at[k, :, (2 * chunk + c) * HEAD_SIZE : (2 * chunk + c + 1) * HEAD_SIZE],
+                sems.at[chunk, k, c],
+            )
+            for c in range(2)
+        ]
+
+    for end in (True, False):
+
+        @pl.when(at_end if end else jnp.logical_not(at_end))
+        def _(end=end):
+            for k in range(BLOCKS):
+                for chunk in range(count):
+                    for copy in copies(chunk, end, k):
+                        copy.start()
+
+    for k in range(BLOCKS):
+        for chunk in range(count):
+            for copy in copies(chunk, False, k):
+                copy.wait()
+        outs[k][:rows] = dot(attended[...], held[k]).astype(jnp.bfloat16)
+
+
+def project_columns(place, attended, chunks, low=None):
+    more = [] if low is None else [low]
+    rows = attended.shape[0] + (0 if low is None else low.shape[0])
+    depth = chunks[0][0].shape[1]
+    width = WIDE * len(chunks)
+    return pl.pallas_call(
+        functools.partial(columns_kernel, len(chunks)),
+        in_specs=[in_smem(), in_vmem()]
+        + [pl.BlockSpec(memory_space=pl.ANY)] * (4 * len(chunks))
+        + [in_vmem()] * len(more),
+        out_specs=[in_vmem()] * BLOCKS,
+        out_shape=[jax.ShapeDtypeStruct((rows, width), jnp.bfloat16)] * BLOCKS,
+        scratch_shapes=[
+            pltpu.VMEM((BLOCKS, depth, width), jnp.bfloat16),
+            pltpu.SemaphoreType.DMA((len(chunks), BLOCKS, 2)),
+        ],
+        compiler_params=kernel_params(),
+        cost_estimate=cost(2 * rows * depth * BLOCKS * width, 2 * (rows * depth + depth * BLOCKS * width + rows * BLOCKS * width), 0),
+        name="project_columns",
+    )(place, attended, *[w for chunk in chunks for w in chunk], *more)
+
+
+def sum_kernel(place, table, chosen_own, chosen_back, *refs):
+    parts, (out, up) = refs[:12], refs[12:]
+    rank, rows = ADAPTER_RANK, out.shape[0]
+
+    @pl.when(place[6] == 1)
+    def _():
+        up[...] = chosen_back[:, rank:, :].reshape(up.shape)
+
+    @pl.when(place[6] == 0)
+    def _():
+        up[...] = chosen_own[:, rank:, :].reshape(up.shape)
+
+    low = sum(v[rows:, :rows].astype(jnp.float32) for v in parts[:4])
+    low = low.astype(jnp.bfloat16).astype(jnp.float32)
+    owner = request_of_rows(table, (1, rows), 1)
+    wide = jnp.concatenate([jnp.where(owner == j, low, 0.0) for j in range(4)], axis=0)
+    spread = wide.T.astype(jnp.bfloat16)
+    core = place[0]
+    for i in range(PLANES):
+        first, at = (0, i * WIDE) if i < 2 else (4 * (i - 1), 0)
+        total = sum(v[:rows, at : at + WIDE].astype(jnp.float32) for v in parts[first : first + 4])
+        for c, mine in ((core, total[:, :HEAD_SIZE]), (1 - core, total[:, HEAD_SIZE:])):
+            begin = pl.multiple_of((2 * place[7 + i] + c) * HEAD_SIZE, HEAD_SIZE)
+            columns = pl.ds(begin, HEAD_SIZE)
+            out[:, columns] = (
+                mine + jnp.dot(spread, up[:, columns], preferred_element_type=jnp.float32)
+            ).astype(jnp.bfloat16)
+
+
+def sum_columns(place, table, chosen_own, chosen_back, parts):
+    rows = parts[-1].shape[0]
+    width = chosen_own.shape[2]
+    return pl.pallas_call(
+        sum_kernel,
+        in_specs=[in_smem()] * 2 + [in_vmem()] * 14,
+        out_specs=in_vmem(),
+        out_shape=jax.ShapeDtypeStruct((rows, width), jnp.bfloat16),
+        scratch_shapes=[pltpu.VMEM((4 * ADAPTER_RANK, width), jnp.bfloat16)],
+        compiler_params=kernel_params(),
+        cost_estimate=cost(2 * rows * width * (8 + 4 * ADAPTER_RANK), 12 * rows * width, 0),
+        name="sum_columns",
+    )(place, table, chosen_own, chosen_back, *parts)
+
+
+def shards_by_plane(
+    hidden_input,
+    input_norm_gain,
+    query_norm_gain,
+    key_norm_gain,
+    query_weight,
+    key_value_weight,
+    output_weight,
+    adapter_down_qkv,
+    adapter_down_output,
+    adapter_up_query,
+    adapter_up_key_value,
+    adapter_up_output,
+    pool,
+    lengths,
+    cached_prefix_pages,
+    prefix_page_table,
+    adapter_of_request,
+    adapter_storage,
+):
+    request_index = lax.axis_index("req")
+    plane, core = request_index // 2, request_index % 2
+    block = lax.axis_index("mlp")
+    at_end = (plane == 0) | (plane == PLANES - 1)
+    near_end = jnp.where(plane < 2, 0, PLANES - 1)
+    near = jnp.where(at_end, jnp.where(plane == 0, 1, 2), near_end)
+    other = jnp.where(at_end, jnp.where(plane == 0, 2, 1), 3 - plane)
+    place = jnp.stack(
+        [core, block, plane, near_end, 3 - plane, 3 - near_end, at_end.astype(jnp.int32)]
+        + [plane, near, other, 6 - plane - near - other]
+    ).astype(jnp.int32)
+    row_count, block_width = hidden_input.shape
+    key_value_width = KEY_VALUE_HEADS // BLOCKS * HEAD_SIZE
+    key_value_begin = block * key_value_width
+
+    half_rows = row_count // 2
+    table = jnp.concatenate([lengths[0], adapter_of_request[0, :, 0]])
+    q_2 = along(query_weight, MIDDLE)
+    end_hidden = along(hidden_input, INWARD)
+    own_1, own_2 = swap_blocks(hidden_input, 1), swap_blocks(hidden_input, 2)
+    kv_0 = lax.dynamic_slice_in_dim(key_value_weight, key_value_begin, key_value_width, 2)
+    up_kv = lax.dynamic_slice_in_dim(adapter_up_key_value, key_value_begin, key_value_width, 3)
+    rest_0 = pack_rows(
+        table,
+        kv_0.reshape(-1, 2 * key_value_width),
+        adapter_down_qkv,
+        adapter_up_query,
+        up_kv.reshape(up_kv.shape[0], ADAPTER_RANK, 2 * key_value_width),
+        adapter_down_output,
+        adapter_up_output,
+    )
+    rest_0, end_hidden, q_2, own_1, own_2, query_later = gate(
+        [rest_0, end_hidden, q_2, own_1, own_2, query_weight], []
+    )
+    rest_1 = along(rest_0, INWARD)
+    rest_2 = along(rest_0, MIDDLE)
+    own_3 = swap_blocks(own_1[:half_rows], 2)
+    own_4 = swap_blocks(own_2[half_rows:], 1)
+    end_1, end_2 = swap_blocks(end_hidden, 1), swap_blocks(end_hidden, 2)
+    rest_1, rest_2, own_3, own_4, end_1, end_2, query_later = gate(
+        [rest_1, rest_2, own_3, own_4, end_1, end_2, query_later], []
+    )
+    end_table = rest_1[7 * ADAPTER_RANK, :8].astype(jnp.int32)
+    q_1 = along(query_later, INWARD)
+    rest_3 = along(rest_1, MIDDLE)
+    end_3 = swap_blocks(end_1[:half_rows], 2)
+    end_4 = swap_blocks(end_2[half_rows:], 1)
+    q_0x, q_2x = along(query_later, CORES), along(q_2, CORES)
+    rest_0x, rest_1x, rest_2x = (along(v, CORES) for v in (rest_0, rest_1, rest_2))
+
+    gain = input_norm_gain.astype(jnp.float32).reshape(BLOCKS, block_width)
+    x, own_done = norm_rows(place, gain, [hidden_input, own_1, own_2, own_3, own_4], 0, None)
+    x, end_done = norm_rows(place, gain, [end_hidden, end_1, end_2, end_3, end_4], 1, x)
+    wo_0 = jnp.transpose(output_weight, (1, 0, 2))
+    q_1, rest_3, wo_0 = gate(
+        [q_1, rest_3, wo_0], [q_0x, q_2x, rest_0x, rest_1x, rest_2x, end_done]
+    )
+    q_3 = along(q_1, MIDDLE)
+    wo_1 = along(wo_0, NEAR)
+    q_1x = along(q_1, CORES)
+    rest_3x = along(rest_3, CORES)
+
+    packed = [rest_0, rest_1, rest_2, rest_3, rest_0x, rest_1x, rest_2x, rest_3x]
+    low, chosen_own, chosen_end, up = rank_terms(
+        place, table, end_table, adapter_storage, x, packed, 2 * key_value_width
+    )
+    lows = [low] + to_blocks([low] * BLOCKS)
+    chosen_back = along(chosen_end, OUTWARD)
+
+    sums, first_done = project_first(
+        place,
+        x,
+        [query_weight, q_0x, q_1, q_1x, q_2, q_2x],
+        [v for pair in zip(packed[:4], packed[4:]) for v in pair],
+    )
+    q_3x = along(q_3, CORES)
+    wo_0, wo_1 = gate([wo_0, wo_1], [first_done, chosen_back] + lows)
+    wo_mid1, wo_mid2 = along(wo_0, MIDDLE), along(wo_1, MIDDLE)
+    raw_own, raw_end = project_last(
+        place, table, end_table, adapter_storage, x, [q_3, q_3x], up, lows, sums
+    )
+    raw_back = along(raw_end, OUTWARD)
+    wo_0x, wo_1x = along(wo_0, CORES), along(wo_1, CORES)
+    (wo_mid1,) = gate([wo_mid1], [raw_back, wo_0x, wo_1x])
+    wo_out2 = along(wo_mid1, OUTWARD)
+
+    cached = lax.dynamic_slice_in_dim(pool, key_value_begin, key_value_width, 2)
+    _, _, token_positions, _ = row_tables(
+        lengths[0], cached_prefix_pages[0], prefix_page_table[0], row_count
+    )
+    half_width = HEAD_SIZE // 2
+    inverse_freq = jnp.exp(
+        jnp.arange(half_width, dtype=jnp.float32) * (-2.0 / HEAD_SIZE) * math.log(rope_base)
+    )
+    angles = token_positions.astype(jnp.float32)[:, None] * inverse_freq[None, :]
+    cosine, sine = jnp.cos(angles), jnp.sin(angles)
+    attended, cache, low_out = attend(
+        place,
+        table,
+        cached_prefix_pages[0],
+        prefix_page_table[0].reshape(-1),
+        raw_own,
+        raw_back,
+        cached[:, 0],
+        cached[:, 1],
+        query_norm_gain.astype(jnp.float32)[None, :],
+        key_norm_gain.astype(jnp.float32)[None, :],
+        jnp.concatenate([cosine, cosine], axis=1),
+        jnp.concatenate([-sine, sine], axis=1),
+        chosen_own,
+        chosen_back,
+    )
+    new_cache = cache.reshape(row_count, 2, key_value_width)
+
+    near_parts = project_columns(
+        place, attended, [(wo_0, wo_0x, wo_0, wo_0x), (wo_1, wo_1x, wo_1, wo_1x)], low_out
+    )
+    parts = [near_parts[0]] + to_blocks(near_parts)
+    (wo_mid2,) = gate([wo_mid2], [attended])
+    wo_out3 = along(wo_mid2, OUTWARD)
+    (wo_out2,) = gate([wo_out2], near_parts[:1])
+    mid_parts = project_columns(
+        place, attended, [(wo_out2, along(wo_out2, CORES), wo_mid1, along(wo_mid1, CORES))]
+    )
+    parts += [mid_parts[0]] + to_blocks(mid_parts)
+    (wo_out3,) = gate([wo_out3], parts)
+    last_parts = project_columns(
+        place, attended, [(wo_out3, along(wo_out3, CORES), wo_mid2, along(wo_mid2, CORES))]
+    )
+    parts += [last_parts[0]] + to_blocks(last_parts)
+    attention_update = sum_columns(place, table, chosen_own, chosen_back, parts)
+    return (attention_update, new_cache)
+
+
 def solution(mesh):
     return jax.shard_map(
-        shards,
+        shards_by_plane if planes_fit(mesh) else shards,
         mesh=mesh,
         in_specs=(
             P("req", "mlp"),

time: 384 us -> 287 us (0.75)
  waiting for transfers between devices: 197 us -> 94.5 us
  blocking collectives: 93.4 us -> 0 us
  starting transfers between devices: 0.23 us -> 78.4 us
  Pallas kernels: 0 us -> 75.7 us
  matrix products: 29.5 us -> 0 us
  between operations: 14.7 us -> 1.17 us
  local copies, waits for them, and re-layouts: 40.1 us -> 28.2 us
    all_gather x5 -> x0, waiting for transfers between devices: 194 us -> none  [the longest x1 72.8 us: shards(): lax.all_gather(output_weight, 'req', axis=2, tiled=True)]
    ppermute x0 -> x48, waiting for transfers between devices: none -> 94.5 us  [the longest x28 46.9 us: along(): return lax.ppermute(value, 'req', pairs)]
    ppermute x0 -> x48, starting transfers between devices: none -> 78.4 us  [the longest x28 54.8 us: along(): return lax.ppermute(value, 'req', pairs)]
    pallas_call x0 -> x19, Pallas kernels: none -> 75.7 us  [the longest x3 15.9 us: project_columns(): pl.pallas_call(functools.partial(columns_kernel, len(chunks)), in_specs=[...]
    all_gather x4 -> x0, blocking collectives: 61.3 us -> none  [the longest x1 16.6 us: shards(): lax.all_gather(request_key_value_up, 'req', axis=0, tiled=True)]
    psum x2 -> x0, blocking collectives: 32.1 us -> none  [the longest x1 16.4 us: shards(): lax.psum(select_rows(out_terms, group_members), 'mlp').astype(jnp.bfloat16)]
    dot_general x12 -> x0, matrix products: 29.5 us -> none  [the longest x1 6.77 us: shards(): jnp.dot(normalized_input, q_part, preferred_element_type=jnp.float32)]
    reshape x1 -> x3, local copies, waits for them, and re-layouts: 11.4 us -> 2.09 us  [the longest x1 0.84 us: shards_by_plane(): new_cache = cache.reshape(row_count, 2, key_value_width)]
  transfers between devices with their start and end apart: 6 -> 48, of which waited for: 4 -> 20; matrix products, arithmetic and copies ran while one was open for 13% -> 9% of each run, Pallas kernels for 0% -> 24%
where the time goes in v1:
time: 287 us; the launch traced here: 284 us
  waiting for transfers between devices  94.5 us (33%)
  starting transfers between devices  78.4 us (27%)
  Pallas kernels  75.7 us (26%)
  local copies, waits for them, and re-layouts  28.2 us (10%)
  other arithmetic  5.95 us (2%)
    ppermute x28, starting transfers between devices, along(): return lax.ppermute(value, 'req', pairs)  54.8 us
    ppermute x28, waiting for transfers between devices, along(): return lax.ppermute(value, 'req', pairs)  46.9 us
    ppermute x8, waiting for transfers between devices, swap_blocks(): return lax.ppermute(value, 'mlp', [(b, b ^ k) for b in range(BLOCKS)])  27.7 us
    ppermute x12, waiting for transfers between devices, to_blocks(): lax.ppermute(piece, 'mlp', [(b, b ^ k) for b in range(BLOCKS)])  20 us
    pallas_call x3, Pallas kernels, project_columns(): pl.pallas_call(functools.partial(columns_kernel, len(chunks)), in_specs=[...  15.9 us
    pallas_call x1, Pallas kernels, project_first(): pl.pallas_call(first_kernel, grid=(6,), in_specs=[in_smem(), pl.BlockSpec...  14.9 us
    unnamed x97, local copies, waits for them, and re-layouts  14.1 us
    ppermute x12, starting transfers between devices, to_blocks(): lax.ppermute(piece, 'mlp', [(b, b ^ k) for b in range(BLOCKS)])  13.2 us
  transfers between devices with their start and end apart: 48, of which 20 were waited for; matrix products, arithmetic and copies ran while one was open for 9% of the time, Pallas kernels for 24%

profile of v1, /device:TPU:0, one launch (start us, length us, event | category | flops | bytes accessed | tf_op | source)
XLA Modules:
  0.0 284.0 jit_solution(7459245511839688235)
XLA Ops:
  2.5 7.7 %collective-permute-start = (bf16[384,1024]{1,0:T(8,128)(2,1)}, bf16[384,1024]{1,0:T(8,128)(2,1)}, u32[]{:S(2)}, u32[]{:S(2)}) collective-permute-start(bf16[384,1024]{1,0:T(8,128)(2,1)} %p0.1), channel_id=1, source_target_pairs={{0,8},{4,12},{24,16},{28,20},{1,9},{5,13},{25,17},{29,21},{2,10},{... | collective-permute-start | bytes 2359304 | tf_op jit(solution)/shard_map/ppermute | solution.py:245
  21.0 5.0 %collective-permute-done.refs_1_ = bf16[384,1024]{1,0:T(8,128)(2,1)} collective-permute-done((bf16[384,1024]{1,0:T(8,128)(2,1)}, bf16[384,1024]{1,0:T(8,128)(2,1)}, u32[]{:S(2)}, u32[]{:S(2)}) %collective-permute-start) | collective-permute-done | bytes 786464 | tf_op jit(solution)/shard_map/ppermute | solution.py:245
  26.0 3.0 %collective-permute-done.2.refs_3_ = bf16[384,1024]{1,0:T(8,128)(2,1)S(1)} collective-permute-done((bf16[384,1024]{1,0:T(8,128)(2,1)}, bf16[384,1024]{1,0:T(8,128)(2,1)S(1)}, u32[]{:S(2)}, u32[]{:S(2)}) %collective-permute-start.2) | collective-permute-done | bytes 786464 | tf_op jit(solution)/shard_map/ppermute | solution.py:249
  43.2 13.3 %collective-permute-done.7.refs_3_ = bf16[192,1024]{1,0:T(8,128)(2,1)S(1)} collective-permute-done((bf16[192,1024]{1,0:T(8,128)(2,1)S(1)}, bf16[192,1024]{1,0:T(8,128)(2,1)S(1)}, u32[]{:S(2)}, u32[]{:S(2)}) %collective-permute-start.7) | collective-permute-done | bytes 393248 | tf_op jit(solution)/shard_map/ppermute | solution.py:249
  66.1 4.6 %collective-permute-done.10.p3 = bf16[192,1024]{1,0:T(8,128)(2,1)S(1)} collective-permute-done((bf16[192,1024]{1,0:T(8,128)(2,1)S(1)}, bf16[192,1024]{1,0:T(8,128)(2,1)S(1)}, u32[]{:S(2)}, u32[]{:S(2)}) %collective-permute-start.10) | collective-permute-done | bytes 393248 | tf_op jit(solution)/shard_map/ppermute | solution.py:249
  73.2 4.3 %collective-permute-start.12 = (bf16[512,1024]{1,0:T(8,128)(2,1)}, bf16[512,1024]{1,0:T(8,128)(2,1)}, u32[]{:S(2)}, u32[]{:S(2)}) collective-permute-start(bf16[512,1024]{1,0:T(8,128)(2,1)} %get-tuple-element.59), channel_id=1, source_target_pairs={{0,8},{4,12},{24,16},{28,20},{1,9},{5,13},{25,17},{29,21},{2,10},{... | collective-permute-start | bytes 3145736 | tf_op jit(solution)/shard_map/ppermute | solution.py:245
  81.1 5.8 %norm_rows.2 = (bf16[4,768,1024]{2,1,0:T(8,128)(2,1)}, f32[8,128]{1,0:T(8,128)}) custom-call(s32[11]{0:T(128)} %stack.48.place, f32[4,1024]{1,0:T(4,128)} %reshape.49.gain, bf16[384,1024]{1,0:T(8,128)(2,1)} %p0.1, bf16[384,1024]{1,0:T(8,128)(2,1)} %get-tuple-element.47.p1, bf16[384,1024]{1,0:T(8,128)(2,1)} %get-tuple-element.48.p2, ...), custom_call_target="tpu_custom_call" | custom-call | flops 6291456 | bytes 6291456 | tf_op jit(solution)/shard_map/norm_rows/pallas_call | solution.py:347
  86.9 5.8 %norm_rows.3 = (bf16[4,768,1024]{2,1,0:T(8,128)(2,1)}, f32[8,128]{1,0:T(8,128)}) custom-call(s32[11]{0:T(128)} %stack.48.place, f32[4,1024]{1,0:T(4,128)} %reshape.49.gain, bf16[384,1024]{1,0:T(8,128)(2,1)} %get-tuple-element.49.p0, bf16[384,1024]{1,0:T(8,128)(2,1)} %get-tuple-element.52.p1, ...), custom_call_target="tpu_custom_call", output_to_operand_aliasing={{0}: (7, {})} | custom-call | flops 6291456 | bytes 6291456 | tf_op jit(solution)/shard_map/norm_rows/pallas_call | solution.py:347
  92.8 5.2 %collective-permute-done.12.refs_0_ = bf16[512,1024]{1,0:T(8,128)(2,1)} collective-permute-done((bf16[512,1024]{1,0:T(8,128)(2,1)}, bf16[512,1024]{1,0:T(8,128)(2,1)}, u32[]{:S(2)}, u32[]{:S(2)}) %collective-permute-start.12) | collective-permute-done | bytes 1048608 | tf_op jit(solution)/shard_map/ppermute | solution.py:245
  100.7 25.9 %collective-permute-start.28 = (bf16[4,1024,128]{2,1,0:T(8,128)(2,1)}, bf16[4,1024,128]{2,1,0:T(8,128)(2,1)S(1)}, u32[]{:S(2)}, u32[]{:S(2)}) collective-permute-start(bf16[4,1024,128]{2,1,0:T(8,128)(2,1)} %get-tuple-element.72.refs_0_), channel_id=1, source_target_pairs={{0,8},{4,12},{8,0},{12,4},{16,24},{20,28},{24,16},{28,20},{1,9},{5... | collective-permute-start | bytes 3145736 | tf_op jit(solution)/shard_map/ppermute | solution.py:245
  127.6 6.4 %rank_terms.1 = (bf16[48,768]{1,0:T(8,128)(2,1)}, bf16[4,32,1024]{2,1,0:T(8,128)(2,1)}, bf16[4,32,1024]{2,1,0:T(8,128)(2,1)}, bf16[256,1536]{1,0:T(8,128)(2,1)}) custom-call(s32[11]{0:T(128)} %stack.48.place, s32[8]{0:T(128)} %pad_add_fusion.table.own_table.refs_0_, s32[8]{0:T(128)} %bitcast_convert_fusion.2.end_table.refs_1_, s32[16]{0:T(128)} %refs_2_.1, ...), custom_call_target="tpu_custom_call" | custom-call | flops 1207959552 | bytes 6815744 | tf_op jit(solution)/shard_map/rank_terms/pallas_call | solution.py:458
  137.6 14.9 %project_first.1 = (f32[768,1536]{1,0:T(8,128)}, f32[8,128]{1,0:T(8,128)}) custom-call(s32[11]{0:T(128)} %stack.48.place, bf16[4,768,1024]{2,1,0:T(8,128)(2,1)} %get-tuple-element.57.x, bf16[512,1024]{1,0:T(8,128)(2,1)} %refs_0_.1, bf16[512,1024]{1,0:T(8,128)(2,1)} %collective-permute-done.14.refs_3_.refs_1_, bf16[512,1024]{1,0:T(8,128)(2,1)} %get-tuple-element.65.refs_2_, ...), custom_call_target="tpu_custom_call" | custom-call | flops 8053063680 | bytes 21495808 | tf_op jit(solution)/shard_map/project_first/pallas_call | solution.py:506
  154.9 9.4 %project_last.1 = (bf16[384,1536]{1,0:T(8,128)(2,1)}, bf16[384,1536]{1,0:T(8,128)(2,1)}) custom-call(s32[11]{0:T(128)} %stack.48.place, bf16[4,768,1024]{2,1,0:T(8,128)(2,1)} %get-tuple-element.57.x, bf16[512,1024]{1,0:T(8,128)(2,1)} %copy-done.25, bf16[512,1024]{1,0:T(8,128)(2,1)} %copy-done.26, bf16[256,1536]{1,0:T(8,128)(2,1)} %get-tuple-element.66.up, ...), custom_call_target="tpu_custom_call" | custom-call | flops 3019898880 | bytes 10747904 | tf_op jit(solution)/shard_map/project_last/pallas_call | solution.py:566
  171.0 22.9 %collective-permute-done.27.back.refs_1_ = bf16[384,1536]{1,0:T(8,128)(2,1)} collective-permute-done((bf16[384,1536]{1,0:T(8,128)(2,1)}, bf16[384,1536]{1,0:T(8,128)(2,1)}, u32[]{:S(2)}, u32[]{:S(2)}) %collective-permute-start.27) | collective-permute-done | bytes 1179680 | tf_op jit(solution)/shard_map/ppermute | solution.py:245
  196.3 3.4 %constant_dynamic-slice_fusion.1 = (bf16[512,1,256]{2,1,0:T(2,128)(2,1)}, bf16[512,1,256]{2,1,0:T(2,128)(2,1)}) fusion(bf16[512,2,1024]{2,1,0:T(2,128)(2,1)} %param.30, s32[]{:T(128)S(6)} %add.29, s32[]{:T(128)S(6)} %select_n.45), kind=kLoop, calls=%fused_computation.13 | loop fusion | bytes 1048584 | tf_op jit(solution)/shard_map/slice | solution.py:917
  204.5 11.7 %attend.1 = (bf16[384,1024]{1,0:T(8,128)(2,1)}, bf16[384,512]{1,0:T(8,128)(2,1)}, f32[16,384]{1,0:T(8,128)}) custom-call(s32[11]{0:T(128)} %stack.48.place, s32[8]{0:T(128)} %pad_add_fusion.table.own_table.refs_0_, s32[4]{0:T(128)} %bitcast.47, s32[32]{0:T(128)} %reshape_squeeze.3.pages, bf16[384,1536]{1,0:T(8,128)(2,1)} %get-tuple-element.69.own, ...), custom_call_target="tpu_custom_call" | custom-call | flops 1409286144 | bytes 2359296 | tf_op jit(solution)/shard_map/attend/pallas_call | solution.py:667
  216.3 5.6 %project_columns.3 = (bf16[400,512]{1,0:T(8,128)(2,1)}, bf16[400,512]{1,0:T(8,128)(2,1)}, bf16[400,512]{1,0:T(8,128)(2,1)}, bf16[400,512]{1,0:T(8,128)(2,1)}) custom-call(s32[11]{0:T(128)} %stack.48.place, bf16[384,1024]{1,0:T(8,128)(2,1)} %get-tuple-element.71.attended.refs_1_, bf16[4,1024,128]{2,1,0:T(8,128)(2,1)} %get-tuple-element.74.refs_0_.refs_2_, ...), custom_call_target="tpu_custom_call" | custom-call | flops 1677721600 | bytes 6651904 | tf_op jit(solution)/shard_map/project_columns/pallas_call | solution.py:732
  230.1 5.2 %project_columns.4 = (bf16[384,256]{1,0:T(8,128)(2,1)}, bf16[384,256]{1,0:T(8,128)(2,1)}, bf16[384,256]{1,0:T(8,128)(2,1)}, bf16[384,256]{1,0:T(8,128)(2,1)}) custom-call(s32[11]{0:T(128)} %stack.48.place, bf16[384,1024]{1,0:T(8,128)(2,1)} %get-tuple-element.71.attended.refs_1_, bf16[4,1024,128]{2,1,0:T(8,128)(2,1)} %gate.13.refs_0_, ...), custom_call_target="tpu_custom_call" | custom-call | flops 805306368 | bytes 3670016 | tf_op jit(solution)/shard_map/project_columns/pallas_call | solution.py:732
  240.1 9.2 %collective-permute-done.32.refs_3_.refs_2_ = bf16[400,512]{1,0:T(8,128)(2,1)S(1)} collective-permute-done((bf16[400,512]{1,0:T(8,128)(2,1)}, bf16[400,512]{1,0:T(8,128)(2,1)S(1)}, u32[]{:S(2)}, u32[]{:S(2)}) %collective-permute-start.32) | collective-permute-done | bytes 409632 | tf_op jit(solution)/shard_map/ppermute | solution.py:254
  249.4 7.5 %collective-permute-done.42.refs_0_ = bf16[4,1024,128]{2,1,0:T(8,128)(2,1)S(1)} collective-permute-done((bf16[4,1024,128]{2,1,0:T(8,128)(2,1)}, bf16[4,1024,128]{2,1,0:T(8,128)(2,1)S(1)}, u32[]{:S(2)}, u32[]{:S(2)}) %collective-permute-start.42) | collective-permute-done | bytes 1048608 | tf_op jit(solution)/shard_map/ppermute | solution.py:245
  261.8 5.1 %project_columns.5 = (bf16[384,256]{1,0:T(8,128)(2,1)}, bf16[384,256]{1,0:T(8,128)(2,1)}, bf16[384,256]{1,0:T(8,128)(2,1)}, bf16[384,256]{1,0:T(8,128)(2,1)}) custom-call(s32[11]{0:T(128)} %stack.48.place, bf16[384,1024]{1,0:T(8,128)(2,1)} %get-tuple-element.71.attended.refs_1_, bf16[4,1024,128]{2,1,0:T(8,128)(2,1)} %gate.15.refs_0_, ...), custom_call_target="tpu_custom_call" | custom-call | flops 805306368 | bytes 3670016 | tf_op jit(solution)/shard_map/project_columns/pallas_call | solution.py:732
  271.3 3.6 %collective-permute-done.45.refs_9_ = bf16[384,256]{1,0:T(8,128)(2,1)S(1)} collective-permute-done((bf16[384,256]{1,0:T(8,128)(2,1)}, bf16[384,256]{1,0:T(8,128)(2,1)S(1)}, u32[]{:S(2)}, u32[]{:S(2)}) %collective-permute-start.45) | collective-permute-done | bytes 196640 | tf_op jit(solution)/shard_map/ppermute | solution.py:254
  275.0 4.6 %collective-permute-done.46.refs_10_ = bf16[384,256]{1,0:T(8,128)(2,1)S(1)} collective-permute-done((bf16[384,256]{1,0:T(8,128)(2,1)}, bf16[384,256]{1,0:T(8,128)(2,1)S(1)}, u32[]{:S(2)}, u32[]{:S(2)}) %collective-permute-start.46) | collective-permute-done | bytes 196640 | tf_op jit(solution)/shard_map/ppermute | solution.py:254
  280.3 3.6 %sum_columns.1 = bf16[384,1024]{1,0:T(8,128)(2,1)} custom-call(s32[11]{0:T(128)} %stack.48.place, s32[8]{0:T(128)} %pad_add_fusion.table.own_table.refs_0_, bf16[4,32,1024]{2,1,0:T(8,128)(2,1)} %get-tuple-element.63.chosen_own, bf16[4,32,1024]{2,1,0:T(8,128)(2,1)} %copy-done.24, bf16[400,512]{1,0:T(8,128)(2,1)} %get-tuple-element.77.refs_1_.refs_0_, ...), custom_call_target="tpu_custom_call" | custom-call | flops 56623104 | bytes 4718592 | tf_op jit(solution)/shard_map/sum_columns/pallas_call | solution.py:781
  (213 shorter events, 89.0 us)
Async XLA Ops:
  0.6 29.7 %collective-permute-start.1 = (bf16[512,1024]{1,0:T(8,128)(2,1)}, bf16[512,1024]{1,0:T(8,128)(2,1)}, u32[]{:S(2)}, u32[]{:S(2)}) collective-permute-start(bf16[512,1024]{1,0:T(8,128)(2,1)} %refs_0_.1), channel_id=1, source_target_pairs={{8,16},{12,20},{16,8},{20,12},{9,17},{13,21},{17,9},{21,13},{10,18... | collective-permute-start | bytes 3145736 | tf_op jit(solution)/shard_map/ppermute | solution.py:245
  2.5 23.6 %collective-permute-start = (bf16[384,1024]{1,0:T(8,128)(2,1)}, bf16[384,1024]{1,0:T(8,128)(2,1)}, u32[]{:S(2)}, u32[]{:S(2)}) collective-permute-start(bf16[384,1024]{1,0:T(8,128)(2,1)} %p0.1), channel_id=1, source_target_pairs={{0,8},{4,12},{24,16},{28,20},{1,9},{5,13},{25,17},{29,21},{2,10},{... | collective-permute-start | bytes 2359304 | tf_op jit(solution)/shard_map/ppermute | solution.py:245
  10.1 18.9 %collective-permute-start.2 = (bf16[384,1024]{1,0:T(8,128)(2,1)}, bf16[384,1024]{1,0:T(8,128)(2,1)S(1)}, u32[]{:S(2)}, u32[]{:S(2)}) collective-permute-start(bf16[384,1024]{1,0:T(8,128)(2,1)} %p0.1), channel_id=1, source_target_pairs={{0,1},{1,0},{2,3},{3,2},{4,5},{5,4},{6,7},{7,6},{8,9},{9,8},{10,11... | collective-permute-start | bytes 2359304 | tf_op jit(solution)/shard_map/ppermute | solution.py:249
  30.4 26.2 %collective-permute-start.8 = (bf16[384,1024]{1,0:T(8,128)(2,1)}, bf16[384,1024]{1,0:T(8,128)(2,1)S(1)}, u32[]{:S(2)}, u32[]{:S(2)}) collective-permute-start(bf16[384,1024]{1,0:T(8,128)(2,1)} %get-tuple-element.49.p0), channel_id=1, source_target_pairs={{0,1},{1,0},{2,3},{3,2},{4,5},{5,4},{6,7},{7,6},{8,9},{9,8},{10,11... | collective-permute-start | bytes 2359304 | tf_op jit(solution)/shard_map/ppermute | solution.py:249
  35.0 21.5 %collective-permute-start.7 = (bf16[192,1024]{1,0:T(8,128)(2,1)S(1)}, bf16[192,1024]{1,0:T(8,128)(2,1)S(1)}, u32[]{:S(2)}, u32[]{:S(2)}) collective-permute-start(bf16[192,1024]{1,0:T(8,128)(2,1)S(1)} %slice.22), channel_id=1, source_target_pairs={{0,1},{1,0},{2,3},{3,2},{4,5},{5,4},{6,7},{7,6},{8,9},{9,8},{10,11... | collective-permute-start | bytes 1179656 | tf_op jit(solution)/shard_map/ppermute | solution.py:249
  36.1 23.5 %collective-permute-start.4 = (bf16[512,1024]{1,0:T(8,128)(2,1)}, bf16[512,1024]{1,0:T(8,128)(2,1)S(1)}, u32[]{:S(2)}, u32[]{:S(2)}) collective-permute-start(bf16[512,1024]{1,0:T(8,128)(2,1)} %get-tuple-element.46.refs_0_.refs_6_.refs_7_), channel_id=1, source_target_pairs={{0,8},{4,12},{24,16},{28,20},{1,9},{5,13},{25,17},{29,21},{2,10},{... | collective-permute-start | bytes 3145736 | tf_op jit(solution)/shard_map/ppermute | solution.py:245
  38.6 20.9 %collective-permute-start.5 = (bf16[512,1024]{1,0:T(8,128)(2,1)}, bf16[512,1024]{1,0:T(8,128)(2,1)}, u32[]{:S(2)}, u32[]{:S(2)}) collective-permute-start(bf16[512,1024]{1,0:T(8,128)(2,1)} %get-tuple-element.46.refs_0_.refs_6_.refs_7_), channel_id=1, source_target_pairs={{8,16},{12,20},{16,8},{20,12},{9,17},{13,21},{17,9},{21,13},{10,18... | collective-permute-start | bytes 3145736 | tf_op jit(solution)/shard_map/ppermute | solution.py:245
  64.8 27.9 %collective-permute-start.17 = (bf16[512,1024]{1,0:T(8,128)(2,1)}, bf16[512,1024]{1,0:T(8,128)(2,1)S(1)}, u32[]{:S(2)}, u32[]{:S(2)}) collective-permute-start(bf16[512,1024]{1,0:T(8,128)(2,1)} %get-tuple-element.51.refs_1_.refs_10_.refs_11_), channel_id=1, source_target_pairs={{0,4},{4,0},{8,12},{12,8},{16,20},{20,16},{24,28},{28,24},{1,5},{5... | collective-permute-start | bytes 3145736 | tf_op jit(solution)/shard_map/ppermute | solution.py:245
  64.8 28.0 %collective-permute-start.13 = (bf16[512,1024]{1,0:T(8,128)(2,1)}, bf16[512,1024]{1,0:T(8,128)(2,1)S(1)}, u32[]{:S(2)}, u32[]{:S(2)}) collective-permute-start(bf16[512,1024]{1,0:T(8,128)(2,1)} %get-tuple-element.51.refs_1_.refs_10_.refs_11_), channel_id=1, source_target_pairs={{8,16},{12,20},{16,8},{20,12},{9,17},{13,21},{17,9},{21,13},{10,18... | collective-permute-start | bytes 3145736 | tf_op jit(solution)/shard_map/ppermute | solution.py:245
  65.5 27.2 %collective-permute-start.18 = (bf16[512,1024]{1,0:T(8,128)(2,1)}, bf16[512,1024]{1,0:T(8,128)(2,1)S(1)}, u32[]{:S(2)}, u32[]{:S(2)}) collective-permute-start(bf16[512,1024]{1,0:T(8,128)(2,1)} %get-tuple-element.58.refs_2_.refs_14_.refs_15_), channel_id=1, source_target_pairs={{0,4},{4,0},{8,12},{12,8},{16,20},{20,16},{24,28},{28,24},{1,5},{5... | collective-permute-start | bytes 3145736 | tf_op jit(solution)/shard_map/ppermute | solution.py:245
  70.7 22.1 %collective-permute-start.14 = (bf16[512,1024]{1,0:T(8,128)(2,1)}, bf16[512,1024]{1,0:T(8,128)(2,1)}, u32[]{:S(2)}, u32[]{:S(2)}) collective-permute-start(bf16[512,1024]{1,0:T(8,128)(2,1)} %get-tuple-element.59), channel_id=1, source_target_pairs={{0,4},{4,0},{8,12},{12,8},{16,20},{20,16},{24,28},{28,24},{1,5},{5... | collective-permute-start | bytes 3145736 | tf_op jit(solution)/shard_map/ppermute | solution.py:245
  73.2 24.8 %collective-permute-start.12 = (bf16[512,1024]{1,0:T(8,128)(2,1)}, bf16[512,1024]{1,0:T(8,128)(2,1)}, u32[]{:S(2)}, u32[]{:S(2)}) collective-permute-start(bf16[512,1024]{1,0:T(8,128)(2,1)} %get-tuple-element.59), channel_id=1, source_target_pairs={{0,8},{4,12},{24,16},{28,20},{1,9},{5,13},{25,17},{29,21},{2,10},{... | collective-permute-start | bytes 3145736 | tf_op jit(solution)/shard_map/ppermute | solution.py:245
  98.7 27.9 %collective-permute-start.19 = (bf16[512,1024]{1,0:T(8,128)(2,1)}, bf16[512,1024]{1,0:T(8,128)(2,1)S(1)}, u32[]{:S(2)}, u32[]{:S(2)}) collective-permute-start(bf16[512,1024]{1,0:T(8,128)(2,1)} %get-tuple-element.62.refs_3_.refs_18_.refs_19_), channel_id=1, source_target_pairs={{0,4},{4,0},{8,12},{12,8},{16,20},{20,16},{24,28},{28,24},{1,5},{5... | collective-permute-start | bytes 3145736 | tf_op jit(solution)/shard_map/ppermute | solution.py:245
  98.8 37.7 %collective-permute-start.23 = (bf16[512,1024]{1,0:T(8,128)(2,1)}, bf16[512,1024]{1,0:T(8,128)(2,1)S(1)}, u32[]{:S(2)}, u32[]{:S(2)}) collective-permute-start(bf16[512,1024]{1,0:T(8,128)(2,1)} %get-tuple-element.65.refs_2_), channel_id=1, source_target_pairs={{0,4},{4,0},{8,12},{12,8},{16,20},{20,16},{24,28},{28,24},{1,5},{5... | collective-permute-start | bytes 3145736 | tf_op jit(solution)/shard_map/ppermute | solution.py:245
  99.3 54.5 %collective-permute-start.22 = (bf16[512,1024]{1,0:T(8,128)(2,1)S(1)}, bf16[512,1024]{1,0:T(8,128)(2,1)S(1)}, u32[]{:S(2)}, u32[]{:S(2)}) collective-permute-start(bf16[512,1024]{1,0:T(8,128)(2,1)S(1)} %collective-permute-done.21.q_core), channel_id=1, source_target_pairs={{0,4},{4,0},{8,12},{12,8},{16,20},{20,16},{24,28},{28,24},{1,5},{5... | collective-permute-start | bytes 3145736 | tf_op jit(solution)/shard_map/ppermute | solution.py:245
  100.7 64.9 %collective-permute-start.28 = (bf16[4,1024,128]{2,1,0:T(8,128)(2,1)}, bf16[4,1024,128]{2,1,0:T(8,128)(2,1)S(1)}, u32[]{:S(2)}, u32[]{:S(2)}) collective-permute-start(bf16[4,1024,128]{2,1,0:T(8,128)(2,1)} %get-tuple-element.72.refs_0_), channel_id=1, source_target_pairs={{0,8},{4,12},{8,0},{12,4},{16,24},{20,28},{24,16},{28,20},{1,9},{5... | collective-permute-start | bytes 3145736 | tf_op jit(solution)/shard_map/ppermute | solution.py:245
  164.2 29.7 %collective-permute-start.27 = (bf16[384,1536]{1,0:T(8,128)(2,1)}, bf16[384,1536]{1,0:T(8,128)(2,1)}, u32[]{:S(2)}, u32[]{:S(2)}) collective-permute-start(bf16[384,1536]{1,0:T(8,128)(2,1)} %get-tuple-element.70), channel_id=1, source_target_pairs={{8,0},{12,4},{16,24},{20,28},{9,1},{13,5},{17,25},{21,29},{10,2},{... | collective-permute-start | bytes 3538952 | tf_op jit(solution)/shard_map/ppermute | solution.py:245
  194.0 29.1 %collective-permute-start.35 = (bf16[4,1024,128]{2,1,0:T(8,128)(2,1)}, bf16[4,1024,128]{2,1,0:T(8,128)(2,1)S(1)}, u32[]{:S(2)}, u32[]{:S(2)}) collective-permute-start(bf16[4,1024,128]{2,1,0:T(8,128)(2,1)} %gate.12.refs_2_), channel_id=1, source_target_pairs={{8,0},{12,4},{16,24},{20,28},{9,1},{13,5},{17,25},{21,29},{10,2},{... | collective-permute-start | bytes 3145736 | tf_op jit(solution)/shard_map/ppermute | solution.py:245
  199.7 24.4 %collective-permute-start.41 = (bf16[4,1024,128]{2,1,0:T(8,128)(2,1)S(1)}, bf16[4,1024,128]{2,1,0:T(8,128)(2,1)S(1)}, u32[]{:S(2)}, u32[]{:S(2)}) collective-permute-start(bf16[4,1024,128]{2,1,0:T(8,128)(2,1)S(1)} %copy-done.3), channel_id=1, source_target_pairs={{8,16},{12,20},{16,8},{20,12},{9,17},{13,21},{17,9},{21,13},{10,18... | collective-permute-start | bytes 3145736 | tf_op jit(solution)/shard_map/ppermute | solution.py:245
  204.5 24.6 %collective-permute-start.37 = (bf16[4,1024,128]{2,1,0:T(8,128)(2,1)}, bf16[4,1024,128]{2,1,0:T(8,128)(2,1)}, u32[]{:S(2)}, u32[]{:S(2)}) collective-permute-start(bf16[4,1024,128]{2,1,0:T(8,128)(2,1)} %gate.12.refs_2_), channel_id=1, source_target_pairs={{0,4},{4,0},{8,12},{12,8},{16,20},{20,16},{24,28},{28,24},{1,5},{5... | collective-permute-start | bytes 3145736 | tf_op jit(solution)/shard_map/ppermute | solution.py:245
  225.1 31.8 %collective-permute-start.42 = (bf16[4,1024,128]{2,1,0:T(8,128)(2,1)}, bf16[4,1024,128]{2,1,0:T(8,128)(2,1)S(1)}, u32[]{:S(2)}, u32[]{:S(2)}) collective-permute-start(bf16[4,1024,128]{2,1,0:T(8,128)(2,1)} %gate.14.refs_2_), channel_id=1, source_target_pairs={{8,0},{12,4},{16,24},{20,28},{9,1},{13,5},{17,25},{21,29},{10,2},{... | collective-permute-start | bytes 3145736 | tf_op jit(solution)/shard_map/ppermute | solution.py:245
  228.1 21.2 %collective-permute-start.32 = (bf16[400,512]{1,0:T(8,128)(2,1)}, bf16[400,512]{1,0:T(8,128)(2,1)S(1)}, u32[]{:S(2)}, u32[]{:S(2)}) collective-permute-start(bf16[400,512]{1,0:T(8,128)(2,1)} %get-tuple-element.79), channel_id=1, source_target_pairs={{0,2},{1,3},{2,0},{3,1},{4,6},{5,7},{6,4},{7,5},{8,10},{9,11},{10,... | collective-permute-start | bytes 1228808 | tf_op jit(solution)/shard_map/ppermute | solution.py:254
  229.1 20.2 %collective-permute-start.33 = (bf16[400,512]{1,0:T(8,128)(2,1)}, bf16[400,512]{1,0:T(8,128)(2,1)S(1)}, u32[]{:S(2)}, u32[]{:S(2)}) collective-permute-start(bf16[400,512]{1,0:T(8,128)(2,1)} %get-tuple-element.80), channel_id=1, source_target_pairs={{0,3},{1,2},{2,1},{3,0},{4,7},{5,6},{6,5},{7,4},{8,11},{9,10},{10,... | collective-permute-start | bytes 1228808 | tf_op jit(solution)/shard_map/ppermute | solution.py:254
  235.3 21.6 %collective-permute-start.38 = (bf16[384,256]{1,0:T(8,128)(2,1)}, bf16[384,256]{1,0:T(8,128)(2,1)S(1)}, u32[]{:S(2)}, u32[]{:S(2)}) collective-permute-start(bf16[384,256]{1,0:T(8,128)(2,1)} %get-tuple-element.82), channel_id=1, source_target_pairs={{0,1},{1,0},{2,3},{3,2},{4,5},{5,4},{6,7},{7,6},{8,9},{9,8},{10,11... | collective-permute-start | bytes 589832 | tf_op jit(solution)/shard_map/ppermute | solution.py:254
  (71 other events, 596.9 us)

commit v2 on v1

--- a/solution.py
+++ b/solution.py
@@ -261,13 +261,14 @@
     del refs
 
 
-def gate(values, earlier):
+def gate(values, earlier, mebibytes=60):
     return pl.pallas_call(
         gate_kernel,
         in_specs=[pl.BlockSpec(memory_space=pl.ANY)] * (len(values) + len(earlier)),
         out_specs=[pl.BlockSpec(memory_space=pl.ANY)] * len(values),
         out_shape=[jax.ShapeDtypeStruct(v.shape, v.dtype) for v in values],
         input_output_aliases={i: i for i in range(len(values))},
+        compiler_params=kernel_params(mebibytes),
         name="gate",
     )(*values, *earlier)
 
@@ -286,8 +287,8 @@
     )
 
 
-def kernel_params():
-    return pltpu.CompilerParams(vmem_limit_bytes=56 * 1024 * 1024)
+def kernel_params(mebibytes):
+    return pltpu.CompilerParams(vmem_limit_bytes=mebibytes * 1024 * 1024)
 
 
 def request_of_rows(table, shape, axis):
@@ -331,42 +332,44 @@
     core = place[0]
     for k, v in enumerate(pieces):
         normed = (v * scale * gain[pl.ds(place[1] ^ k, 1), :]).astype(jnp.bfloat16)
-        out[k, :, core_columns(core, half)] = normed[:, :half]
-        out[k, :, core_columns(1 - core, half)] = normed[:, half:]
+        first = 2 * place[11 + k]
+        out[:, core_columns(first + core, half)] = normed[:, :half]
+        out[:, core_columns(first + 1 - core, half)] = normed[:, half:]
     done[...] = jnp.zeros(done.shape, jnp.float32)
 
 
 def norm_rows(place, gain, pieces, group, given):
-    rows, width = pieces[0].shape
-    tiles = 4
+    tiles, width = 4, gain.shape[1]
+    rows = pieces[0][0].shape[0]
     tile = rows // tiles
     more = [] if given is None else [given]
-    whole = pl.BlockSpec((tile, width), lambda i, place: (i, 0))
-    front = pl.BlockSpec((tile, width), lambda i, place: (jnp.minimum(i, tiles // 2 - 1), 0))
-    back = pl.BlockSpec((tile, width), lambda i, place: (jnp.maximum(i - tiles // 2, 0), 0))
+    index = [lambda i: i] * 3
+    index += [lambda i: jnp.minimum(i, tiles // 2 - 1), lambda i: jnp.maximum(i - tiles // 2, 0)]
     return pl.pallas_call(
         norm_kernel,
         grid_spec=pltpu.PrefetchScalarGridSpec(
             num_scalar_prefetch=1,
             grid=(tiles,),
             in_specs=[pl.BlockSpec((BLOCKS, width), lambda i, place: (0, 0))]
-            + [whole] * 3
-            + [front, back]
+            + [
+                pl.BlockSpec((tile, width), lambda i, place, f=f, at=at: (f + at(i), 0))
+                for (_, f), at in zip(pieces, index)
+            ]
             + [pl.BlockSpec(memory_space=pl.ANY)] * len(more),
             out_specs=[
-                pl.BlockSpec((BLOCKS, tile, width), lambda i, place: (0, tiles * group + i, 0)),
+                pl.BlockSpec((tile, BLOCKS * width), lambda i, place: (tiles * group + i, 0)),
                 pl.BlockSpec((8, 128), lambda i, place: (0, 0)),
             ],
         ),
         out_shape=[
-            jax.ShapeDtypeStruct((BLOCKS, GROUPS * rows, width), jnp.bfloat16),
+            jax.ShapeDtypeStruct((GROUPS * rows, BLOCKS * width), jnp.bfloat16),
             jax.ShapeDtypeStruct((8, 128), jnp.float32),
         ],
         input_output_aliases={7: 0} if more else {},
-        compiler_params=kernel_params(),
+        compiler_params=kernel_params(56),
         cost_estimate=cost(16 * rows * width, 4 * BLOCKS * rows * width),
         name="norm_rows",
-    )(place, gain, *pieces, *more)
+    )(place, gain, *[p for p, _ in pieces], *more)
 
 
 SLOT_ROWS = 128
@@ -403,17 +406,17 @@
         in_specs=[in_smem()] + [in_vmem()] * 6,
         out_specs=in_vmem(),
         out_shape=jax.ShapeDtypeStruct((2 * SLOT_ROWS + kv.shape[0] // 2, width), jnp.bfloat16),
-        compiler_params=kernel_params(),
+        compiler_params=kernel_params(56),
         cost_estimate=cost(0, 4 * width * (2 * SLOT_ROWS + kv.shape[0] // 2), 0),
         name="pack_rows",
     )(table, kv, *adapters)
 
 
 def rank_kernel(place, own_table, end_table, storage, x, *refs):
-    packed, (low, chosen_own, chosen_end, up, down) = refs[:8], refs[8:]
+    packed, (low, chosen_own, chosen_end, up, up_kv, down) = refs[:8], refs[8:]
     slots = slot_list(place)
-    rank, rows, q_width = ADAPTER_RANK, x.shape[1] // GROUPS, x.shape[2]
-    kv_columns, half, core = up.shape[1] - q_width, q_width // 2, place[0]
+    rank, rows, q_width = ADAPTER_RANK, x.shape[0] // GROUPS, x.shape[1]
+    kv_columns, half, core = up_kv.shape[1], q_width // 2, place[0]
     for t, ref in enumerate(packed):
         for s in range(2):
             i, first = 2 * t + s, s * SLOT_ROWS
@@ -421,14 +424,14 @@
                 down[3 * rank * i : 3 * rank * (i + 1), columns] = ref[
                     first : first + 3 * rank, core_columns(c, half)
                 ]
-            up[rank * i : rank * (i + 1), :q_width] = ref[first + 3 * rank : first + 4 * rank, :]
-            up[rank * i : rank * (i + 1), q_width:] = ref[
+            up[rank * i : rank * (i + 1), :] = ref[first + 3 * rank : first + 4 * rank, :]
+            up_kv[rank * i : rank * (i + 1), :] = ref[
                 first + 4 * rank : first + 5 * rank, :kv_columns
             ]
     for g, (table, chosen) in enumerate(((own_table, chosen_own), (end_table, chosen_end))):
         terms = lax.dot_general(
             down[...],
-            x[0, g * rows : (g + 1) * rows, :],
+            x[g * rows : (g + 1) * rows, :],
             (((1,), (1,)), ((), ())),
             preferred_element_type=jnp.float32,
         )
@@ -448,145 +451,126 @@
 
 
 def rank_terms(place, own_table, end_table, storage, x, packed, kv_columns):
-    _, rows, width = x.shape
+    rows, width = x.shape[0], x.shape[1] // BLOCKS
     chosen = jax.ShapeDtypeStruct((4, 2 * ADAPTER_RANK, width), jnp.bfloat16)
-    up = jax.ShapeDtypeStruct((16 * ADAPTER_RANK, width + kv_columns), jnp.bfloat16)
+    up = jax.ShapeDtypeStruct((16 * ADAPTER_RANK, width), jnp.bfloat16)
+    up_kv = jax.ShapeDtypeStruct((16 * ADAPTER_RANK, kv_columns), jnp.bfloat16)
     low = jax.ShapeDtypeStruct((3 * ADAPTER_RANK, rows), jnp.bfloat16)
-    first = pl.BlockSpec((1, rows, width), lambda i: (0, 0, 0))
-    slots = pl.BlockSpec((2 * SLOT_ROWS, width), lambda i: (0, 0))
-    whole = lambda shape: pl.BlockSpec(shape, lambda i: (0,) * len(shape))
+    slots = pl.BlockSpec((2 * SLOT_ROWS, width), lambda i, place: (0, 0))
+    whole = lambda shape: pl.BlockSpec(shape, lambda i, place: (0,) * len(shape))
     return pl.pallas_call(
         rank_kernel,
-        grid=(1,),
-        in_specs=[in_smem()] * 4 + [first] + [slots] * 8,
-        out_specs=[whole(v.shape) for v in (low, chosen, chosen, up)],
-        out_shape=[low, chosen, chosen, up],
-        scratch_shapes=[pltpu.VMEM((16 * 3 * ADAPTER_RANK, width), jnp.bfloat16)],
-        compiler_params=kernel_params(),
-        cost_estimate=cost(2 * 16 * 3 * ADAPTER_RANK * rows * width, 2 * width * (rows + 18 * SLOT_ROWS + 256), 0),
+        grid_spec=pltpu.PrefetchScalarGridSpec(
+            num_scalar_prefetch=1,
+            grid=(1,),
+            in_specs=[in_smem()] * 3
+            + [pl.BlockSpec((rows, width), lambda i, place: (0, place[11]))]
+            + [slots] * 8,
+            out_specs=[whole(v.shape) for v in (low, chosen, chosen, up, up_kv)],
+            scratch_shapes=[pltpu.VMEM((16 * 3 * ADAPTER_RANK, width), jnp.bfloat16)],
+        ),
+        out_shape=[low, chosen, chosen, up, up_kv],
+        compiler_params=kernel_params(56),
+        cost_estimate=cost(
+            2 * 16 * 3 * ADAPTER_RANK * rows * width, 2 * width * (rows + 18 * SLOT_ROWS + 256)
+        ),
         name="rank_terms",
     )(place, own_table, end_table, storage, x, *packed)
 
 
-def first_kernel(place, x, *refs):
-    weights, packed, (out, done) = refs[:6], refs[6:22], refs[22:]
-    half, depth = x.shape[2] // 2, packed[0].shape[0]
-    step = pl.program_id(0)
-
-    @pl.when(step < 4)
-    def _():
-        total = None
-        for i, w in enumerate(weights):
-            k, c = place[2 + i // 2] ^ place[1], i % 2
-            term = dot(x[k, :, c * half : (c + 1) * half], w[...])
-            total = term if total is None else total + term
-        out[...] = total
-
-    @pl.when(step >= 4)
-    def _():
-        total = None
-        for i, w in enumerate(packed):
-            k, c = place[2 + i // 4] ^ place[1], i % 4
-            term = dot(x[k, :, c * depth : (c + 1) * depth], w[...])
-            total = term if total is None else total + term
-        out[...] = total
-
-    done[...] = jnp.zeros(done.shape, jnp.float32)
-
-
-def project_first(place, x, queries, packed):
-    _, rows, width = x.shape
-    depth = queries[0].shape[0]
-    tile = pl.BlockSpec((rows, WIDE), lambda n: (0, n))
-    query = pl.BlockSpec((depth, WIDE), lambda n: (0, jnp.minimum(n, 3)))
-    key_values = [
-        pl.BlockSpec((depth // 2, WIDE), lambda n, b=b: (1, b + jnp.maximum(n - 4, 0)))
-        for b in (0, 2)
-    ]
+def spread_ranks(place, tables, storage, lows, part, spread):
+    rank = ADAPTER_RANK
+    rows = spread.shape[0] // GROUPS
+    slots = slot_list(place)
+    low = sum(v[part * rank : (part + 1) * rank].astype(jnp.float32) for v in lows)
+    low = low.astype(jnp.bfloat16).astype(jnp.float32)
+    for g, table in enumerate(tables):
+        row_slots = slots_of_rows(table, storage, rows)
+        mine = low[:, g * rows : (g + 1) * rows]
+        wide = jnp.concatenate([jnp.where(row_slots == s, mine, 0.0) for s in slots], axis=0)
+        spread[g * rows : (g + 1) * rows, :] = wide.T.astype(jnp.bfloat16)
+
+
+def project_kernel(is_q, place, own_table, end_table, storage, x, *refs):
+    sources, lows, up = refs[:8], refs[8:12], refs[12]
+    own, end, spread, held, x_held, sems = refs[13:]
+    rows, width = own.shape[0], x.shape[1] // BLOCKS
+    depth = held.shape[0] // 8
+
+    def copies(chunk):
+        block = slice(chunk * width, (chunk + 1) * width)
+        first = 0 if is_q else 2 * SLOT_ROWS
+        return [pltpu.make_async_copy(x.at[:, block], x_held.at[:, block], sems.at[chunk, 2])] + [
+            pltpu.make_async_copy(
+                sources[2 * chunk + c].at[first:, :],
+                held.at[(2 * chunk + c) * depth : (2 * chunk + c + 1) * depth, :],
+                sems.at[chunk, c],
+            )
+            for c in range(2)
+        ]
+
+    for chunk in range(BLOCKS):
+        for copy in copies(chunk):
+            copy.start()
+    tables = (own_table, end_table)
+    total = None
+    if is_q:
+        spread_ranks(place, tables, storage, lows, 0, spread)
+        low = dot(spread[...], up[...])
+    else:
+        low = []
+        for part in range(2):
+            spread_ranks(place, tables, storage, lows, 1 + part, spread)
+            low.append(dot(spread[...], up[:, part * WIDE : (part + 1) * WIDE]))
+        low = jnp.concatenate(low, axis=1)
+    for chunk in range(BLOCKS):
+        for copy in copies(chunk):
+            copy.wait()
+        w = held[2 * chunk * depth : 2 * (chunk + 1) * depth, :]
+        if not is_q:
+            columns = own.shape[1]
+            w = jnp.concatenate(
+                [
+                    w[c * depth : (c + 1) * depth, h * columns : (h + 1) * columns]
+                    for c in range(2)
+                    for h in range(2)
+                ],
+                axis=0,
+            )
+        term = dot(x_held[:, chunk * width : (chunk + 1) * width], w)
+        total = low + term if total is None else total + term
+    total = total.astype(jnp.bfloat16)
+    own[...] = total[:rows]
+    end[...] = total[rows:]
+
+
+def project(place, own_table, end_table, storage, x, sources, lows, up, is_q):
+    rows, width = x.shape[0], x.shape[1] // BLOCKS
+    columns = up.shape[1]
+    anywhere = pl.BlockSpec(memory_space=pl.ANY)
     return pl.pallas_call(
-        first_kernel,
-        grid=(6,),
-        in_specs=[in_smem(), pl.BlockSpec(x.shape, lambda n: (0, 0, 0))]
-        + [query] * 6
-        + key_values * 8,
-        out_specs=[tile, pl.BlockSpec((8, 128), lambda n: (0, 0))],
-        out_shape=[
-            jax.ShapeDtypeStruct((rows, 6 * WIDE), jnp.float32),
-            jax.ShapeDtypeStruct((8, 128), jnp.float32),
+        functools.partial(project_kernel, is_q),
+        in_specs=[in_smem()] * 4 + [anywhere] * 9 + [in_vmem()] * 5,
+        out_specs=[in_vmem()] * 2,
+        out_shape=[jax.ShapeDtypeStruct((rows // GROUPS, columns), jnp.bfloat16)] * 2,
+        scratch_shapes=[
+            pltpu.VMEM((rows, 16 * ADAPTER_RANK), jnp.bfloat16),
+            pltpu.VMEM(((8 if is_q else 4) * sources[0].shape[0], width), jnp.bfloat16),
+            pltpu.VMEM(x.shape, jnp.bfloat16),
+            pltpu.SemaphoreType.DMA((BLOCKS, 3)),
         ],
-        compiler_params=kernel_params(),
-        cost_estimate=cost(2 * rows * width * (3 * width + 2 * width), 8 * rows * width + 2 * width * (3 * width + 2 * width) + 24 * rows * WIDE, 0),
-        name="project_first",
-    )(place, x, *queries, *[p for p in packed for _ in range(2)])
-
-
-def last_kernel(place, x, q_core, q_other, up, given, *refs):
-    own_table, end_table, storage = refs[:3]
-    lows, (own, end, spread) = refs[3:7], refs[7:]
-    rank, rows, half = ADAPTER_RANK, x.shape[1] // GROUPS, x.shape[2] // 2
-    step = pl.program_id(0)
-    for part, at in enumerate((0, 4, 5)):
-
-        @pl.when(step == at)
-        def _(part=part):
-            slots = slot_list(place)
-            low = sum(v[part * rank : (part + 1) * rank].astype(jnp.float32) for v in lows)
-            low = low.astype(jnp.bfloat16).astype(jnp.float32)
-            for g, table in enumerate((own_table, end_table)):
-                row_slots = slots_of_rows(table, storage, rows)
-                mine = low[:, g * rows : (g + 1) * rows]
-                wide = jnp.concatenate([jnp.where(row_slots == s, mine, 0.0) for s in slots], axis=0)
-                spread[g * rows : (g + 1) * rows, :] = wide.T.astype(jnp.bfloat16)
-
-    @pl.when(step < 4)
-    def _():
-        total = (
-            given[...]
-            + dot(spread[...], up[...])
-            + dot(x[0, :, :half], q_core[...])
-            + dot(x[0, :, half:], q_other[...])
-        ).astype(jnp.bfloat16)
-        own[...] = total[:rows]
-        end[...] = total[rows:]
-
-    @pl.when(step >= 4)
-    def _():
-        total = (given[...] + dot(spread[...], up[...])).astype(jnp.bfloat16)
-        own[...] = total[:rows]
-        end[...] = total[rows:]
-
-
-def project_last(place, own_table, end_table, storage, x, queries, up, lows, sums):
-    _, rows, width = x.shape
-    depth = queries[0].shape[0]
-    features = pl.BlockSpec((1, rows, width), lambda n, place: (place[5] ^ place[1], 0, 0))
-    tile = pl.BlockSpec((rows // GROUPS, WIDE), lambda n, place: (0, n))
-    query = pl.BlockSpec((depth, WIDE), lambda n, place: (0, jnp.minimum(n, 3)))
-    low = pl.BlockSpec(lows[0].shape, lambda n, place: (0, 0))
-    return pl.pallas_call(
-        last_kernel,
-        grid_spec=pltpu.PrefetchScalarGridSpec(
-            num_scalar_prefetch=1,
-            grid=(6,),
-            in_specs=[features]
-            + [query] * 2
-            + [pl.BlockSpec((up.shape[0], WIDE), lambda n, place: (0, n))]
-            + [pl.BlockSpec((rows, WIDE), lambda n, place: (0, n))]
-            + [in_smem()] * 3
-            + [low] * 4,
-            out_specs=[tile, tile],
-            scratch_shapes=[pltpu.VMEM((rows, 16 * ADAPTER_RANK), jnp.bfloat16)],
+        compiler_params=kernel_params(56),
+        cost_estimate=cost(
+            2 * rows * (BLOCKS * width + 256) * columns,
+            2 * BLOCKS * width * (rows + columns) + 2 * rows * columns,
         ),
-        out_shape=[jax.ShapeDtypeStruct((rows // GROUPS, 6 * WIDE), jnp.bfloat16)] * 2,
-        compiler_params=kernel_params(),
-        cost_estimate=cost(2 * rows * (width + 256) * 6 * WIDE, 2 * rows * width + 2 * width * width + 36 * rows * WIDE, 0),
-        name="project_last",
-    )(place, x, *queries, up, sums, own_table, end_table, storage, *lows)
+        name="project_query" if is_q else "project_key_value",
+    )(place, own_table, end_table, storage, x, *sources, *lows, up)
 
 
 def attention_kernel(
-    place, table, prefix, pages, own, back, k_pool, v_pool, q_gain, k_gain, cosine, sine,
-    chosen_own, chosen_back, out, cache, low, raw, keys, values, allowed, down,
+    place, table, prefix, pages, own, back, kv_own, kv_back, k_pool, v_pool, q_gain, k_gain,
+    cosine, sine, chosen_own, chosen_back, out, cache, low, raw, raw_kv, keys, values, allowed, down,
 ):
     rows, pool_rows = own.shape[0], k_pool.shape[0]
     page_count = pool_rows // PAGE
@@ -594,11 +578,13 @@
     @pl.when(place[6] == 1)
     def _():
         raw[...] = back[...]
+        raw_kv[...] = kv_back[...]
         down[...] = chosen_back[:, :ADAPTER_RANK, :].reshape(down.shape)
 
     @pl.when(place[6] == 0)
     def _():
         raw[...] = own[...]
+        raw_kv[...] = kv_own[...]
         down[...] = chosen_own[:, :ADAPTER_RANK, :].reshape(down.shape)
 
     owner = request_of_rows(table, (rows, 1), 0)
@@ -626,17 +612,15 @@
     q_width = out.shape[1]
     per_key = q_width // HEAD_SIZE // kv_heads
     kv_width = kv_heads * HEAD_SIZE
-    cache[:, kv_width:] = raw[:, q_width + kv_width :]
+    cache[:, kv_width:] = raw_kv[:, kv_width:]
     for h in range(kv_heads):
         head = slice(h * HEAD_SIZE, (h + 1) * HEAD_SIZE)
         keys[:pool_rows] = k_pool[:, head]
         values[:pool_rows] = v_pool[:, head]
-        k_new = turned(raw[:, q_width + h * HEAD_SIZE : q_width + (h + 1) * HEAD_SIZE], k_gain)
+        k_new = turned(raw_kv[:, head], k_gain)
         keys[pool_rows:] = k_new
         cache[:, head] = k_new
-        values[pool_rows:] = raw[
-            :, q_width + kv_width + h * HEAD_SIZE : q_width + kv_width + (h + 1) * HEAD_SIZE
-        ]
+        values[pool_rows:] = raw_kv[:, kv_width + h * HEAD_SIZE : kv_width + (h + 1) * HEAD_SIZE]
         for g in range(per_key):
             place_q = slice((h * per_key + g) * HEAD_SIZE, (h * per_key + g + 1) * HEAD_SIZE)
             query = turned(raw[:, place_q], q_gain)
@@ -658,15 +642,14 @@
     )
 
 
-def attend(place, table, prefix, pages, own, back, k_pool, v_pool, q_gain, k_gain, cosine, sine,
-           chosen_own, chosen_back):
-    rows = own.shape[0]
+def attend(place, table, prefix, pages, own, back, kv_own, kv_back, k_pool, v_pool, q_gain, k_gain,
+           cosine, sine, chosen_own, chosen_back):
+    rows, q_width = own.shape
     kv_width = k_pool.shape[1]
-    q_width = own.shape[1] - 2 * kv_width
     keys = k_pool.shape[0] + rows
     return pl.pallas_call(
         attention_kernel,
-        in_specs=[in_smem()] * 4 + [in_vmem()] * 10,
+        in_specs=[in_smem()] * 4 + [in_vmem()] * 12,
         out_specs=[in_vmem()] * 3,
         out_shape=[
             jax.ShapeDtypeStruct((rows, q_width), jnp.bfloat16),
@@ -675,73 +658,89 @@
         ],
         scratch_shapes=[
             pltpu.VMEM(own.shape, jnp.bfloat16),
+            pltpu.VMEM(kv_own.shape, jnp.bfloat16),
             pltpu.VMEM((keys, HEAD_SIZE), jnp.bfloat16),
             pltpu.VMEM((keys, HEAD_SIZE), jnp.bfloat16),
             pltpu.VMEM((rows, keys), jnp.int32),
             pltpu.VMEM((4 * ADAPTER_RANK, chosen_own.shape[2]), jnp.bfloat16),
         ],
-        compiler_params=kernel_params(),
+        compiler_params=kernel_params(56),
         cost_estimate=cost(4 * rows * keys * q_width, 6 * rows * q_width, rows * keys * (q_width // HEAD_SIZE)),
         name="attend",
-    )(place, table, prefix, pages, own, back, k_pool, v_pool, q_gain, k_gain, cosine, sine,
-      chosen_own, chosen_back)
+    )(place, table, prefix, pages, own, back, kv_own, kv_back, k_pool, v_pool, q_gain, k_gain,
+      cosine, sine, chosen_own, chosen_back)
 
 
 def columns_kernel(count, place, attended, *refs):
-    sources, outs, (held, sems) = refs[: 4 * count], refs[-2 - BLOCKS : -2], refs[-2:]
+    sources, rest = refs[: 4 * count], refs[4 * count :]
+    low = rest[0] if len(rest) > 2 * BLOCKS + 4 else None
+    outs, made, (rows_held, held, sems, out_sems) = rest[-2 * BLOCKS - 4 : -BLOCKS - 4], rest[-BLOCKS - 4 : -4], rest[-4:]
     rows = attended.shape[0]
-    if len(refs) > 4 * count + BLOCKS + 2:
-        low = refs[4 * count]
-        for out in outs:
-            out[rows:, :rows] = low[...].astype(jnp.bfloat16)
-            out[rows:, rows:] = jnp.zeros((low.shape[0], out.shape[1] - rows), jnp.bfloat16)
     at_end = place[6] == 1
 
     def copies(chunk, end, k):
         pair = sources[4 * chunk + (0 if end else 2) :][:2]
         return [
             pltpu.make_async_copy(
-                pair[c].at[place[1] ^ k],
-                held.at[k, :, (2 * chunk + c) * HEAD_SIZE : (2 * chunk + c + 1) * HEAD_SIZE],
-                sems.at[chunk, k, c],
+                pair[c].at[place[1] ^ k], held.at[chunk, c, k], sems.at[chunk, k, c]
             )
             for c in range(2)
         ]
 
+    given = pltpu.make_async_copy(attended, rows_held, sems.at[count, 0, 0])
+    given.start()
     for end in (True, False):
 
         @pl.when(at_end if end else jnp.logical_not(at_end))
         def _(end=end):
-            for k in range(BLOCKS):
+            for k in (3, 2, 1, 0):
                 for chunk in range(count):
                     for copy in copies(chunk, end, k):
                         copy.start()
 
-    for k in range(BLOCKS):
+    given.wait()
+    sent = []
+    for k in (3, 2, 1, 0):
         for chunk in range(count):
             for copy in copies(chunk, False, k):
                 copy.wait()
-        outs[k][:rows] = dot(attended[...], held[k]).astype(jnp.bfloat16)
-
-
-def project_columns(place, attended, chunks, low=None):
+        w = jnp.concatenate([held[chunk, c, k] for chunk in range(count) for c in range(2)], axis=1)
+        made[k][:rows] = dot(rows_held[...], w).astype(jnp.bfloat16)
+        if low is not None:
+            made[k][rows:, :rows] = low[...].astype(jnp.bfloat16)
+            made[k][rows:, rows:] = jnp.zeros(
+                (low.shape[0], made[k].shape[1] - rows), jnp.bfloat16
+            )
+        sent.append(pltpu.make_async_copy(made[k], outs[k], out_sems.at[k]))
+        sent[-1].start()
+    for copy in sent:
+        copy.wait()
+
+
+def project_columns(place, attended, chunks, low=None, mebibytes=56):
     more = [] if low is None else [low]
     rows = attended.shape[0] + (0 if low is None else low.shape[0])
     depth = chunks[0][0].shape[1]
     width = WIDE * len(chunks)
     return pl.pallas_call(
         functools.partial(columns_kernel, len(chunks)),
-        in_specs=[in_smem(), in_vmem()]
-        + [pl.BlockSpec(memory_space=pl.ANY)] * (4 * len(chunks))
+        in_specs=[in_smem()]
+        + [pl.BlockSpec(memory_space=pl.ANY)] * (1 + 4 * len(chunks))
         + [in_vmem()] * len(more),
-        out_specs=[in_vmem()] * BLOCKS,
+        out_specs=[pl.BlockSpec(memory_space=pl.ANY)] * BLOCKS,
         out_shape=[jax.ShapeDtypeStruct((rows, width), jnp.bfloat16)] * BLOCKS,
-        scratch_shapes=[
-            pltpu.VMEM((BLOCKS, depth, width), jnp.bfloat16),
-            pltpu.SemaphoreType.DMA((len(chunks), BLOCKS, 2)),
+        scratch_shapes=[pltpu.VMEM((rows, width), jnp.bfloat16)] * BLOCKS
+        + [
+            pltpu.VMEM(attended.shape, jnp.bfloat16),
+            pltpu.VMEM((len(chunks), 2, BLOCKS, depth, HEAD_SIZE), jnp.bfloat16),
+            pltpu.SemaphoreType.DMA((len(chunks) + 1, BLOCKS, 2)),
+            pltpu.SemaphoreType.DMA((BLOCKS,)),
         ],
-        compiler_params=kernel_params(),
-        cost_estimate=cost(2 * rows * depth * BLOCKS * width, 2 * (rows * depth + depth * BLOCKS * width + rows * BLOCKS * width), 0),
+        compiler_params=kernel_params(mebibytes),
+        cost_estimate=cost(
+            2 * rows * depth * BLOCKS * width,
+            2 * (rows * depth + depth * BLOCKS * width + rows * BLOCKS * width),
+        ),
         name="project_columns",
     )(place, attended, *[w for chunk in chunks for w in chunk], *more)
 
@@ -784,7 +783,7 @@
         out_specs=in_vmem(),
         out_shape=jax.ShapeDtypeStruct((rows, width), jnp.bfloat16),
         scratch_shapes=[pltpu.VMEM((4 * ADAPTER_RANK, width), jnp.bfloat16)],
-        compiler_params=kernel_params(),
+        compiler_params=kernel_params(56),
         cost_estimate=cost(2 * rows * width * (8 + 4 * ADAPTER_RANK), 12 * rows * width, 0),
         name="sum_columns",
     )(place, table, chosen_own, chosen_back, *parts)
@@ -814,12 +813,13 @@
     plane, core = request_index // 2, request_index % 2
     block = lax.axis_index("mlp")
     at_end = (plane == 0) | (plane == PLANES - 1)
-    near_end = jnp.where(plane < 2, 0, PLANES - 1)
-    near = jnp.where(at_end, jnp.where(plane == 0, 1, 2), near_end)
+    near = plane ^ 1
+    inner = [core, block, plane, near, 3 - plane, 3 - near]
     other = jnp.where(at_end, jnp.where(plane == 0, 2, 1), 3 - plane)
     place = jnp.stack(
-        [core, block, plane, near_end, 3 - plane, 3 - near_end, at_end.astype(jnp.int32)]
+        inner + [at_end.astype(jnp.int32)]
         + [plane, near, other, 6 - plane - near - other]
+        + [sum(i * (p == block ^ k).astype(jnp.int32) for i, p in enumerate(inner[2:])) for k in range(BLOCKS)]
     ).astype(jnp.int32)
     row_count, block_width = hidden_input.shape
     key_value_width = KEY_VALUE_HEADS // BLOCKS * HEAD_SIZE
@@ -841,71 +841,90 @@
         adapter_down_output,
         adapter_up_output,
     )
-    rest_0, end_hidden, q_2, own_1, own_2, query_later = gate(
-        [rest_0, end_hidden, q_2, own_1, own_2, query_weight], []
+    _, _, token_positions, _ = row_tables(
+        lengths[0], cached_prefix_pages[0], prefix_page_table[0], row_count
+    )
+    half_width = HEAD_SIZE // 2
+    inverse_freq = jnp.exp(
+        jnp.arange(half_width, dtype=jnp.float32) * (-2.0 / HEAD_SIZE) * math.log(rope_base)
+    )
+    angles = token_positions.astype(jnp.float32)[:, None] * inverse_freq[None, :]
+    cosine, sine = jnp.cos(angles), jnp.sin(angles)
+    cosine = jnp.concatenate([cosine, cosine], axis=1)
+    sine = jnp.concatenate([-sine, sine], axis=1)
+    cached = lax.dynamic_slice_in_dim(pool, key_value_begin, key_value_width, 2)
+    k_pool, v_pool = cached[:, 0], cached[:, 1]
+    wo_0 = jnp.transpose(output_weight, (1, 0, 2))
+
+    to_1 = jnp.concatenate([end_hidden, own_2[half_rows:]], axis=0)
+    to_2 = jnp.concatenate([end_hidden, own_1[:half_rows]], axis=0)
+    rest_0, to_1, to_2, q_2, query_later, cosine, sine, k_pool, v_pool, wo_0 = gate(
+        [rest_0, to_1, to_2, q_2, query_weight, cosine, sine, k_pool, v_pool, wo_0], []
     )
     rest_1 = along(rest_0, INWARD)
     rest_2 = along(rest_0, MIDDLE)
-    own_3 = swap_blocks(own_1[:half_rows], 2)
-    own_4 = swap_blocks(own_2[half_rows:], 1)
-    end_1, end_2 = swap_blocks(end_hidden, 1), swap_blocks(end_hidden, 2)
-    rest_1, rest_2, own_3, own_4, end_1, end_2, query_later = gate(
-        [rest_1, rest_2, own_3, own_4, end_1, end_2, query_later], []
-    )
+    from_1, from_2 = swap_blocks(to_1, 1), swap_blocks(to_2, 2)
+    q_0x, q_2x, rest_0x = (along(v, CORES) for v in (query_later, q_2, rest_0))
+
+    rest_1, rest_2, from_1, from_2, query_later = gate(
+        [rest_1, rest_2, from_1, from_2, query_later], [q_0x, q_2x, rest_0x]
+    )
+    half_1, half_2 = from_1[:half_rows], from_2[half_rows:row_count]
     end_table = rest_1[7 * ADAPTER_RANK, :8].astype(jnp.int32)
     q_1 = along(query_later, INWARD)
     rest_3 = along(rest_1, MIDDLE)
-    end_3 = swap_blocks(end_1[:half_rows], 2)
-    end_4 = swap_blocks(end_2[half_rows:], 1)
-    q_0x, q_2x = along(query_later, CORES), along(q_2, CORES)
-    rest_0x, rest_1x, rest_2x = (along(v, CORES) for v in (rest_0, rest_1, rest_2))
+    end_3, end_4 = swap_blocks(half_1, 2), swap_blocks(half_2, 1)
 
     gain = input_norm_gain.astype(jnp.float32).reshape(BLOCKS, block_width)
-    x, own_done = norm_rows(place, gain, [hidden_input, own_1, own_2, own_3, own_4], 0, None)
-    x, end_done = norm_rows(place, gain, [end_hidden, end_1, end_2, end_3, end_4], 1, x)
-    wo_0 = jnp.transpose(output_weight, (1, 0, 2))
-    q_1, rest_3, wo_0 = gate(
-        [q_1, rest_3, wo_0], [q_0x, q_2x, rest_0x, rest_1x, rest_2x, end_done]
-    )
+    own_pieces = [(hidden_input, 0), (own_1, 0), (own_2, 0), (from_2, 4), (from_1, 4)]
+    end_pieces = [(end_hidden, 0), (from_1, 0), (from_2, 0), (end_3, 0), (end_4, 0)]
+    x, own_done = norm_rows(place, gain, own_pieces, 0, None)
+    x, end_done = norm_rows(place, gain, end_pieces, 1, x)
+    q_1, rest_1, rest_2, rest_3, wo_0 = gate([q_1, rest_1, rest_2, rest_3, wo_0], [end_done])
     q_3 = along(q_1, MIDDLE)
     wo_1 = along(wo_0, NEAR)
+    rest_1x, rest_2x, rest_3x = (along(v, CORES) for v in (rest_1, rest_2, rest_3))
     q_1x = along(q_1, CORES)
-    rest_3x = along(rest_3, CORES)
 
     packed = [rest_0, rest_1, rest_2, rest_3, rest_0x, rest_1x, rest_2x, rest_3x]
-    low, chosen_own, chosen_end, up = rank_terms(
+    low, chosen_own, chosen_end, up, up_kv = rank_terms(
         place, table, end_table, adapter_storage, x, packed, 2 * key_value_width
     )
     lows = [low] + to_blocks([low] * BLOCKS)
     chosen_back = along(chosen_end, OUTWARD)
 
-    sums, first_done = project_first(
+    kv_own, kv_end = project(
         place,
+        table,
+        end_table,
+        adapter_storage,
         x,
-        [query_weight, q_0x, q_1, q_1x, q_2, q_2x],
         [v for pair in zip(packed[:4], packed[4:]) for v in pair],
-    )
+        lows,
+        up_kv,
+        False,
+    )
+    kv_back = along(kv_end, OUTWARD)
+    q_3, wo_0, wo_1 = gate([q_3, wo_0, wo_1], [kv_own])
     q_3x = along(q_3, CORES)
-    wo_0, wo_1 = gate([wo_0, wo_1], [first_done, chosen_back] + lows)
     wo_mid1, wo_mid2 = along(wo_0, MIDDLE), along(wo_1, MIDDLE)
-    raw_own, raw_end = project_last(
-        place, table, end_table, adapter_storage, x, [q_3, q_3x], up, lows, sums
-    )
+    raw_own, raw_end = project(
+        place,
+        table,
+        end_table,
+        adapter_storage,
+        x,
+        [query_weight, q_0x, q_1, q_1x, q_2, q_2x, q_3, q_3x],
+        lows,
+        up,
+        True,
+    )
+    raw_end, kv_back, chosen_back = gate([raw_end, kv_back, chosen_back], [])
     raw_back = along(raw_end, OUTWARD)
     wo_0x, wo_1x = along(wo_0, CORES), along(wo_1, CORES)
-    (wo_mid1,) = gate([wo_mid1], [raw_back, wo_0x, wo_1x])
+    wo_mid1, raw_back = gate([wo_mid1, raw_back], [wo_0x, wo_1x])
     wo_out2 = along(wo_mid1, OUTWARD)
 
-    cached = lax.dynamic_slice_in_dim(pool, key_value_begin, key_value_width, 2)
-    _, _, token_positions, _ = row_tables(
-        lengths[0], cached_prefix_pages[0], prefix_page_table[0], row_count
-    )
-    half_width = HEAD_SIZE // 2
-    inverse_freq = jnp.exp(
-        jnp.arange(half_width, dtype=jnp.float32) * (-2.0 / HEAD_SIZE) * math.log(rope_base)
-    )
-    angles = token_positions.astype(jnp.float32)[:, None] * inverse_freq[None, :]
-    cosine, sine = jnp.cos(angles), jnp.sin(angles)
     attended, cache, low_out = attend(
         place,
         table,
@@ -913,31 +932,36 @@
         prefix_page_table[0].reshape(-1),
         raw_own,
         raw_back,
-        cached[:, 0],
-        cached[:, 1],
+        kv_own,
+        kv_back,
+        k_pool,
+        v_pool,
         query_norm_gain.astype(jnp.float32)[None, :],
         key_norm_gain.astype(jnp.float32)[None, :],
-        jnp.concatenate([cosine, cosine], axis=1),
-        jnp.concatenate([-sine, sine], axis=1),
+        cosine,
+        sine,
         chosen_own,
         chosen_back,
     )
     new_cache = cache.reshape(row_count, 2, key_value_width)
 
+    attended, wo_mid2 = gate([attended, wo_mid2], [])
+    wo_out3 = along(wo_mid2, OUTWARD)
     near_parts = project_columns(
         place, attended, [(wo_0, wo_0x, wo_0, wo_0x), (wo_1, wo_1x, wo_1, wo_1x)], low_out
     )
     parts = [near_parts[0]] + to_blocks(near_parts)
-    (wo_mid2,) = gate([wo_mid2], [attended])
-    wo_out3 = along(wo_mid2, OUTWARD)
     (wo_out2,) = gate([wo_out2], near_parts[:1])
     mid_parts = project_columns(
         place, attended, [(wo_out2, along(wo_out2, CORES), wo_mid1, along(wo_mid1, CORES))]
     )
     parts += [mid_parts[0]] + to_blocks(mid_parts)
-    (wo_out3,) = gate([wo_out3], parts)
+    (wo_out3,) = gate([wo_out3], parts[:5], 1)
     last_parts = project_columns(
-        place, attended, [(wo_out3, along(wo_out3, CORES), wo_mid2, along(wo_mid2, CORES))]
+        place,
+        attended,
+        [(wo_out3, along(wo_out3, CORES), wo_mid2, along(wo_mid2, CORES))],
+        mebibytes=12,
     )
     parts += [last_parts[0]] + to_blocks(last_parts)
     attention_update = sum_columns(place, table, chosen_own, chosen_back, parts)

time: 287 us -> 250 us (0.87)
  starting transfers between devices: 78.4 us -> 57 us
  waiting for transfers between devices: 94.5 us -> 81 us
  Pallas kernels: 75.7 us -> 70.6 us
  other arithmetic: 5.95 us -> 8.89 us
    ppermute x8 -> x6, waiting for transfers between devices: 27.7 us -> 3.01 us  [swap_blocks(): return lax.ppermute(value, 'mlp', [(b, b ^ k) for b in range(BLOCKS)])]
    ppermute x28 -> x29, starting transfers between devices: 54.8 us -> 34.7 us  [along(): return lax.ppermute(value, 'req', pairs)]
    ppermute x28 -> x29, waiting for transfers between devices: 46.9 us -> 56.1 us  [along(): return lax.ppermute(value, 'req', pairs)]
    unnamed x97 -> x103, local copies, waits for them, and re-layouts: 14.1 us -> 19.3 us
    pallas_call x3, Pallas kernels: 30.7 us -> 26.4 us  [the longest x2 19.3 us: project(): pl.pallas_call(functools.partial(project_kernel, is_q), in_specs=[in_smem...]
    ppermute x8 -> x6, starting transfers between devices: 10.3 us -> 8.22 us  [swap_blocks(): return lax.ppermute(value, 'mlp', [(b, b ^ k) for b in range(BLOCKS)])]
  transfers between devices with their start and end apart: 48 -> 47, of which waited for: 20 -> 18; matrix products, arithmetic and copies ran while one was open for 9% -> 10% of each run, Pallas kernels for 24% -> 27%
where the time goes in v2:
time: 250 us; the launch traced here: 249 us
  waiting for transfers between devices  81 us (32%)
  Pallas kernels  70.6 us (28%)
  starting transfers between devices  57 us (23%)
  local copies, waits for them, and re-layouts  30.1 us (12%)
  other arithmetic  8.89 us (4%)
    ppermute x29, waiting for transfers between devices, along(): return lax.ppermute(value, 'req', pairs)  56.1 us
    ppermute x29, starting transfers between devices, along(): return lax.ppermute(value, 'req', pairs)  34.7 us
    ppermute x12, waiting for transfers between devices, to_blocks(): lax.ppermute(piece, 'mlp', [(b, b ^ k) for b in range(BLOCKS)])  21.9 us
    pallas_call x2, Pallas kernels, project(): pl.pallas_call(functools.partial(project_kernel, is_q), in_specs=[in_smem...  19.3 us
    unnamed x103, local copies, waits for them, and re-layouts  19.3 us
    pallas_call x3, Pallas kernels, project_columns(): pl.pallas_call(functools.partial(columns_kernel, len(chunks)), in_specs=[...  14.7 us
    ppermute x12, starting transfers between devices, to_blocks(): lax.ppermute(piece, 'mlp', [(b, b ^ k) for b in range(BLOCKS)])  14.1 us
    pallas_call x1, Pallas kernels, attend(): pl.pallas_call(attention_kernel, in_specs=[in_smem()] * 4 + [in_vmem()] *...  11.8 us
  transfers between devices with their start and end apart: 47, of which 18 were waited for; matrix products, arithmetic and copies ran while one was open for 10% of the time, Pallas kernels for 27%

profile of v2, /device:TPU:0, one launch (start us, length us, event | category | flops | bytes accessed | tf_op | source)
XLA Modules:
  0.0 248.7 jit_solution(123874341023494617)
XLA Ops:
  0.6 3.0 %collective-permute-start.1 = (bf16[384,1024]{1,0:T(8,128)(2,1)}, bf16[384,1024]{1,0:T(8,128)(2,1)}, u32[]{:S(2)}, u32[]{:S(2)}) collective-permute-start(bf16[384,1024]{1,0:T(8,128)(2,1)} %p0.1), channel_id=1, source_target_pairs={{0,2},{1,3},{2,0},{3,1},{4,6},{5,7},{6,4},{7,5},{8,10},{9,11},{10,... | collective-permute-start | bytes 2359304 | tf_op jit(solution)/shard_map/ppermute | solution.py:249
  5.2 3.5 %collective-permute-start = (bf16[384,1024]{1,0:T(8,128)(2,1)}, bf16[384,1024]{1,0:T(8,128)(2,1)S(1)}, u32[]{:S(2)}, u32[]{:S(2)}) collective-permute-start(bf16[384,1024]{1,0:T(8,128)(2,1)} %p0.1), channel_id=1, source_target_pairs={{0,8},{4,12},{24,16},{28,20},{1,9},{5,13},{25,17},{29,21},{2,10},{... | collective-permute-start | bytes 2359304 | tf_op jit(solution)/shard_map/ppermute | solution.py:245
  30.3 6.2 %collective-permute-start.4 = (bf16[512,1024]{1,0:T(8,128)(2,1)}, bf16[512,1024]{1,0:T(8,128)(2,1)S(1)}, u32[]{:S(2)}, u32[]{:S(2)}) collective-permute-start(bf16[512,1024]{1,0:T(8,128)(2,1)} %get-tuple-element.59.refs_0_), channel_id=1, source_target_pairs={{0,8},{4,12},{24,16},{28,20},{1,9},{5,13},{25,17},{29,21},{2,10},{... | collective-permute-start | bytes 3145736 | tf_op jit(solution)/shard_map/ppermute | solution.py:245
  38.6 21.3 %collective-permute-done.4.refs_0_ = bf16[512,1024]{1,0:T(8,128)(2,1)S(1)} collective-permute-done((bf16[512,1024]{1,0:T(8,128)(2,1)}, bf16[512,1024]{1,0:T(8,128)(2,1)S(1)}, u32[]{:S(2)}, u32[]{:S(2)}) %collective-permute-start.4) | collective-permute-done | bytes 1048608 | tf_op jit(solution)/shard_map/ppermute | solution.py:245
  59.9 2.8 %collective-permute-done.9.refs_6_.refs_5_ = bf16[512,1024]{1,0:T(8,128)(2,1)S(1)} collective-permute-done((bf16[512,1024]{1,0:T(8,128)(2,1)}, bf16[512,1024]{1,0:T(8,128)(2,1)S(1)}, u32[]{:S(2)}, u32[]{:S(2)}) %collective-permute-start.9) | collective-permute-done | bytes 1048608 | tf_op jit(solution)/shard_map/ppermute | solution.py:245
  66.0 4.2 %collective-permute-start.13 = (bf16[512,1024]{1,0:T(8,128)(2,1)}, bf16[512,1024]{1,0:T(8,128)(2,1)}, u32[]{:S(2)}, u32[]{:S(2)}) collective-permute-start(bf16[512,1024]{1,0:T(8,128)(2,1)} %get-tuple-element.69), channel_id=1, source_target_pairs={{0,8},{4,12},{24,16},{28,20},{1,9},{5,13},{25,17},{29,21},{2,10},{... | collective-permute-start | bytes 3145736 | tf_op jit(solution)/shard_map/ppermute | solution.py:245
  76.6 5.8 %norm_rows.2 = (bf16[768,4096]{1,0:T(8,128)(2,1)}, f32[8,128]{1,0:T(8,128)}) custom-call(s32[15]{0:T(128)} %stack.61.place, f32[4,1024]{1,0:T(4,128)} %reshape.49.gain, bf16[384,1024]{1,0:T(8,128)(2,1)} %p0.1, bf16[384,1024]{1,0:T(8,128)(2,1)} %collective-permute-done.2.p1, bf16[384,1024]{1,0:T(8,128)(2,1)} %collective-permute-done.1.p2, ...), custom_call_target="tpu_custom_call" | custom-call | flops 6291456 | bytes 6291456 | tf_op jit(solution)/shard_map/norm_rows/pallas_call | solution.py:348
  84.9 5.8 %norm_rows.3 = (bf16[768,4096]{1,0:T(8,128)(2,1)}, f32[8,128]{1,0:T(8,128)}) custom-call(s32[15]{0:T(128)} %stack.61.place, f32[4,1024]{1,0:T(4,128)} %reshape.49.gain, bf16[384,1024]{1,0:T(8,128)(2,1)} %copy-done.24, bf16[576,1024]{1,0:T(8,128)(2,1)} %get-tuple-element.65.p4.p1, ...), custom_call_target="tpu_custom_call", output_to_operand_aliasing={{0}: (7, {})} | custom-call | flops 6291456 | bytes 6291456 | tf_op jit(solution)/shard_map/norm_rows/pallas_call | solution.py:348
  94.4 6.5 %collective-permute-start.20 = (bf16[4,1024,128]{2,1,0:T(8,128)(2,1)}, bf16[4,1024,128]{2,1,0:T(8,128)(2,1)S(1)}, u32[]{:S(2)}, u32[]{:S(2)}) collective-permute-start(bf16[4,1024,128]{2,1,0:T(8,128)(2,1)} %get-tuple-element.78.refs_1_), channel_id=1, source_target_pairs={{0,8},{4,12},{8,0},{12,4},{16,24},{20,28},{24,16},{28,20},{1,9},{5... | collective-permute-start | bytes 3145736 | tf_op jit(solution)/shard_map/ppermute | solution.py:245
  102.6 7.1 %rank_terms.1 = (bf16[48,768]{1,0:T(8,128)(2,1)}, bf16[4,32,1024]{2,1,0:T(8,128)(2,1)}, bf16[4,32,1024]{2,1,0:T(8,128)(2,1)}, bf16[256,1024]{1,0:T(8,128)(2,1)}, bf16[256,512]{1,0:T(8,128)(2,1)}) custom-call(s32[15]{0:T(128)} %stack.61.place, s32[8]{0:T(128)} %pad_add_fusion.table.own_table, s32[8]{0:T(128)} %bitcast_convert_fusion.2.end_table, s32[16]{0:T(128)} %storage.5, ...), custom_call_target="tpu_custom_call" | custom-call | flops 1207959552 | bytes 6815744 | tf_op jit(solution)/shard_map/rank_terms/pallas_call | solution.py:461
  117.2 7.4 %project_key_value.1 = (bf16[384,512]{1,0:T(8,128)(2,1)}, bf16[384,512]{1,0:T(8,128)(2,1)}) custom-call(s32[15]{0:T(128)} %stack.61.place, s32[8]{0:T(128)} %pad_add_fusion.table.own_table, s32[8]{0:T(128)} %bitcast_convert_fusion.2.end_table, s32[16]{0:T(128)} %storage.5, bf16[768,4096]{1,0:T(8,128)(2,1)} %get-tuple-element.68.x, ...), custom_call_target="tpu_custom_call" | custom-call | flops 3422552064 | bytes 11272192 | tf_op jit(solution)/shard_map/project_key_value/pallas_call | solution.py:551
  131.9 12.0 %project_query.1 = (bf16[384,1024]{1,0:T(8,128)(2,1)}, bf16[384,1024]{1,0:T(8,128)(2,1)}) custom-call(s32[15]{0:T(128)} %stack.61.place, s32[8]{0:T(128)} %pad_add_fusion.table.own_table, s32[8]{0:T(128)} %bitcast_convert_fusion.2.end_table, s32[16]{0:T(128)} %storage.5, bf16[768,4096]{1,0:T(8,128)(2,1)} %get-tuple-element.68.x, bf16[512,1024]{1,0:T(8,128)(2,1)} %refs_0_.1, ...), custom_call_target="tpu_custom_call" | custom-call | flops 6845104128 | bytes 16252928 | tf_op jit(solution)/shard_map/project_query/pallas_call | solution.py:551
  148.1 19.5 %collective-permute-done.28.refs_1_ = bf16[384,1024]{1,0:T(8,128)(2,1)} collective-permute-done((bf16[384,1024]{1,0:T(8,128)(2,1)}, bf16[384,1024]{1,0:T(8,128)(2,1)}, u32[]{:S(2)}, u32[]{:S(2)}) %collective-permute-start.28) | collective-permute-done | bytes 786464 | tf_op jit(solution)/shard_map/ppermute | solution.py:245
  170.2 11.8 %attend.1 = (bf16[384,1024]{1,0:T(8,128)(2,1)}, bf16[384,512]{1,0:T(8,128)(2,1)}, f32[16,384]{1,0:T(8,128)}) custom-call(s32[15]{0:T(128)} %stack.61.place, s32[8]{0:T(128)} %pad_add_fusion.table.own_table, s32[4]{0:T(128)} %bitcast.50, s32[32]{0:T(128)} %reshape_squeeze.3.pages, bf16[384,1024]{1,0:T(8,128)(2,1)} %get-tuple-element.88.own, ...), custom_call_target="tpu_custom_call" | custom-call | flops 1409286144 | bytes 2359296 | tf_op jit(solution)/shard_map/attend/pallas_call | solution.py:650
  182.9 5.5 %project_columns.3 = (bf16[400,512]{1,0:T(8,128)(2,1)}, bf16[400,512]{1,0:T(8,128)(2,1)}, bf16[400,512]{1,0:T(8,128)(2,1)}, bf16[400,512]{1,0:T(8,128)(2,1)}) custom-call(s32[15]{0:T(128)} %stack.61.place, bf16[384,1024]{1,0:T(8,128)(2,1)} %get-tuple-element.99.attended, bf16[4,1024,128]{2,1,0:T(8,128)(2,1)} %get-tuple-element.89.refs_0_.refs_2_, ...), custom_call_target="tpu_custom_call" | custom-call | flops 1677721600 | bytes 6651904 | tf_op jit(solution)/shard_map/project_columns/pallas_call | solution.py:725
  188.4 5.3 %collective-permute-done.35.refs_0_ = bf16[4,1024,128]{2,1,0:T(8,128)(2,1)S(1)} collective-permute-done((bf16[4,1024,128]{2,1,0:T(8,128)(2,1)}, bf16[4,1024,128]{2,1,0:T(8,128)(2,1)S(1)}, u32[]{:S(2)}, u32[]{:S(2)}) %collective-permute-start.35) | collective-permute-done | bytes 1048608 | tf_op jit(solution)/shard_map/ppermute | solution.py:245
  201.8 5.0 %project_columns.4 = (bf16[384,256]{1,0:T(8,128)(2,1)}, bf16[384,256]{1,0:T(8,128)(2,1)}, bf16[384,256]{1,0:T(8,128)(2,1)}, bf16[384,256]{1,0:T(8,128)(2,1)}) custom-call(s32[15]{0:T(128)} %stack.61.place, bf16[384,1024]{1,0:T(8,128)(2,1)} %get-tuple-element.99.attended, bf16[4,1024,128]{2,1,0:T(8,128)(2,1)} %gate.16.refs_0_, ...), custom_call_target="tpu_custom_call" | custom-call | flops 805306368 | bytes 3670016 | tf_op jit(solution)/shard_map/project_columns/pallas_call | solution.py:725
  206.8 3.1 %collective-permute-done.32.refs_2_.refs_1_ = bf16[400,512]{1,0:T(8,128)(2,1)S(1)} collective-permute-done((bf16[400,512]{1,0:T(8,128)(2,1)}, bf16[400,512]{1,0:T(8,128)(2,1)S(1)}, u32[]{:S(2)}, u32[]{:S(2)}) %collective-permute-start.32) | collective-permute-done | bytes 409632 | tf_op jit(solution)/shard_map/ppermute | solution.py:254
  209.9 7.9 %collective-permute-done.33.refs_3_.refs_2_ = bf16[400,512]{1,0:T(8,128)(2,1)S(1)} collective-permute-done((bf16[400,512]{1,0:T(8,128)(2,1)}, bf16[400,512]{1,0:T(8,128)(2,1)S(1)}, u32[]{:S(2)}, u32[]{:S(2)}) %collective-permute-start.33) | collective-permute-done | bytes 409632 | tf_op jit(solution)/shard_map/ppermute | solution.py:254
  217.8 4.3 %collective-permute-done.41.refs_0_ = bf16[4,1024,128]{2,1,0:T(8,128)(2,1)S(1)} collective-permute-done((bf16[4,1024,128]{2,1,0:T(8,128)(2,1)S(1)}, bf16[4,1024,128]{2,1,0:T(8,128)(2,1)S(1)}, u32[]{:S(2)}, u32[]{:S(2)}) %collective-permute-start.41) | collective-permute-done | bytes 1048608 | tf_op jit(solution)/shard_map/ppermute | solution.py:245
  227.5 4.2 %project_columns.5 = (bf16[384,256]{1,0:T(8,128)(2,1)S(1)}, bf16[384,256]{1,0:T(8,128)(2,1)S(1)}, bf16[384,256]{1,0:T(8,128)(2,1)S(1)}, bf16[384,256]{1,0:T(8,128)(2,1)S(1)}) custom-call(s32[15]{0:T(128)S(1)} %copy-done.11, bf16[384,1024]{1,0:T(8,128)(2,1)S(1)} %copy-done.2, bf16[4,1024,128]{2,1,0:T(8,128)(2,1)S(1)} %gate.17.refs_0_, ...), custom_call_target="tpu_custom_call" | custom-call | flops 805306368 | bytes 3670016 | tf_op jit(solution)/shard_map/project_columns/pallas_call | solution.py:725
  236.7 3.5 %collective-permute-done.44.refs_9_ = bf16[384,256]{1,0:T(8,128)(2,1)S(1)} collective-permute-done((bf16[384,256]{1,0:T(8,128)(2,1)S(1)}, bf16[384,256]{1,0:T(8,128)(2,1)S(1)}, u32[]{:S(2)}, u32[]{:S(2)}) %collective-permute-start.44) | collective-permute-done | bytes 196640 | tf_op jit(solution)/shard_map/ppermute | solution.py:254
  240.2 4.0 %collective-permute-done.45.refs_10_ = bf16[384,256]{1,0:T(8,128)(2,1)S(1)} collective-permute-done((bf16[384,256]{1,0:T(8,128)(2,1)S(1)}, bf16[384,256]{1,0:T(8,128)(2,1)S(1)}, u32[]{:S(2)}, u32[]{:S(2)}) %collective-permute-start.45) | collective-permute-done | bytes 196640 | tf_op jit(solution)/shard_map/ppermute | solution.py:254
  245.0 3.8 %sum_columns.1 = bf16[384,1024]{1,0:T(8,128)(2,1)} custom-call(s32[15]{0:T(128)} %stack.61.place, s32[8]{0:T(128)} %pad_add_fusion.table.own_table, bf16[4,32,1024]{2,1,0:T(8,128)(2,1)} %get-tuple-element.76.chosen_own, bf16[4,32,1024]{2,1,0:T(8,128)(2,1)} %get-tuple-element.87.chosen_back, bf16[400,512]{1,0:T(8,128)(2,1)} %get-tuple-element.101.refs_1_.refs_0_, ...), custom_call_target="tpu_custom_call" | custom-call | flops 56623104 | bytes 4718592 | tf_op jit(solution)/shard_map/sum_columns/pallas_call | solution.py:780
  (219 shorter events, 84.2 us)
Async XLA Ops:
  0.6 25.8 %collective-permute-start.1 = (bf16[384,1024]{1,0:T(8,128)(2,1)}, bf16[384,1024]{1,0:T(8,128)(2,1)}, u32[]{:S(2)}, u32[]{:S(2)}) collective-permute-start(bf16[384,1024]{1,0:T(8,128)(2,1)} %p0.1), channel_id=1, source_target_pairs={{0,2},{1,3},{2,0},{3,1},{4,6},{5,7},{6,4},{7,5},{8,10},{9,11},{10,... | collective-permute-start | bytes 2359304 | tf_op jit(solution)/shard_map/ppermute | solution.py:249
  3.7 23.8 %collective-permute-start.2 = (bf16[384,1024]{1,0:T(8,128)(2,1)}, bf16[384,1024]{1,0:T(8,128)(2,1)}, u32[]{:S(2)}, u32[]{:S(2)}) collective-permute-start(bf16[384,1024]{1,0:T(8,128)(2,1)} %p0.1), channel_id=1, source_target_pairs={{0,1},{1,0},{2,3},{3,2},{4,5},{5,4},{6,7},{7,6},{8,9},{9,8},{10,11... | collective-permute-start | bytes 2359304 | tf_op jit(solution)/shard_map/ppermute | solution.py:249
  5.2 23.4 %collective-permute-start = (bf16[384,1024]{1,0:T(8,128)(2,1)}, bf16[384,1024]{1,0:T(8,128)(2,1)S(1)}, u32[]{:S(2)}, u32[]{:S(2)}) collective-permute-start(bf16[384,1024]{1,0:T(8,128)(2,1)} %p0.1), channel_id=1, source_target_pairs={{0,8},{4,12},{24,16},{28,20},{1,9},{5,13},{25,17},{29,21},{2,10},{... | collective-permute-start | bytes 2359304 | tf_op jit(solution)/shard_map/ppermute | solution.py:245
  8.7 21.6 %collective-permute-start.3 = (bf16[512,1024]{1,0:T(8,128)(2,1)}, bf16[512,1024]{1,0:T(8,128)(2,1)}, u32[]{:S(2)}, u32[]{:S(2)}) collective-permute-start(bf16[512,1024]{1,0:T(8,128)(2,1)} %refs_0_.1), channel_id=1, source_target_pairs={{8,16},{12,20},{16,8},{20,12},{9,17},{13,21},{17,9},{21,13},{10,18... | collective-permute-start | bytes 3145736 | tf_op jit(solution)/shard_map/ppermute | solution.py:245
  30.3 29.6 %collective-permute-start.4 = (bf16[512,1024]{1,0:T(8,128)(2,1)}, bf16[512,1024]{1,0:T(8,128)(2,1)S(1)}, u32[]{:S(2)}, u32[]{:S(2)}) collective-permute-start(bf16[512,1024]{1,0:T(8,128)(2,1)} %get-tuple-element.59.refs_0_), channel_id=1, source_target_pairs={{0,8},{4,12},{24,16},{28,20},{1,9},{5,13},{25,17},{29,21},{2,10},{... | collective-permute-start | bytes 3145736 | tf_op jit(solution)/shard_map/ppermute | solution.py:245
  36.6 28.4 %collective-permute-start.6 = (bf16[576,1024]{1,0:T(8,128)(2,1)}, bf16[576,1024]{1,0:T(8,128)(2,1)S(1)}, u32[]{:S(2)}, u32[]{:S(2)}) collective-permute-start(bf16[576,1024]{1,0:T(8,128)(2,1)} %get-tuple-element.60), channel_id=1, source_target_pairs={{0,1},{1,0},{2,3},{3,2},{4,5},{5,4},{6,7},{7,6},{8,9},{9,8},{10,11... | collective-permute-start | bytes 3538952 | tf_op jit(solution)/shard_map/ppermute | solution.py:249
  37.2 28.1 %collective-permute-start.7 = (bf16[576,1024]{1,0:T(8,128)(2,1)}, bf16[576,1024]{1,0:T(8,128)(2,1)}, u32[]{:S(2)}, u32[]{:S(2)}) collective-permute-start(bf16[576,1024]{1,0:T(8,128)(2,1)} %get-tuple-element.61), channel_id=1, source_target_pairs={{0,2},{1,3},{2,0},{3,1},{4,6},{5,7},{6,4},{7,5},{8,10},{9,11},{10,... | collective-permute-start | bytes 3538952 | tf_op jit(solution)/shard_map/ppermute | solution.py:249
  37.8 22.1 %collective-permute-start.5 = (bf16[512,1024]{1,0:T(8,128)(2,1)}, bf16[512,1024]{1,0:T(8,128)(2,1)S(1)}, u32[]{:S(2)}, u32[]{:S(2)}) collective-permute-start(bf16[512,1024]{1,0:T(8,128)(2,1)} %get-tuple-element.59.refs_0_), channel_id=1, source_target_pairs={{8,16},{12,20},{16,8},{20,12},{9,17},{13,21},{17,9},{21,13},{10,18... | collective-permute-start | bytes 3145736 | tf_op jit(solution)/shard_map/ppermute | solution.py:245
  38.5 21.4 %collective-permute-start.8 = (bf16[512,1024]{1,0:T(8,128)(2,1)}, bf16[512,1024]{1,0:T(8,128)(2,1)S(1)}, u32[]{:S(2)}, u32[]{:S(2)}) collective-permute-start(bf16[512,1024]{1,0:T(8,128)(2,1)} %get-tuple-element.62.refs_4_), channel_id=1, source_target_pairs={{0,4},{4,0},{8,12},{12,8},{16,20},{20,16},{24,28},{28,24},{1,5},{5... | collective-permute-start | bytes 3145736 | tf_op jit(solution)/shard_map/ppermute | solution.py:245
  66.0 26.2 %collective-permute-start.13 = (bf16[512,1024]{1,0:T(8,128)(2,1)}, bf16[512,1024]{1,0:T(8,128)(2,1)}, u32[]{:S(2)}, u32[]{:S(2)}) collective-permute-start(bf16[512,1024]{1,0:T(8,128)(2,1)} %get-tuple-element.69), channel_id=1, source_target_pairs={{0,8},{4,12},{24,16},{28,20},{1,9},{5,13},{25,17},{29,21},{2,10},{... | collective-permute-start | bytes 3145736 | tf_op jit(solution)/shard_map/ppermute | solution.py:245
  70.1 22.1 %collective-permute-start.14 = (bf16[512,1024]{1,0:T(8,128)(2,1)}, bf16[512,1024]{1,0:T(8,128)(2,1)S(1)}, u32[]{:S(2)}, u32[]{:S(2)}) collective-permute-start(bf16[512,1024]{1,0:T(8,128)(2,1)} %get-tuple-element.64.refs_1_), channel_id=1, source_target_pairs={{8,16},{12,20},{16,8},{20,12},{9,17},{13,21},{17,9},{21,13},{10,18... | collective-permute-start | bytes 3145736 | tf_op jit(solution)/shard_map/ppermute | solution.py:245
  93.7 30.8 %collective-permute-start.19 = (bf16[512,1024]{1,0:T(8,128)(2,1)}, bf16[512,1024]{1,0:T(8,128)(2,1)S(1)}, u32[]{:S(2)}, u32[]{:S(2)}) collective-permute-start(bf16[512,1024]{1,0:T(8,128)(2,1)} %get-tuple-element.77.refs_2_), channel_id=1, source_target_pairs={{8,16},{12,20},{16,8},{20,12},{9,17},{13,21},{17,9},{21,13},{10,18... | collective-permute-start | bytes 3145736 | tf_op jit(solution)/shard_map/ppermute | solution.py:245
  94.4 30.3 %collective-permute-start.20 = (bf16[4,1024,128]{2,1,0:T(8,128)(2,1)}, bf16[4,1024,128]{2,1,0:T(8,128)(2,1)S(1)}, u32[]{:S(2)}, u32[]{:S(2)}) collective-permute-start(bf16[4,1024,128]{2,1,0:T(8,128)(2,1)} %get-tuple-element.78.refs_1_), channel_id=1, source_target_pairs={{0,8},{4,12},{8,0},{12,4},{16,24},{20,28},{24,16},{28,20},{1,9},{5... | collective-permute-start | bytes 3145736 | tf_op jit(solution)/shard_map/ppermute | solution.py:245
  125.8 18.0 %collective-permute-start.26 = (bf16[4,32,1024]{2,1,0:T(8,128)(2,1)}, bf16[4,32,1024]{2,1,0:T(8,128)(2,1)S(1)}, u32[]{:S(2)}, u32[]{:S(2)}) collective-permute-start(bf16[4,32,1024]{2,1,0:T(8,128)(2,1)} %get-tuple-element.86), channel_id=1, source_target_pairs={{8,0},{12,4},{16,24},{20,28},{9,1},{13,5},{17,25},{21,29},{10,2},{... | collective-permute-start | bytes 786440 | tf_op jit(solution)/shard_map/ppermute | solution.py:245
  127.1 20.9 %collective-permute-start.27 = (bf16[4,1024,128]{2,1,0:T(8,128)(2,1)}, bf16[4,1024,128]{2,1,0:T(8,128)(2,1)}, u32[]{:S(2)}, u32[]{:S(2)}) collective-permute-start(bf16[4,1024,128]{2,1,0:T(8,128)(2,1)} %get-tuple-element.89.refs_0_.refs_2_), channel_id=1, source_target_pairs={{8,16},{12,20},{16,8},{20,12},{9,17},{13,21},{17,9},{21,13},{10,18... | collective-permute-start | bytes 3145736 | tf_op jit(solution)/shard_map/ppermute | solution.py:245
  129.0 19.0 %collective-permute-start.29 = (bf16[4,1024,128]{2,1,0:T(8,128)(2,1)}, bf16[4,1024,128]{2,1,0:T(8,128)(2,1)S(1)}, u32[]{:S(2)}, u32[]{:S(2)}) collective-permute-start(bf16[4,1024,128]{2,1,0:T(8,128)(2,1)} %get-tuple-element.89.refs_0_.refs_2_), channel_id=1, source_target_pairs={{0,4},{4,0},{8,12},{12,8},{16,20},{20,16},{24,28},{28,24},{1,5},{5... | collective-permute-start | bytes 3145736 | tf_op jit(solution)/shard_map/ppermute | solution.py:245
  145.9 21.7 %collective-permute-start.28 = (bf16[384,1024]{1,0:T(8,128)(2,1)}, bf16[384,1024]{1,0:T(8,128)(2,1)}, u32[]{:S(2)}, u32[]{:S(2)}) collective-permute-start(bf16[384,1024]{1,0:T(8,128)(2,1)} %get-tuple-element.90), channel_id=1, source_target_pairs={{8,0},{12,4},{16,24},{20,28},{9,1},{13,5},{17,25},{21,29},{10,2},{... | collective-permute-start | bytes 2359304 | tf_op jit(solution)/shard_map/ppermute | solution.py:245
  147.3 34.7 %collective-permute-start.31 = (bf16[4,1024,128]{2,1,0:T(8,128)(2,1)S(1)}, bf16[4,1024,128]{2,1,0:T(8,128)(2,1)S(1)}, u32[]{:S(2)}, u32[]{:S(2)}) collective-permute-start(bf16[4,1024,128]{2,1,0:T(8,128)(2,1)S(1)} %copy-done.18), channel_id=1, source_target_pairs={{8,16},{12,20},{16,8},{20,12},{9,17},{13,21},{17,9},{21,13},{10,18... | collective-permute-start | bytes 3145736 | tf_op jit(solution)/shard_map/ppermute | solution.py:245
  167.5 26.2 %collective-permute-start.35 = (bf16[4,1024,128]{2,1,0:T(8,128)(2,1)}, bf16[4,1024,128]{2,1,0:T(8,128)(2,1)S(1)}, u32[]{:S(2)}, u32[]{:S(2)}) collective-permute-start(bf16[4,1024,128]{2,1,0:T(8,128)(2,1)} %get-tuple-element.105.refs_2_), channel_id=1, source_target_pairs={{8,0},{12,4},{16,24},{20,28},{9,1},{13,5},{17,25},{21,29},{10,2},{... | collective-permute-start | bytes 3145736 | tf_op jit(solution)/shard_map/ppermute | solution.py:245
  168.8 31.2 %collective-permute-start.37 = (bf16[4,1024,128]{2,1,0:T(8,128)(2,1)}, bf16[4,1024,128]{2,1,0:T(8,128)(2,1)}, u32[]{:S(2)}, u32[]{:S(2)}) collective-permute-start(bf16[4,1024,128]{2,1,0:T(8,128)(2,1)} %get-tuple-element.105.refs_2_), channel_id=1, source_target_pairs={{0,4},{4,0},{8,12},{12,8},{16,20},{20,16},{24,28},{28,24},{1,5},{5... | collective-permute-start | bytes 3145736 | tf_op jit(solution)/shard_map/ppermute | solution.py:245
  195.9 26.2 %collective-permute-start.41 = (bf16[4,1024,128]{2,1,0:T(8,128)(2,1)S(1)}, bf16[4,1024,128]{2,1,0:T(8,128)(2,1)S(1)}, u32[]{:S(2)}, u32[]{:S(2)}) collective-permute-start(bf16[4,1024,128]{2,1,0:T(8,128)(2,1)S(1)} %copy-done.4), channel_id=1, source_target_pairs={{8,0},{12,4},{16,24},{20,28},{9,1},{13,5},{17,25},{21,29},{10,2},{... | collective-permute-start | bytes 3145736 | tf_op jit(solution)/shard_map/ppermute | solution.py:245
  198.4 19.4 %collective-permute-start.33 = (bf16[400,512]{1,0:T(8,128)(2,1)}, bf16[400,512]{1,0:T(8,128)(2,1)S(1)}, u32[]{:S(2)}, u32[]{:S(2)}) collective-permute-start(bf16[400,512]{1,0:T(8,128)(2,1)} %get-tuple-element.103), channel_id=1, source_target_pairs={{0,2},{1,3},{2,0},{3,1},{4,6},{5,7},{6,4},{7,5},{8,10},{9,11},{10,... | collective-permute-start | bytes 1228808 | tf_op jit(solution)/shard_map/ppermute | solution.py:254
  200.1 17.8 %collective-permute-start.34 = (bf16[400,512]{1,0:T(8,128)(2,1)S(1)}, bf16[400,512]{1,0:T(8,128)(2,1)S(1)}, u32[]{:S(2)}, u32[]{:S(2)}) collective-permute-start(bf16[400,512]{1,0:T(8,128)(2,1)S(1)} %copy-done.48), channel_id=1, source_target_pairs={{0,3},{1,2},{2,1},{3,0},{4,7},{5,6},{6,5},{7,4},{8,11},{9,10},{10,... | collective-permute-start | bytes 1228808 | tf_op jit(solution)/shard_map/ppermute | solution.py:254
  200.8 26.7 %collective-permute-start.43 = (bf16[4,1024,128]{2,1,0:T(8,128)(2,1)S(1)}, bf16[4,1024,128]{2,1,0:T(8,128)(2,1)S(1)}, u32[]{:S(2)}, u32[]{:S(2)}) collective-permute-start(bf16[4,1024,128]{2,1,0:T(8,128)(2,1)S(1)} %copy-done.4), channel_id=1, source_target_pairs={{0,4},{4,0},{8,12},{12,8},{16,20},{20,16},{24,28},{28,24},{1,5},{5... | collective-permute-start | bytes 3145736 | tf_op jit(solution)/shard_map/ppermute | solution.py:245
  (73 other events, 493.8 us)

commit v3 on v2

--- a/solution.py
+++ b/solution.py
@@ -223,6 +223,7 @@
 PLANES = 4
 BLOCKS = 4
 GROUPS = 2
+HIDDEN = -1e30
 WIDE = 256
 
 
@@ -493,7 +494,7 @@
 
 def project_kernel(is_q, place, own_table, end_table, storage, x, *refs):
     sources, lows, up = refs[:8], refs[8:12], refs[12]
-    own, end, spread, held, x_held, sems = refs[13:]
+    own, end, spread, held, x_held, sems = refs[-6:]
     rows, width = own.shape[0], x.shape[1] // BLOCKS
     depth = held.shape[0] // 8
 
@@ -541,18 +542,30 @@
         total = low + term if total is None else total + term
     total = total.astype(jnp.bfloat16)
     own[...] = total[:rows]
-    end[...] = total[rows:]
-
-
-def project(place, own_table, end_table, storage, x, sources, lows, up, is_q):
+    end[:rows] = total[rows:]
+    if not is_q:
+        chosen_end = refs[13]
+        count, each, _ = chosen_end.shape
+        for h in range(width // columns):
+            for j in range(count):
+                first = rows + (count * h + j) * each
+                end[first : first + each] = chosen_end[j, :, h * columns : (h + 1) * columns]
+
+
+def project(place, own_table, end_table, storage, x, sources, lows, up, is_q, chosen_end=None):
     rows, width = x.shape[0], x.shape[1] // BLOCKS
     columns = up.shape[1]
+    more = [] if is_q else [chosen_end]
+    extra = 0 if is_q else chosen_end.size // columns
     anywhere = pl.BlockSpec(memory_space=pl.ANY)
     return pl.pallas_call(
         functools.partial(project_kernel, is_q),
-        in_specs=[in_smem()] * 4 + [anywhere] * 9 + [in_vmem()] * 5,
+        in_specs=[in_smem()] * 4 + [anywhere] * 9 + [in_vmem()] * (5 + len(more)),
         out_specs=[in_vmem()] * 2,
-        out_shape=[jax.ShapeDtypeStruct((rows // GROUPS, columns), jnp.bfloat16)] * 2,
+        out_shape=[
+            jax.ShapeDtypeStruct((rows // GROUPS, columns), jnp.bfloat16),
+            jax.ShapeDtypeStruct((rows // GROUPS + extra, columns), jnp.bfloat16),
+        ],
         scratch_shapes=[
             pltpu.VMEM((rows, 16 * ADAPTER_RANK), jnp.bfloat16),
             pltpu.VMEM(((8 if is_q else 4) * sources[0].shape[0], width), jnp.bfloat16),
@@ -565,12 +578,32 @@
             2 * BLOCKS * width * (rows + columns) + 2 * rows * columns,
         ),
         name="project_query" if is_q else "project_key_value",
-    )(place, own_table, end_table, storage, x, *sources, *lows, up)
+    )(place, own_table, end_table, storage, x, *sources, *lows, up, *more)
+
+
+def take_adapters(out, at_end, chosen_own, kv_back, rows, first):
+    rank = ADAPTER_RANK
+    count, each, width = chosen_own.shape
+    columns = kv_back.shape[1]
+
+    @pl.when(jnp.logical_not(at_end))
+    def _():
+        for j in range(count):
+            out[rank * j : rank * (j + 1), :] = chosen_own[j, first : first + rank, :]
+
+    @pl.when(at_end)
+    def _():
+        for h in range(width // columns):
+            for j in range(count):
+                start = rows + (count * h + j) * each + first
+                out[rank * j : rank * (j + 1), h * columns : (h + 1) * columns] = kv_back[
+                    start : start + rank, :
+                ]
 
 
 def attention_kernel(
     place, table, prefix, pages, own, back, kv_own, kv_back, k_pool, v_pool, q_gain, k_gain,
-    cosine, sine, chosen_own, chosen_back, out, cache, low, raw, raw_kv, keys, values, allowed, down,
+    cosine, sine, chosen_own, out, cache, low, raw, raw_kv, keys, values, allowed, down,
 ):
     rows, pool_rows = own.shape[0], k_pool.shape[0]
     page_count = pool_rows // PAGE
@@ -578,14 +611,14 @@
     @pl.when(place[6] == 1)
     def _():
         raw[...] = back[...]
-        raw_kv[...] = kv_back[...]
-        down[...] = chosen_back[:, :ADAPTER_RANK, :].reshape(down.shape)
+        raw_kv[...] = kv_back[:rows]
 
     @pl.when(place[6] == 0)
     def _():
         raw[...] = own[...]
         raw_kv[...] = kv_own[...]
-        down[...] = chosen_own[:, :ADAPTER_RANK, :].reshape(down.shape)
+
+    take_adapters(down, place[6] == 1, chosen_own, kv_back, rows, 0)
 
     owner = request_of_rows(table, (rows, 1), 0)
     page = lax.broadcasted_iota(jnp.int32, (1, pool_rows), 1) // PAGE
@@ -595,11 +628,11 @@
         for i in range(page_count):
             mine = jnp.where((page == pages[8 * j + i]) & (i < prefix[j]), 1, mine)
         seen = jnp.where(owner == j, mine, seen)
-    allowed[:, :pool_rows] = seen
+    allowed[:, :pool_rows] = jnp.where(seen > 0, 0.0, HIDDEN)
     row = lax.broadcasted_iota(jnp.int32, (rows, rows), 0)
     column = lax.broadcasted_iota(jnp.int32, (rows, rows), 1)
     same = owner == request_of_rows(table, (1, rows), 1)
-    allowed[:, pool_rows:] = (same & (column <= row)).astype(jnp.int32)
+    allowed[:, pool_rows:] = jnp.where(same & (column <= row), 0.0, HIDDEN)
 
     def turned(value, gain):
         value = value.astype(jnp.float32)
@@ -626,9 +659,9 @@
             query = turned(raw[:, place_q], q_gain)
             scores = lax.dot_general(
                 query, keys[...], (((1,), (1,)), ((), ())), preferred_element_type=jnp.float32
-            ) * (1.0 / math.sqrt(HEAD_SIZE))
-            grown = jnp.where(allowed[...] > 0, jnp.exp(scores), 0.0)
-            weights = (grown / jnp.sum(grown, axis=1, keepdims=True)).astype(jnp.bfloat16)
+            )
+            grown = jnp.exp(scores * (1.0 / math.sqrt(HEAD_SIZE)) + allowed[...])
+            weights = (grown * (1.0 / jnp.sum(grown, axis=1, keepdims=True))).astype(jnp.bfloat16)
             out[:, place_q] = jnp.dot(
                 weights, values[...], preferred_element_type=jnp.float32
             ).astype(jnp.bfloat16)
@@ -643,13 +676,13 @@
 
 
 def attend(place, table, prefix, pages, own, back, kv_own, kv_back, k_pool, v_pool, q_gain, k_gain,
-           cosine, sine, chosen_own, chosen_back):
+           cosine, sine, chosen_own):
     rows, q_width = own.shape
     kv_width = k_pool.shape[1]
     keys = k_pool.shape[0] + rows
     return pl.pallas_call(
         attention_kernel,
-        in_specs=[in_smem()] * 4 + [in_vmem()] * 12,
+        in_specs=[in_smem()] * 4 + [in_vmem()] * 11,
         out_specs=[in_vmem()] * 3,
         out_shape=[
             jax.ShapeDtypeStruct((rows, q_width), jnp.bfloat16),
@@ -661,14 +694,14 @@
             pltpu.VMEM(kv_own.shape, jnp.bfloat16),
             pltpu.VMEM((keys, HEAD_SIZE), jnp.bfloat16),
             pltpu.VMEM((keys, HEAD_SIZE), jnp.bfloat16),
-            pltpu.VMEM((rows, keys), jnp.int32),
+            pltpu.VMEM((rows, keys), jnp.float32),
             pltpu.VMEM((4 * ADAPTER_RANK, chosen_own.shape[2]), jnp.bfloat16),
         ],
         compiler_params=kernel_params(56),
         cost_estimate=cost(4 * rows * keys * q_width, 6 * rows * q_width, rows * keys * (q_width // HEAD_SIZE)),
         name="attend",
     )(place, table, prefix, pages, own, back, kv_own, kv_back, k_pool, v_pool, q_gain, k_gain,
-      cosine, sine, chosen_own, chosen_back)
+      cosine, sine, chosen_own)
 
 
 def columns_kernel(count, place, attended, *refs):
@@ -745,18 +778,10 @@
     )(place, attended, *[w for chunk in chunks for w in chunk], *more)
 
 
-def sum_kernel(place, table, chosen_own, chosen_back, *refs):
-    parts, (out, up) = refs[:12], refs[12:]
+def sum_kernel(place, table, chosen_own, kv_back, *refs):
+    parts, (out, last, up) = refs[:8], refs[8:]
     rank, rows = ADAPTER_RANK, out.shape[0]
-
-    @pl.when(place[6] == 1)
-    def _():
-        up[...] = chosen_back[:, rank:, :].reshape(up.shape)
-
-    @pl.when(place[6] == 0)
-    def _():
-        up[...] = chosen_own[:, rank:, :].reshape(up.shape)
-
+    take_adapters(up, place[6] == 1, chosen_own, kv_back, rows, rank)
     low = sum(v[rows:, :rows].astype(jnp.float32) for v in parts[:4])
     low = low.astype(jnp.bfloat16).astype(jnp.float32)
     owner = request_of_rows(table, (1, rows), 1)
@@ -764,29 +789,62 @@
     spread = wide.T.astype(jnp.bfloat16)
     core = place[0]
     for i in range(PLANES):
-        first, at = (0, i * WIDE) if i < 2 else (4 * (i - 1), 0)
-        total = sum(v[:rows, at : at + WIDE].astype(jnp.float32) for v in parts[first : first + 4])
-        for c, mine in ((core, total[:, :HEAD_SIZE]), (1 - core, total[:, HEAD_SIZE:])):
+        for h, c in enumerate((core, 1 - core)):
             begin = pl.multiple_of((2 * place[7 + i] + c) * HEAD_SIZE, HEAD_SIZE)
-            columns = pl.ds(begin, HEAD_SIZE)
-            out[:, columns] = (
-                mine + jnp.dot(spread, up[:, columns], preferred_element_type=jnp.float32)
-            ).astype(jnp.bfloat16)
-
-
-def sum_columns(place, table, chosen_own, chosen_back, parts):
+            total = dot(spread, up[:, pl.ds(begin, HEAD_SIZE)])
+            if i == PLANES - 1:
+                last[:, h * HEAD_SIZE : (h + 1) * HEAD_SIZE] = total
+                out[:, pl.ds(begin, HEAD_SIZE)] = total.astype(jnp.bfloat16)
+                continue
+            first, at = (0, i * WIDE + h * HEAD_SIZE) if i < 2 else (4, h * HEAD_SIZE)
+            for v in parts[first : first + 4]:
+                total = total + v[:rows, at : at + HEAD_SIZE].astype(jnp.float32)
+            out[:, pl.ds(begin, HEAD_SIZE)] = total.astype(jnp.bfloat16)
+
+
+def sum_columns(place, table, chosen_own, kv_back, parts):
     rows = parts[-1].shape[0]
     width = chosen_own.shape[2]
     return pl.pallas_call(
         sum_kernel,
-        in_specs=[in_smem()] * 2 + [in_vmem()] * 14,
-        out_specs=in_vmem(),
-        out_shape=jax.ShapeDtypeStruct((rows, width), jnp.bfloat16),
+        in_specs=[in_smem()] * 2 + [in_vmem()] * 10,
+        out_specs=[in_vmem()] * 2,
+        out_shape=[
+            jax.ShapeDtypeStruct((rows, width), jnp.bfloat16),
+            jax.ShapeDtypeStruct((rows, WIDE), jnp.float32),
+        ],
         scratch_shapes=[pltpu.VMEM((4 * ADAPTER_RANK, width), jnp.bfloat16)],
         compiler_params=kernel_params(56),
-        cost_estimate=cost(2 * rows * width * (8 + 4 * ADAPTER_RANK), 12 * rows * width, 0),
+        cost_estimate=cost(2 * rows * width * (8 + 4 * ADAPTER_RANK), 12 * rows * width),
         name="sum_columns",
-    )(place, table, chosen_own, chosen_back, *parts)
+    )(place, table, chosen_own, kv_back, *parts)
+
+
+def last_columns_kernel(place, given, p0, p1, p2, p3, whole, out):
+    del place, whole
+    total = given[...] + sum(v[...].astype(jnp.float32) for v in (p0, p1, p2, p3))
+    out[...] = total.astype(jnp.bfloat16)
+
+
+def last_columns(place, given, parts, whole):
+    rows = given.shape[0]
+    tile = pl.BlockSpec((rows, HEAD_SIZE), lambda i, place: (0, i))
+    return pl.pallas_call(
+        last_columns_kernel,
+        grid_spec=pltpu.PrefetchScalarGridSpec(
+            num_scalar_prefetch=1,
+            grid=(2,),
+            in_specs=[tile] * 5 + [pl.BlockSpec(memory_space=pl.ANY)],
+            out_specs=pl.BlockSpec(
+                (rows, HEAD_SIZE), lambda i, place: (0, 2 * place[10] + (place[0] ^ i))
+            ),
+        ),
+        out_shape=jax.ShapeDtypeStruct(whole.shape, whole.dtype),
+        input_output_aliases={6: 0},
+        compiler_params=kernel_params(12),
+        cost_estimate=cost(8 * rows * WIDE, 16 * rows * WIDE),
+        name="last_columns",
+    )(place, given, *parts, whole)
 
 
 def shards_by_plane(
@@ -891,7 +949,6 @@
         place, table, end_table, adapter_storage, x, packed, 2 * key_value_width
     )
     lows = [low] + to_blocks([low] * BLOCKS)
-    chosen_back = along(chosen_end, OUTWARD)
 
     kv_own, kv_end = project(
         place,
@@ -903,6 +960,7 @@
         lows,
         up_kv,
         False,
+        chosen_end,
     )
     kv_back = along(kv_end, OUTWARD)
     q_3, wo_0, wo_1 = gate([q_3, wo_0, wo_1], [kv_own])
@@ -919,7 +977,7 @@
         up,
         True,
     )
-    raw_end, kv_back, chosen_back = gate([raw_end, kv_back, chosen_back], [])
+    raw_end, kv_back = gate([raw_end, kv_back], [])
     raw_back = along(raw_end, OUTWARD)
     wo_0x, wo_1x = along(wo_0, CORES), along(wo_1, CORES)
     wo_mid1, raw_back = gate([wo_mid1, raw_back], [wo_0x, wo_1x])
@@ -941,7 +999,6 @@
         cosine,
         sine,
         chosen_own,
-        chosen_back,
     )
     new_cache = cache.reshape(row_count, 2, key_value_width)
 
@@ -964,7 +1021,8 @@
         mebibytes=12,
     )
     parts += [last_parts[0]] + to_blocks(last_parts)
-    attention_update = sum_columns(place, table, chosen_own, chosen_back, parts)
+    whole, given = sum_columns(place, table, chosen_own, kv_back, parts[:8])
+    attention_update = last_columns(place, given, parts[8:], whole)
     return (attention_update, new_cache)
 
 

time: 250 us -> 248 us (level)
  waiting for transfers between devices: 81 us -> 78.1 us
    ppermute x12, waiting for transfers between devices: 21.9 us -> 17.5 us  [to_blocks(): lax.ppermute(piece, 'mlp', [(b, b ^ k) for b in range(BLOCKS)])]
    ppermute x29 -> x28, waiting for transfers between devices: 56.1 us -> 57.6 us  [along(): return lax.ppermute(value, 'req', pairs)]
    ppermute x29 -> x28, starting transfers between devices: 34.7 us -> 33.2 us  [along(): return lax.ppermute(value, 'req', pairs)]
    pallas_call x1 -> x2, Pallas kernels: 3.77 us -> 5.08 us  [the longest x1 3.55 us: sum_columns(): pl.pallas_call(sum_kernel, in_specs=[in_smem()] * 2 + [in_vmem()] * 10, o...]
    unnamed x103 -> x95, local copies, waits for them, and re-layouts: 19.3 us -> 19.3 us
  transfers between devices with their start and end apart: 47 -> 46, of which waited for: 18 -> 16; matrix products, arithmetic and copies ran while one was open for 10% -> 10% of each run, Pallas kernels for 27% -> 29%
where the time goes in v3:
time: 248 us; the launch traced here: 247 us
  waiting for transfers between devices  78.1 us (31%)
  Pallas kernels  71.9 us (29%)
  starting transfers between devices  55.6 us (22%)
  local copies, waits for them, and re-layouts  31.1 us (13%)
  other arithmetic  8.91 us (4%)
    ppermute x28, waiting for transfers between devices, along(): return lax.ppermute(value, 'req', pairs)  57.6 us
    ppermute x28, starting transfers between devices, along(): return lax.ppermute(value, 'req', pairs)  33.2 us
    pallas_call x2, Pallas kernels, project(): pl.pallas_call(functools.partial(project_kernel, is_q), in_specs=[in_smem...  19.5 us
    unnamed x95, local copies, waits for them, and re-layouts  19.3 us
    ppermute x12, waiting for transfers between devices, to_blocks(): lax.ppermute(piece, 'mlp', [(b, b ^ k) for b in range(BLOCKS)])  17.5 us
    pallas_call x3, Pallas kernels, project_columns(): pl.pallas_call(functools.partial(columns_kernel, len(chunks)), in_specs=[...  14.9 us
    ppermute x12, starting transfers between devices, to_blocks(): lax.ppermute(piece, 'mlp', [(b, b ^ k) for b in range(BLOCKS)])  14.1 us
    pallas_call x2, Pallas kernels, norm_rows(): pl.pallas_call(norm_kernel, grid_spec=pltpu.PrefetchScalarGridSpec(num_sc...  11.6 us
  transfers between devices with their start and end apart: 46, of which 16 were waited for; matrix products, arithmetic and copies ran while one was open for 10% of the time, Pallas kernels for 29%

profile of v3, /device:TPU:0, one launch (start us, length us, event | category | flops | bytes accessed | tf_op | source)
XLA Modules:
  0.0 246.7 jit_solution(17350005831143040501)
XLA Ops:
  0.6 3.0 %collective-permute-start.1 = (bf16[384,1024]{1,0:T(8,128)(2,1)}, bf16[384,1024]{1,0:T(8,128)(2,1)}, u32[]{:S(2)}, u32[]{:S(2)}) collective-permute-start(bf16[384,1024]{1,0:T(8,128)(2,1)} %p0.1), channel_id=1, source_target_pairs={{0,2},{1,3},{2,0},{3,1},{4,6},{5,7},{6,4},{7,5},{8,10},{9,11},{10,... | collective-permute-start | bytes 2359304 | tf_op jit(solution)/shard_map/ppermute | solution.py:250
  5.2 3.5 %collective-permute-start = (bf16[384,1024]{1,0:T(8,128)(2,1)}, bf16[384,1024]{1,0:T(8,128)(2,1)S(1)}, u32[]{:S(2)}, u32[]{:S(2)}) collective-permute-start(bf16[384,1024]{1,0:T(8,128)(2,1)} %p0.1), channel_id=1, source_target_pairs={{0,8},{4,12},{24,16},{28,20},{1,9},{5,13},{25,17},{29,21},{2,10},{... | collective-permute-start | bytes 2359304 | tf_op jit(solution)/shard_map/ppermute | solution.py:246
  30.4 6.1 %collective-permute-start.4 = (bf16[512,1024]{1,0:T(8,128)(2,1)}, bf16[512,1024]{1,0:T(8,128)(2,1)S(1)}, u32[]{:S(2)}, u32[]{:S(2)}) collective-permute-start(bf16[512,1024]{1,0:T(8,128)(2,1)} %get-tuple-element.60.refs_0_), channel_id=1, source_target_pairs={{0,8},{4,12},{24,16},{28,20},{1,9},{5,13},{25,17},{29,21},{2,10},{... | collective-permute-start | bytes 3145736 | tf_op jit(solution)/shard_map/ppermute | solution.py:246
  38.6 21.3 %collective-permute-done.4.refs_0_ = bf16[512,1024]{1,0:T(8,128)(2,1)S(1)} collective-permute-done((bf16[512,1024]{1,0:T(8,128)(2,1)}, bf16[512,1024]{1,0:T(8,128)(2,1)S(1)}, u32[]{:S(2)}, u32[]{:S(2)}) %collective-permute-start.4) | collective-permute-done | bytes 1048608 | tf_op jit(solution)/shard_map/ppermute | solution.py:246
  59.9 2.8 %collective-permute-done.9.refs_6_.refs_5_ = bf16[512,1024]{1,0:T(8,128)(2,1)S(1)} collective-permute-done((bf16[512,1024]{1,0:T(8,128)(2,1)}, bf16[512,1024]{1,0:T(8,128)(2,1)S(1)}, u32[]{:S(2)}, u32[]{:S(2)}) %collective-permute-start.9) | collective-permute-done | bytes 1048608 | tf_op jit(solution)/shard_map/ppermute | solution.py:246
  66.0 4.1 %collective-permute-start.13 = (bf16[512,1024]{1,0:T(8,128)(2,1)}, bf16[512,1024]{1,0:T(8,128)(2,1)}, u32[]{:S(2)}, u32[]{:S(2)}) collective-permute-start(bf16[512,1024]{1,0:T(8,128)(2,1)} %get-tuple-element.70), channel_id=1, source_target_pairs={{0,8},{4,12},{24,16},{28,20},{1,9},{5,13},{25,17},{29,21},{2,10},{... | collective-permute-start | bytes 3145736 | tf_op jit(solution)/shard_map/ppermute | solution.py:246
  76.6 5.8 %norm_rows.2 = (bf16[768,4096]{1,0:T(8,128)(2,1)}, f32[8,128]{1,0:T(8,128)}) custom-call(s32[15]{0:T(128)} %stack.61.place, f32[4,1024]{1,0:T(4,128)} %reshape.49.gain, bf16[384,1024]{1,0:T(8,128)(2,1)} %p0.1, bf16[384,1024]{1,0:T(8,128)(2,1)} %collective-permute-done.2.p1, bf16[384,1024]{1,0:T(8,128)(2,1)} %collective-permute-done.1.p2, ...), custom_call_target="tpu_custom_call" | custom-call | flops 6291456 | bytes 6291456 | tf_op jit(solution)/shard_map/norm_rows/pallas_call | solution.py:349
  84.9 5.8 %norm_rows.3 = (bf16[768,4096]{1,0:T(8,128)(2,1)}, f32[8,128]{1,0:T(8,128)}) custom-call(s32[15]{0:T(128)} %stack.61.place, f32[4,1024]{1,0:T(4,128)} %reshape.49.gain, bf16[384,1024]{1,0:T(8,128)(2,1)} %copy-done.25, bf16[576,1024]{1,0:T(8,128)(2,1)} %get-tuple-element.66.p4.p1, ...), custom_call_target="tpu_custom_call", output_to_operand_aliasing={{0}: (7, {})} | custom-call | flops 6291456 | bytes 6291456 | tf_op jit(solution)/shard_map/norm_rows/pallas_call | solution.py:349
  94.4 6.5 %collective-permute-start.20 = (bf16[4,1024,128]{2,1,0:T(8,128)(2,1)}, bf16[4,1024,128]{2,1,0:T(8,128)(2,1)S(1)}, u32[]{:S(2)}, u32[]{:S(2)}) collective-permute-start(bf16[4,1024,128]{2,1,0:T(8,128)(2,1)} %get-tuple-element.79.refs_1_), channel_id=1, source_target_pairs={{0,8},{4,12},{8,0},{12,4},{16,24},{20,28},{24,16},{28,20},{1,9},{5... | collective-permute-start | bytes 3145736 | tf_op jit(solution)/shard_map/ppermute | solution.py:246
  102.5 7.1 %rank_terms.1 = (bf16[48,768]{1,0:T(8,128)(2,1)}, bf16[4,32,1024]{2,1,0:T(8,128)(2,1)}, bf16[4,32,1024]{2,1,0:T(8,128)(2,1)}, bf16[256,1024]{1,0:T(8,128)(2,1)}, bf16[256,512]{1,0:T(8,128)(2,1)}) custom-call(s32[15]{0:T(128)} %stack.61.place, s32[8]{0:T(128)} %pad_add_fusion.table.own_table, s32[8]{0:T(128)} %bitcast_convert_fusion.2.end_table, s32[16]{0:T(128)} %storage.5, ...), custom_call_target="tpu_custom_call" | custom-call | flops 1207959552 | bytes 6815744 | tf_op jit(solution)/shard_map/rank_terms/pallas_call | solution.py:462
  117.2 7.6 %project_key_value.1 = (bf16[384,512]{1,0:T(8,128)(2,1)}, bf16[640,512]{1,0:T(8,128)(2,1)}) custom-call(s32[15]{0:T(128)} %stack.61.place, s32[8]{0:T(128)} %pad_add_fusion.table.own_table, s32[8]{0:T(128)} %bitcast_convert_fusion.2.end_table, s32[16]{0:T(128)} %storage.5, bf16[768,4096]{1,0:T(8,128)(2,1)} %get-tuple-element.69.x, ...), custom_call_target="tpu_custom_call" | custom-call | flops 3422552064 | bytes 11272192 | tf_op jit(solution)/shard_map/project_key_value/pallas_call | solution.py:561
  130.8 12.0 %project_query.1 = (bf16[384,1024]{1,0:T(8,128)(2,1)}, bf16[384,1024]{1,0:T(8,128)(2,1)}) custom-call(s32[15]{0:T(128)} %stack.61.place, s32[8]{0:T(128)} %pad_add_fusion.table.own_table, s32[8]{0:T(128)} %bitcast_convert_fusion.2.end_table, s32[16]{0:T(128)} %storage.5, bf16[768,4096]{1,0:T(8,128)(2,1)} %get-tuple-element.69.x, bf16[512,1024]{1,0:T(8,128)(2,1)} %refs_0_.1, ...), custom_call_target="tpu_custom_call" | custom-call | flops 6845104128 | bytes 16252928 | tf_op jit(solution)/shard_map/project_query/pallas_call | solution.py:561
  142.8 2.5 %collective-permute-done.25.refs_1_ = bf16[640,512]{1,0:T(8,128)(2,1)S(1)} collective-permute-done((bf16[640,512]{1,0:T(8,128)(2,1)}, bf16[640,512]{1,0:T(8,128)(2,1)S(1)}, u32[]{:S(2)}, u32[]{:S(2)}) %collective-permute-start.25) | collective-permute-done | bytes 655392 | tf_op jit(solution)/shard_map/ppermute | solution.py:246
  148.4 19.3 %collective-permute-done.27.refs_1_ = bf16[384,1024]{1,0:T(8,128)(2,1)} collective-permute-done((bf16[384,1024]{1,0:T(8,128)(2,1)}, bf16[384,1024]{1,0:T(8,128)(2,1)}, u32[]{:S(2)}, u32[]{:S(2)}) %collective-permute-start.27) | collective-permute-done | bytes 786464 | tf_op jit(solution)/shard_map/ppermute | solution.py:246
  170.2 11.4 %attend.1 = (bf16[384,1024]{1,0:T(8,128)(2,1)}, bf16[384,512]{1,0:T(8,128)(2,1)}, f32[16,384]{1,0:T(8,128)}) custom-call(s32[15]{0:T(128)} %stack.61.place, s32[8]{0:T(128)} %pad_add_fusion.table.own_table, s32[4]{0:T(128)} %bitcast.50, s32[32]{0:T(128)} %reshape_squeeze.3.pages, bf16[384,1024]{1,0:T(8,128)(2,1)} %get-tuple-element.89.own, ...), custom_call_target="tpu_custom_call" | custom-call | flops 1409286144 | bytes 2359296 | tf_op jit(solution)/shard_map/attend/pallas_call | solution.py:683
  182.6 5.5 %project_columns.3 = (bf16[400,512]{1,0:T(8,128)(2,1)}, bf16[400,512]{1,0:T(8,128)(2,1)}, bf16[400,512]{1,0:T(8,128)(2,1)}, bf16[400,512]{1,0:T(8,128)(2,1)}) custom-call(s32[15]{0:T(128)} %stack.61.place, bf16[384,1024]{1,0:T(8,128)(2,1)} %get-tuple-element.99.attended, bf16[4,1024,128]{2,1,0:T(8,128)(2,1)} %get-tuple-element.90.refs_0_.refs_2_, ...), custom_call_target="tpu_custom_call" | custom-call | flops 1677721600 | bytes 6651904 | tf_op jit(solution)/shard_map/project_columns/pallas_call | solution.py:758
  188.1 5.6 %collective-permute-done.34.refs_0_ = bf16[4,1024,128]{2,1,0:T(8,128)(2,1)S(1)} collective-permute-done((bf16[4,1024,128]{2,1,0:T(8,128)(2,1)}, bf16[4,1024,128]{2,1,0:T(8,128)(2,1)S(1)}, u32[]{:S(2)}, u32[]{:S(2)}) %collective-permute-start.34) | collective-permute-done | bytes 1048608 | tf_op jit(solution)/shard_map/ppermute | solution.py:246
  201.8 5.0 %project_columns.4 = (bf16[384,256]{1,0:T(8,128)(2,1)}, bf16[384,256]{1,0:T(8,128)(2,1)}, bf16[384,256]{1,0:T(8,128)(2,1)}, bf16[384,256]{1,0:T(8,128)(2,1)}) custom-call(s32[15]{0:T(128)} %stack.61.place, bf16[384,1024]{1,0:T(8,128)(2,1)} %get-tuple-element.99.attended, bf16[4,1024,128]{2,1,0:T(8,128)(2,1)} %gate.16.refs_0_, ...), custom_call_target="tpu_custom_call" | custom-call | flops 805306368 | bytes 3670016 | tf_op jit(solution)/shard_map/project_columns/pallas_call | solution.py:758
  206.9 3.0 %collective-permute-done.31.refs_1_.refs_2_ = bf16[400,512]{1,0:T(8,128)(2,1)S(1)} collective-permute-done((bf16[400,512]{1,0:T(8,128)(2,1)}, bf16[400,512]{1,0:T(8,128)(2,1)S(1)}, u32[]{:S(2)}, u32[]{:S(2)}) %collective-permute-start.31) | collective-permute-done | bytes 409632 | tf_op jit(solution)/shard_map/ppermute | solution.py:255
  209.9 7.7 %collective-permute-done.32.refs_2_.refs_3_ = bf16[400,512]{1,0:T(8,128)(2,1)S(1)} collective-permute-done((bf16[400,512]{1,0:T(8,128)(2,1)}, bf16[400,512]{1,0:T(8,128)(2,1)S(1)}, u32[]{:S(2)}, u32[]{:S(2)}) %collective-permute-start.32) | collective-permute-done | bytes 409632 | tf_op jit(solution)/shard_map/ppermute | solution.py:255
  217.6 4.5 %collective-permute-done.40.refs_0_ = bf16[4,1024,128]{2,1,0:T(8,128)(2,1)S(1)} collective-permute-done((bf16[4,1024,128]{2,1,0:T(8,128)(2,1)S(1)}, bf16[4,1024,128]{2,1,0:T(8,128)(2,1)S(1)}, u32[]{:S(2)}, u32[]{:S(2)}) %collective-permute-start.40) | collective-permute-done | bytes 1048608 | tf_op jit(solution)/shard_map/ppermute | solution.py:246
  227.5 4.4 %project_columns.5 = (bf16[384,256]{1,0:T(8,128)(2,1)S(1)}, bf16[384,256]{1,0:T(8,128)(2,1)S(1)}, bf16[384,256]{1,0:T(8,128)(2,1)S(1)}, bf16[384,256]{1,0:T(8,128)(2,1)S(1)}) custom-call(s32[15]{0:T(128)S(1)} %copy-done.11, bf16[384,1024]{1,0:T(8,128)(2,1)S(1)} %copy-done.2, bf16[4,1024,128]{2,1,0:T(8,128)(2,1)S(1)} %gate.17.refs_0_, ...), custom_call_target="tpu_custom_call" | custom-call | flops 805306368 | bytes 3670016 | tf_op jit(solution)/shard_map/project_columns/pallas_call | solution.py:758
  237.3 3.5 %sum_columns.1 = (bf16[384,1024]{1,0:T(8,128)(2,1)}, f32[384,256]{1,0:T(8,128)}) custom-call(s32[15]{0:T(128)} %stack.61.place, s32[8]{0:T(128)} %pad_add_fusion.table.own_table, bf16[4,32,1024]{2,1,0:T(8,128)(2,1)} %get-tuple-element.77.chosen_own, bf16[640,512]{1,0:T(8,128)(2,1)} %get-tuple-element.88.kv_back, ...), custom_call_target="tpu_custom_call" | custom-call | flops 56623104 | bytes 4718592 | tf_op jit(solution)/shard_map/sum_columns/pallas_call | solution.py:808
  240.9 3.2 %collective-permute-done.44.p2 = bf16[384,256]{1,0:T(8,128)(2,1)S(1)} collective-permute-done((bf16[384,256]{1,0:T(8,128)(2,1)S(1)}, bf16[384,256]{1,0:T(8,128)(2,1)S(1)}, u32[]{:S(2)}, u32[]{:S(2)}) %collective-permute-start.44) | collective-permute-done | bytes 196640 | tf_op jit(solution)/shard_map/ppermute | solution.py:255
  (210 shorter events, 84.2 us)
Async XLA Ops:
  0.6 25.9 %collective-permute-start.1 = (bf16[384,1024]{1,0:T(8,128)(2,1)}, bf16[384,1024]{1,0:T(8,128)(2,1)}, u32[]{:S(2)}, u32[]{:S(2)}) collective-permute-start(bf16[384,1024]{1,0:T(8,128)(2,1)} %p0.1), channel_id=1, source_target_pairs={{0,2},{1,3},{2,0},{3,1},{4,6},{5,7},{6,4},{7,5},{8,10},{9,11},{10,... | collective-permute-start | bytes 2359304 | tf_op jit(solution)/shard_map/ppermute | solution.py:250
  3.7 23.9 %collective-permute-start.2 = (bf16[384,1024]{1,0:T(8,128)(2,1)}, bf16[384,1024]{1,0:T(8,128)(2,1)}, u32[]{:S(2)}, u32[]{:S(2)}) collective-permute-start(bf16[384,1024]{1,0:T(8,128)(2,1)} %p0.1), channel_id=1, source_target_pairs={{0,1},{1,0},{2,3},{3,2},{4,5},{5,4},{6,7},{7,6},{8,9},{9,8},{10,11... | collective-permute-start | bytes 2359304 | tf_op jit(solution)/shard_map/ppermute | solution.py:250
  5.2 23.5 %collective-permute-start = (bf16[384,1024]{1,0:T(8,128)(2,1)}, bf16[384,1024]{1,0:T(8,128)(2,1)S(1)}, u32[]{:S(2)}, u32[]{:S(2)}) collective-permute-start(bf16[384,1024]{1,0:T(8,128)(2,1)} %p0.1), channel_id=1, source_target_pairs={{0,8},{4,12},{24,16},{28,20},{1,9},{5,13},{25,17},{29,21},{2,10},{... | collective-permute-start | bytes 2359304 | tf_op jit(solution)/shard_map/ppermute | solution.py:246
  8.7 21.7 %collective-permute-start.3 = (bf16[512,1024]{1,0:T(8,128)(2,1)}, bf16[512,1024]{1,0:T(8,128)(2,1)}, u32[]{:S(2)}, u32[]{:S(2)}) collective-permute-start(bf16[512,1024]{1,0:T(8,128)(2,1)} %refs_0_.1), channel_id=1, source_target_pairs={{8,16},{12,20},{16,8},{20,12},{9,17},{13,21},{17,9},{21,13},{10,18... | collective-permute-start | bytes 3145736 | tf_op jit(solution)/shard_map/ppermute | solution.py:246
  30.4 29.5 %collective-permute-start.4 = (bf16[512,1024]{1,0:T(8,128)(2,1)}, bf16[512,1024]{1,0:T(8,128)(2,1)S(1)}, u32[]{:S(2)}, u32[]{:S(2)}) collective-permute-start(bf16[512,1024]{1,0:T(8,128)(2,1)} %get-tuple-element.60.refs_0_), channel_id=1, source_target_pairs={{0,8},{4,12},{24,16},{28,20},{1,9},{5,13},{25,17},{29,21},{2,10},{... | collective-permute-start | bytes 3145736 | tf_op jit(solution)/shard_map/ppermute | solution.py:246
  36.6 28.4 %collective-permute-start.6 = (bf16[576,1024]{1,0:T(8,128)(2,1)}, bf16[576,1024]{1,0:T(8,128)(2,1)S(1)}, u32[]{:S(2)}, u32[]{:S(2)}) collective-permute-start(bf16[576,1024]{1,0:T(8,128)(2,1)} %get-tuple-element.61), channel_id=1, source_target_pairs={{0,1},{1,0},{2,3},{3,2},{4,5},{5,4},{6,7},{7,6},{8,9},{9,8},{10,11... | collective-permute-start | bytes 3538952 | tf_op jit(solution)/shard_map/ppermute | solution.py:250
  37.2 28.1 %collective-permute-start.7 = (bf16[576,1024]{1,0:T(8,128)(2,1)}, bf16[576,1024]{1,0:T(8,128)(2,1)}, u32[]{:S(2)}, u32[]{:S(2)}) collective-permute-start(bf16[576,1024]{1,0:T(8,128)(2,1)} %get-tuple-element.62), channel_id=1, source_target_pairs={{0,2},{1,3},{2,0},{3,1},{4,6},{5,7},{6,4},{7,5},{8,10},{9,11},{10,... | collective-permute-start | bytes 3538952 | tf_op jit(solution)/shard_map/ppermute | solution.py:250
  37.8 22.1 %collective-permute-start.5 = (bf16[512,1024]{1,0:T(8,128)(2,1)}, bf16[512,1024]{1,0:T(8,128)(2,1)S(1)}, u32[]{:S(2)}, u32[]{:S(2)}) collective-permute-start(bf16[512,1024]{1,0:T(8,128)(2,1)} %get-tuple-element.60.refs_0_), channel_id=1, source_target_pairs={{8,16},{12,20},{16,8},{20,12},{9,17},{13,21},{17,9},{21,13},{10,18... | collective-permute-start | bytes 3145736 | tf_op jit(solution)/shard_map/ppermute | solution.py:246
  38.5 21.4 %collective-permute-start.8 = (bf16[512,1024]{1,0:T(8,128)(2,1)}, bf16[512,1024]{1,0:T(8,128)(2,1)S(1)}, u32[]{:S(2)}, u32[]{:S(2)}) collective-permute-start(bf16[512,1024]{1,0:T(8,128)(2,1)} %get-tuple-element.63.refs_4_), channel_id=1, source_target_pairs={{0,4},{4,0},{8,12},{12,8},{16,20},{20,16},{24,28},{28,24},{1,5},{5... | collective-permute-start | bytes 3145736 | tf_op jit(solution)/shard_map/ppermute | solution.py:246
  66.0 26.2 %collective-permute-start.13 = (bf16[512,1024]{1,0:T(8,128)(2,1)}, bf16[512,1024]{1,0:T(8,128)(2,1)}, u32[]{:S(2)}, u32[]{:S(2)}) collective-permute-start(bf16[512,1024]{1,0:T(8,128)(2,1)} %get-tuple-element.70), channel_id=1, source_target_pairs={{0,8},{4,12},{24,16},{28,20},{1,9},{5,13},{25,17},{29,21},{2,10},{... | collective-permute-start | bytes 3145736 | tf_op jit(solution)/shard_map/ppermute | solution.py:246
  70.1 22.0 %collective-permute-start.14 = (bf16[512,1024]{1,0:T(8,128)(2,1)}, bf16[512,1024]{1,0:T(8,128)(2,1)S(1)}, u32[]{:S(2)}, u32[]{:S(2)}) collective-permute-start(bf16[512,1024]{1,0:T(8,128)(2,1)} %get-tuple-element.65.refs_1_), channel_id=1, source_target_pairs={{8,16},{12,20},{16,8},{20,12},{9,17},{13,21},{17,9},{21,13},{10,18... | collective-permute-start | bytes 3145736 | tf_op jit(solution)/shard_map/ppermute | solution.py:246
  93.7 31.1 %collective-permute-start.19 = (bf16[512,1024]{1,0:T(8,128)(2,1)}, bf16[512,1024]{1,0:T(8,128)(2,1)S(1)}, u32[]{:S(2)}, u32[]{:S(2)}) collective-permute-start(bf16[512,1024]{1,0:T(8,128)(2,1)} %get-tuple-element.78.refs_2_), channel_id=1, source_target_pairs={{8,16},{12,20},{16,8},{20,12},{9,17},{13,21},{17,9},{21,13},{10,18... | collective-permute-start | bytes 3145736 | tf_op jit(solution)/shard_map/ppermute | solution.py:246
  94.4 30.4 %collective-permute-start.20 = (bf16[4,1024,128]{2,1,0:T(8,128)(2,1)}, bf16[4,1024,128]{2,1,0:T(8,128)(2,1)S(1)}, u32[]{:S(2)}, u32[]{:S(2)}) collective-permute-start(bf16[4,1024,128]{2,1,0:T(8,128)(2,1)} %get-tuple-element.79.refs_1_), channel_id=1, source_target_pairs={{0,8},{4,12},{8,0},{12,4},{16,24},{20,28},{24,16},{28,20},{1,9},{5... | collective-permute-start | bytes 3145736 | tf_op jit(solution)/shard_map/ppermute | solution.py:246
  126.1 19.2 %collective-permute-start.25 = (bf16[640,512]{1,0:T(8,128)(2,1)}, bf16[640,512]{1,0:T(8,128)(2,1)S(1)}, u32[]{:S(2)}, u32[]{:S(2)}) collective-permute-start(bf16[640,512]{1,0:T(8,128)(2,1)} %get-tuple-element.87), channel_id=1, source_target_pairs={{8,0},{12,4},{16,24},{20,28},{9,1},{13,5},{17,25},{21,29},{10,2},{... | collective-permute-start | bytes 1966088 | tf_op jit(solution)/shard_map/ppermute | solution.py:246
  127.4 21.0 %collective-permute-start.26 = (bf16[4,1024,128]{2,1,0:T(8,128)(2,1)}, bf16[4,1024,128]{2,1,0:T(8,128)(2,1)}, u32[]{:S(2)}, u32[]{:S(2)}) collective-permute-start(bf16[4,1024,128]{2,1,0:T(8,128)(2,1)} %get-tuple-element.90.refs_0_.refs_2_), channel_id=1, source_target_pairs={{8,16},{12,20},{16,8},{20,12},{9,17},{13,21},{17,9},{21,13},{10,18... | collective-permute-start | bytes 3145736 | tf_op jit(solution)/shard_map/ppermute | solution.py:246
  129.3 19.1 %collective-permute-start.28 = (bf16[4,1024,128]{2,1,0:T(8,128)(2,1)}, bf16[4,1024,128]{2,1,0:T(8,128)(2,1)S(1)}, u32[]{:S(2)}, u32[]{:S(2)}) collective-permute-start(bf16[4,1024,128]{2,1,0:T(8,128)(2,1)} %get-tuple-element.90.refs_0_.refs_2_), channel_id=1, source_target_pairs={{0,4},{4,0},{8,12},{12,8},{16,20},{20,16},{24,28},{28,24},{1,5},{5... | collective-permute-start | bytes 3145736 | tf_op jit(solution)/shard_map/ppermute | solution.py:246
  129.8 18.6 %collective-permute-start.29 = (bf16[4,1024,128]{2,1,0:T(8,128)(2,1)}, bf16[4,1024,128]{2,1,0:T(8,128)(2,1)}, u32[]{:S(2)}, u32[]{:S(2)}) collective-permute-start(bf16[4,1024,128]{2,1,0:T(8,128)(2,1)} %get-tuple-element.92.refs_4_.refs_6_), channel_id=1, source_target_pairs={{0,4},{4,0},{8,12},{12,8},{16,20},{20,16},{24,28},{28,24},{1,5},{5... | collective-permute-start | bytes 3145736 | tf_op jit(solution)/shard_map/ppermute | solution.py:246
  146.2 21.5 %collective-permute-start.27 = (bf16[384,1024]{1,0:T(8,128)(2,1)}, bf16[384,1024]{1,0:T(8,128)(2,1)}, u32[]{:S(2)}, u32[]{:S(2)}) collective-permute-start(bf16[384,1024]{1,0:T(8,128)(2,1)} %get-tuple-element.91), channel_id=1, source_target_pairs={{8,0},{12,4},{16,24},{20,28},{9,1},{13,5},{17,25},{21,29},{10,2},{... | collective-permute-start | bytes 2359304 | tf_op jit(solution)/shard_map/ppermute | solution.py:246
  147.6 34.0 %collective-permute-start.30 = (bf16[4,1024,128]{2,1,0:T(8,128)(2,1)S(1)}, bf16[4,1024,128]{2,1,0:T(8,128)(2,1)S(1)}, u32[]{:S(2)}, u32[]{:S(2)}) collective-permute-start(bf16[4,1024,128]{2,1,0:T(8,128)(2,1)S(1)} %copy-done.19), channel_id=1, source_target_pairs={{8,16},{12,20},{16,8},{20,12},{9,17},{13,21},{17,9},{21,13},{10,18... | collective-permute-start | bytes 3145736 | tf_op jit(solution)/shard_map/ppermute | solution.py:246
  167.7 26.0 %collective-permute-start.34 = (bf16[4,1024,128]{2,1,0:T(8,128)(2,1)}, bf16[4,1024,128]{2,1,0:T(8,128)(2,1)S(1)}, u32[]{:S(2)}, u32[]{:S(2)}) collective-permute-start(bf16[4,1024,128]{2,1,0:T(8,128)(2,1)} %get-tuple-element.105.refs_2_), channel_id=1, source_target_pairs={{8,0},{12,4},{16,24},{20,28},{9,1},{13,5},{17,25},{21,29},{10,2},{... | collective-permute-start | bytes 3145736 | tf_op jit(solution)/shard_map/ppermute | solution.py:246
  169.0 30.8 %collective-permute-start.36 = (bf16[4,1024,128]{2,1,0:T(8,128)(2,1)}, bf16[4,1024,128]{2,1,0:T(8,128)(2,1)}, u32[]{:S(2)}, u32[]{:S(2)}) collective-permute-start(bf16[4,1024,128]{2,1,0:T(8,128)(2,1)} %get-tuple-element.105.refs_2_), channel_id=1, source_target_pairs={{0,4},{4,0},{8,12},{12,8},{16,20},{20,16},{24,28},{28,24},{1,5},{5... | collective-permute-start | bytes 3145736 | tf_op jit(solution)/shard_map/ppermute | solution.py:246
  195.9 26.2 %collective-permute-start.40 = (bf16[4,1024,128]{2,1,0:T(8,128)(2,1)S(1)}, bf16[4,1024,128]{2,1,0:T(8,128)(2,1)S(1)}, u32[]{:S(2)}, u32[]{:S(2)}) collective-permute-start(bf16[4,1024,128]{2,1,0:T(8,128)(2,1)S(1)} %copy-done.4), channel_id=1, source_target_pairs={{8,0},{12,4},{16,24},{20,28},{9,1},{13,5},{17,25},{21,29},{10,2},{... | collective-permute-start | bytes 3145736 | tf_op jit(solution)/shard_map/ppermute | solution.py:246
  198.2 19.4 %collective-permute-start.32 = (bf16[400,512]{1,0:T(8,128)(2,1)}, bf16[400,512]{1,0:T(8,128)(2,1)S(1)}, u32[]{:S(2)}, u32[]{:S(2)}) collective-permute-start(bf16[400,512]{1,0:T(8,128)(2,1)} %get-tuple-element.103), channel_id=1, source_target_pairs={{0,2},{1,3},{2,0},{3,1},{4,6},{5,7},{6,4},{7,5},{8,10},{9,11},{10,... | collective-permute-start | bytes 1228808 | tf_op jit(solution)/shard_map/ppermute | solution.py:255
  200.8 26.7 %collective-permute-start.42 = (bf16[4,1024,128]{2,1,0:T(8,128)(2,1)S(1)}, bf16[4,1024,128]{2,1,0:T(8,128)(2,1)S(1)}, u32[]{:S(2)}, u32[]{:S(2)}) collective-permute-start(bf16[4,1024,128]{2,1,0:T(8,128)(2,1)S(1)} %copy-done.4), channel_id=1, source_target_pairs={{0,4},{4,0},{8,12},{12,8},{16,20},{20,16},{24,28},{28,24},{1,5},{5... | collective-permute-start | bytes 3145736 | tf_op jit(solution)/shard_map/ppermute | solution.py:246
  (68 other events, 455.7 us)

commit v4 on v3

--- a/solution.py
+++ b/solution.py
@@ -262,7 +262,7 @@
     del refs
 
 
-def gate(values, earlier, mebibytes=60):
+def gate(values, earlier, mebibytes=1):
     return pl.pallas_call(
         gate_kernel,
         in_specs=[pl.BlockSpec(memory_space=pl.ANY)] * (len(values) + len(earlier)),

time: 248 us -> 247 us (level)
  starting transfers between devices: 55.6 us -> 60.1 us
  waiting for transfers between devices: 78.1 us -> 74.9 us
    ppermute x28, starting transfers between devices: 33.2 us -> 38 us  [along(): return lax.ppermute(value, 'req', pairs)]
    ppermute x28, waiting for transfers between devices: 57.6 us -> 53.1 us  [along(): return lax.ppermute(value, 'req', pairs)]
    unnamed x95 -> x129, local copies, waits for them, and re-layouts: 19.3 us -> 19.1 us
  transfers between devices with their start and end apart: 46 -> 46, of which waited for: 16 -> 17; matrix products, arithmetic and copies ran while one was open for 10% -> 8% of each run, Pallas kernels for 29% -> 29%
where the time goes in v4:
time: 247 us; the launch traced here: 246 us
  waiting for transfers between devices  74.9 us (30%)
  Pallas kernels  72.2 us (29%)
  starting transfers between devices  60.1 us (24%)
  local copies, waits for them, and re-layouts  30.4 us (12%)
  other arithmetic  6.73 us (3%)
    ppermute x28, waiting for transfers between devices, along(): return lax.ppermute(value, 'req', pairs)  53.1 us
    ppermute x28, starting transfers between devices, along(): return lax.ppermute(value, 'req', pairs)  38 us
    pallas_call x2, Pallas kernels, project(): pl.pallas_call(functools.partial(project_kernel, is_q), in_specs=[in_smem...  19.6 us
    unnamed x129, local copies, waits for them, and re-layouts  19.1 us
    ppermute x12, waiting for transfers between devices, to_blocks(): lax.ppermute(piece, 'mlp', [(b, b ^ k) for b in range(BLOCKS)])  17.8 us
    pallas_call x3, Pallas kernels, project_columns(): pl.pallas_call(functools.partial(columns_kernel, len(chunks)), in_specs=[...  14.9 us
    ppermute x12, starting transfers between devices, to_blocks(): lax.ppermute(piece, 'mlp', [(b, b ^ k) for b in range(BLOCKS)])  14.1 us
    pallas_call x2, Pallas kernels, norm_rows(): pl.pallas_call(norm_kernel, grid_spec=pltpu.PrefetchScalarGridSpec(num_sc...  11.7 us
  transfers between devices with their start and end apart: 46, of which 17 were waited for; matrix products, arithmetic and copies ran while one was open for 8% of the time, Pallas kernels for 29%

profile of v4, /device:TPU:0, one launch (start us, length us, event | category | flops | bytes accessed | tf_op | source)
XLA Modules:
  0.0 245.8 jit_solution(6400040519274858084)
XLA Ops:
  0.6 3.0 %collective-permute-start.1 = (bf16[384,1024]{1,0:T(8,128)(2,1)}, bf16[384,1024]{1,0:T(8,128)(2,1)}, u32[]{:S(2)}, u32[]{:S(2)}) collective-permute-start(bf16[384,1024]{1,0:T(8,128)(2,1)} %p0.1), channel_id=1, source_target_pairs={{0,2},{1,3},{2,0},{3,1},{4,6},{5,7},{6,4},{7,5},{8,10},{9,11},{10,... | collective-permute-start | bytes 2359304 | tf_op jit(solution)/shard_map/ppermute | solution.py:250
  5.2 4.4 %collective-permute-start = (bf16[384,1024]{1,0:T(8,128)(2,1)}, bf16[384,1024]{1,0:T(8,128)(2,1)}, u32[]{:S(2)}, u32[]{:S(2)}) collective-permute-start(bf16[384,1024]{1,0:T(8,128)(2,1)} %p0.1), channel_id=1, source_target_pairs={{0,8},{4,12},{24,16},{28,20},{1,9},{5,13},{25,17},{29,21},{2,10},{... | collective-permute-start | bytes 2359304 | tf_op jit(solution)/shard_map/ppermute | solution.py:246
  19.2 2.4 pack_rows.1.refs_0_
  27.8 8.9 %collective-permute-start.4 = (bf16[512,1024]{1,0:T(8,128)(2,1)S(1)}, bf16[512,1024]{1,0:T(8,128)(2,1)S(1)}, u32[]{:S(2)}, u32[]{:S(2)}) collective-permute-start(bf16[512,1024]{1,0:T(8,128)(2,1)S(1)} %get-tuple-element.60.refs_0_), channel_id=1, source_target_pairs={{0,8},{4,12},{24,16},{28,20},{1,9},{5,13},{25,17},{29,21},{2,10},{... | collective-permute-start | bytes 3145736 | tf_op jit(solution)/shard_map/ppermute | solution.py:246
  38.7 20.9 %collective-permute-done.4.refs_0_ = bf16[512,1024]{1,0:T(8,128)(2,1)S(1)} collective-permute-done((bf16[512,1024]{1,0:T(8,128)(2,1)S(1)}, bf16[512,1024]{1,0:T(8,128)(2,1)S(1)}, u32[]{:S(2)}, u32[]{:S(2)}) %collective-permute-start.4) | collective-permute-done | bytes 1048608 | tf_op jit(solution)/shard_map/ppermute | solution.py:246
  59.7 2.8 %collective-permute-done.9.refs_6_.refs_5_ = bf16[512,1024]{1,0:T(8,128)(2,1)S(1)} collective-permute-done((bf16[512,1024]{1,0:T(8,128)(2,1)}, bf16[512,1024]{1,0:T(8,128)(2,1)S(1)}, u32[]{:S(2)}, u32[]{:S(2)}) %collective-permute-start.9) | collective-permute-done | bytes 1048608 | tf_op jit(solution)/shard_map/ppermute | solution.py:246
  62.5 2.3 collective-permute-done.6.refs_2_
  65.2 3.9 %collective-permute-start.13 = (bf16[512,1024]{1,0:T(8,128)(2,1)S(1)}, bf16[512,1024]{1,0:T(8,128)(2,1)}, u32[]{:S(2)}, u32[]{:S(2)}) collective-permute-start(bf16[512,1024]{1,0:T(8,128)(2,1)S(1)} %get-tuple-element.70), channel_id=1, source_target_pairs={{0,8},{4,12},{24,16},{28,20},{1,9},{5,13},{25,17},{29,21},{2,10},{... | collective-permute-start | bytes 3145736 | tf_op jit(solution)/shard_map/ppermute | solution.py:246
  75.8 5.8 %norm_rows.2 = (bf16[768,4096]{1,0:T(8,128)(2,1)}, f32[8,128]{1,0:T(8,128)}) custom-call(s32[15]{0:T(128)} %stack.61.place, f32[4,1024]{1,0:T(4,128)} %reshape.49.gain, bf16[384,1024]{1,0:T(8,128)(2,1)} %p0.1, bf16[384,1024]{1,0:T(8,128)(2,1)} %collective-permute-done.2.p1, bf16[384,1024]{1,0:T(8,128)(2,1)} %collective-permute-done.1.p2, ...), custom_call_target="tpu_custom_call" | custom-call | flops 6291456 | bytes 6291456 | tf_op jit(solution)/shard_map/norm_rows/pallas_call | solution.py:349
  83.7 5.9 %norm_rows.3 = (bf16[768,4096]{1,0:T(8,128)(2,1)}, f32[8,128]{1,0:T(8,128)}) custom-call(s32[15]{0:T(128)} %stack.61.place, f32[4,1024]{1,0:T(4,128)} %reshape.49.gain, bf16[384,1024]{1,0:T(8,128)(2,1)} %collective-permute-done.p0, bf16[576,1024]{1,0:T(8,128)(2,1)} %copy-done.9, bf16[576,1024]{1,0:T(8,128)(2,1)} %copy-done.10, ...), custom_call_target="tpu_custom_call", output_to_operand_aliasing={{0}: (7, {})} | custom-call | flops 6291456 | bytes 6291456 | tf_op jit(solution)/shard_map/norm_rows/pallas_call | solution.py:349
  92.8 6.7 %collective-permute-start.20 = (bf16[4,1024,128]{2,1,0:T(8,128)(2,1)S(1)}, bf16[4,1024,128]{2,1,0:T(8,128)(2,1)S(1)}, u32[]{:S(2)}, u32[]{:S(2)}) collective-permute-start(bf16[4,1024,128]{2,1,0:T(8,128)(2,1)S(1)} %get-tuple-element.79.refs_1_), channel_id=1, source_target_pairs={{0,8},{4,12},{8,0},{12,4},{16,24},{20,28},{24,16},{28,20},{1,9},{5... | collective-permute-start | bytes 3145736 | tf_op jit(solution)/shard_map/ppermute | solution.py:246
  101.5 7.1 %rank_terms.1 = (bf16[48,768]{1,0:T(8,128)(2,1)}, bf16[4,32,1024]{2,1,0:T(8,128)(2,1)}, bf16[4,32,1024]{2,1,0:T(8,128)(2,1)}, bf16[256,1024]{1,0:T(8,128)(2,1)}, bf16[256,512]{1,0:T(8,128)(2,1)}) custom-call(s32[15]{0:T(128)} %stack.61.place, s32[8]{0:T(128)} %pad_add_fusion.table.own_table, s32[8]{0:T(128)} %bitcast_convert_fusion.2.end_table, s32[16]{0:T(128)} %storage.5, ...), custom_call_target="tpu_custom_call" | custom-call | flops 1207959552 | bytes 6815744 | tf_op jit(solution)/shard_map/rank_terms/pallas_call | solution.py:462
  115.9 7.5 %project_key_value.1 = (bf16[384,512]{1,0:T(8,128)(2,1)}, bf16[640,512]{1,0:T(8,128)(2,1)}) custom-call(s32[15]{0:T(128)} %stack.61.place, s32[8]{0:T(128)} %pad_add_fusion.table.own_table, s32[8]{0:T(128)} %bitcast_convert_fusion.2.end_table, s32[16]{0:T(128)} %storage.5, bf16[768,4096]{1,0:T(8,128)(2,1)} %get-tuple-element.69.x, ...), custom_call_target="tpu_custom_call" | custom-call | flops 3422552064 | bytes 11272192 | tf_op jit(solution)/shard_map/project_key_value/pallas_call | solution.py:561
  129.5 12.0 %project_query.1 = (bf16[384,1024]{1,0:T(8,128)(2,1)}, bf16[384,1024]{1,0:T(8,128)(2,1)}) custom-call(s32[15]{0:T(128)} %stack.61.place, s32[8]{0:T(128)} %pad_add_fusion.table.own_table, s32[8]{0:T(128)} %bitcast_convert_fusion.2.end_table, s32[16]{0:T(128)} %storage.5, bf16[768,4096]{1,0:T(8,128)(2,1)} %get-tuple-element.69.x, bf16[512,1024]{1,0:T(8,128)(2,1)} %refs_0_.1, ...), custom_call_target="tpu_custom_call" | custom-call | flops 6845104128 | bytes 16252928 | tf_op jit(solution)/shard_map/project_query/pallas_call | solution.py:561
  146.0 19.2 %collective-permute-done.27.refs_1_ = bf16[384,1024]{1,0:T(8,128)(2,1)S(1)} collective-permute-done((bf16[384,1024]{1,0:T(8,128)(2,1)}, bf16[384,1024]{1,0:T(8,128)(2,1)S(1)}, u32[]{:S(2)}, u32[]{:S(2)}) %collective-permute-start.27) | collective-permute-done | bytes 786464 | tf_op jit(solution)/shard_map/ppermute | solution.py:246
  168.7 11.5 %attend.1 = (bf16[384,1024]{1,0:T(8,128)(2,1)}, bf16[384,512]{1,0:T(8,128)(2,1)}, f32[16,384]{1,0:T(8,128)}) custom-call(s32[15]{0:T(128)} %stack.61.place, s32[8]{0:T(128)} %pad_add_fusion.table.own_table, s32[4]{0:T(128)} %bitcast.50, s32[32]{0:T(128)} %reshape_squeeze.3.pages, bf16[384,1024]{1,0:T(8,128)(2,1)} %get-tuple-element.89.own, ...), custom_call_target="tpu_custom_call" | custom-call | flops 1409286144 | bytes 2359296 | tf_op jit(solution)/shard_map/attend/pallas_call | solution.py:683
  184.5 5.5 %project_columns.3 = (bf16[400,512]{1,0:T(8,128)(2,1)}, bf16[400,512]{1,0:T(8,128)(2,1)}, bf16[400,512]{1,0:T(8,128)(2,1)}, bf16[400,512]{1,0:T(8,128)(2,1)}) custom-call(s32[15]{0:T(128)} %stack.61.place, bf16[384,1024]{1,0:T(8,128)(2,1)} %copy-done.12, bf16[4,1024,128]{2,1,0:T(8,128)(2,1)} %copy-done.2, bf16[4,1024,128]{2,1,0:T(8,128)(2,1)} %copy-done.16, ...), custom_call_target="tpu_custom_call" | custom-call | flops 1677721600 | bytes 6651904 | tf_op jit(solution)/shard_map/project_columns/pallas_call | solution.py:758
  200.2 5.0 %project_columns.4 = (bf16[384,256]{1,0:T(8,128)(2,1)}, bf16[384,256]{1,0:T(8,128)(2,1)}, bf16[384,256]{1,0:T(8,128)(2,1)}, bf16[384,256]{1,0:T(8,128)(2,1)}) custom-call(s32[15]{0:T(128)} %stack.61.place, bf16[384,1024]{1,0:T(8,128)(2,1)} %copy-done.12, bf16[4,1024,128]{2,1,0:T(8,128)(2,1)} %gate.16.refs_0_, bf16[4,1024,128]{2,1,0:T(8,128)(2,1)} %copy-done.45, ...), custom_call_target="tpu_custom_call" | custom-call | flops 805306368 | bytes 3670016 | tf_op jit(solution)/shard_map/project_columns/pallas_call | solution.py:758
  205.2 2.9 %collective-permute-done.31.refs_1_.refs_2_ = bf16[400,512]{1,0:T(8,128)(2,1)S(1)} collective-permute-done((bf16[400,512]{1,0:T(8,128)(2,1)S(1)}, bf16[400,512]{1,0:T(8,128)(2,1)S(1)}, u32[]{:S(2)}, u32[]{:S(2)}) %collective-permute-start.31) | collective-permute-done | bytes 409632 | tf_op jit(solution)/shard_map/ppermute | solution.py:255
  208.2 8.1 %collective-permute-done.32.refs_2_.refs_3_ = bf16[400,512]{1,0:T(8,128)(2,1)S(1)} collective-permute-done((bf16[400,512]{1,0:T(8,128)(2,1)S(1)}, bf16[400,512]{1,0:T(8,128)(2,1)S(1)}, u32[]{:S(2)}, u32[]{:S(2)}) %collective-permute-start.32) | collective-permute-done | bytes 409632 | tf_op jit(solution)/shard_map/ppermute | solution.py:255
  216.3 4.6 %collective-permute-done.40.refs_0_ = bf16[4,1024,128]{2,1,0:T(8,128)(2,1)S(1)} collective-permute-done((bf16[4,1024,128]{2,1,0:T(8,128)(2,1)S(1)}, bf16[4,1024,128]{2,1,0:T(8,128)(2,1)S(1)}, u32[]{:S(2)}, u32[]{:S(2)}) %collective-permute-start.40) | collective-permute-done | bytes 1048608 | tf_op jit(solution)/shard_map/ppermute | solution.py:246
  226.2 4.4 %project_columns.5 = (bf16[384,256]{1,0:T(8,128)(2,1)S(1)}, bf16[384,256]{1,0:T(8,128)(2,1)S(1)}, bf16[384,256]{1,0:T(8,128)(2,1)S(1)}, bf16[384,256]{1,0:T(8,128)(2,1)S(1)}) custom-call(s32[15]{0:T(128)S(1)} %copy-done.38, bf16[384,1024]{1,0:T(8,128)(2,1)S(1)} %copy-done.13, bf16[4,1024,128]{2,1,0:T(8,128)(2,1)S(1)} %gate.17.refs_0_, ...), custom_call_target="tpu_custom_call" | custom-call | flops 805306368 | bytes 3670016 | tf_op jit(solution)/shard_map/project_columns/pallas_call | solution.py:758
  236.0 3.5 %sum_columns.1 = (bf16[384,1024]{1,0:T(8,128)(2,1)}, f32[384,256]{1,0:T(8,128)}) custom-call(s32[15]{0:T(128)} %stack.61.place, s32[8]{0:T(128)} %pad_add_fusion.table.own_table, bf16[4,32,1024]{2,1,0:T(8,128)(2,1)} %get-tuple-element.77.chosen_own, bf16[640,512]{1,0:T(8,128)(2,1)} %copy-done.23, bf16[400,512]{1,0:T(8,128)(2,1)} %get-tuple-element.101.refs_1_.refs_0_, ...), custom_call_target="tpu_custom_call" | custom-call | flops 56623104 | bytes 4718592 | tf_op jit(solution)/shard_map/sum_columns/pallas_call | solution.py:808
  239.6 3.5 %collective-permute-done.44.p2 = bf16[384,256]{1,0:T(8,128)(2,1)S(1)} collective-permute-done((bf16[384,256]{1,0:T(8,128)(2,1)S(1)}, bf16[384,256]{1,0:T(8,128)(2,1)S(1)}, u32[]{:S(2)}, u32[]{:S(2)}) %collective-permute-start.44) | collective-permute-done | bytes 196640 | tf_op jit(solution)/shard_map/ppermute | solution.py:255
  (244 shorter events, 82.6 us)
Async XLA Ops:
  0.6 23.4 %collective-permute-start.1 = (bf16[384,1024]{1,0:T(8,128)(2,1)}, bf16[384,1024]{1,0:T(8,128)(2,1)}, u32[]{:S(2)}, u32[]{:S(2)}) collective-permute-start(bf16[384,1024]{1,0:T(8,128)(2,1)} %p0.1), channel_id=1, source_target_pairs={{0,2},{1,3},{2,0},{3,1},{4,6},{5,7},{6,4},{7,5},{8,10},{9,11},{10,... | collective-permute-start | bytes 2359304 | tf_op jit(solution)/shard_map/ppermute | solution.py:250
  3.7 21.4 %collective-permute-start.2 = (bf16[384,1024]{1,0:T(8,128)(2,1)}, bf16[384,1024]{1,0:T(8,128)(2,1)}, u32[]{:S(2)}, u32[]{:S(2)}) collective-permute-start(bf16[384,1024]{1,0:T(8,128)(2,1)} %p0.1), channel_id=1, source_target_pairs={{0,1},{1,0},{2,3},{3,2},{4,5},{5,4},{6,7},{7,6},{8,9},{9,8},{10,11... | collective-permute-start | bytes 2359304 | tf_op jit(solution)/shard_map/ppermute | solution.py:250
  5.2 20.9 %collective-permute-start = (bf16[384,1024]{1,0:T(8,128)(2,1)}, bf16[384,1024]{1,0:T(8,128)(2,1)}, u32[]{:S(2)}, u32[]{:S(2)}) collective-permute-start(bf16[384,1024]{1,0:T(8,128)(2,1)} %p0.1), channel_id=1, source_target_pairs={{0,8},{4,12},{24,16},{28,20},{1,9},{5,13},{25,17},{29,21},{2,10},{... | collective-permute-start | bytes 2359304 | tf_op jit(solution)/shard_map/ppermute | solution.py:246
  9.6 18.1 %collective-permute-start.3 = (bf16[512,1024]{1,0:T(8,128)(2,1)}, bf16[512,1024]{1,0:T(8,128)(2,1)}, u32[]{:S(2)}, u32[]{:S(2)}) collective-permute-start(bf16[512,1024]{1,0:T(8,128)(2,1)} %refs_0_.1), channel_id=1, source_target_pairs={{8,16},{12,20},{16,8},{20,12},{9,17},{13,21},{17,9},{21,13},{10,18... | collective-permute-start | bytes 3145736 | tf_op jit(solution)/shard_map/ppermute | solution.py:246
  27.8 31.8 %collective-permute-start.4 = (bf16[512,1024]{1,0:T(8,128)(2,1)S(1)}, bf16[512,1024]{1,0:T(8,128)(2,1)S(1)}, u32[]{:S(2)}, u32[]{:S(2)}) collective-permute-start(bf16[512,1024]{1,0:T(8,128)(2,1)S(1)} %get-tuple-element.60.refs_0_), channel_id=1, source_target_pairs={{0,8},{4,12},{24,16},{28,20},{1,9},{5,13},{25,17},{29,21},{2,10},{... | collective-permute-start | bytes 3145736 | tf_op jit(solution)/shard_map/ppermute | solution.py:246
  36.7 28.1 %collective-permute-start.6 = (bf16[576,1024]{1,0:T(8,128)(2,1)S(1)}, bf16[576,1024]{1,0:T(8,128)(2,1)S(1)}, u32[]{:S(2)}, u32[]{:S(2)}) collective-permute-start(bf16[576,1024]{1,0:T(8,128)(2,1)S(1)} %get-tuple-element.61), channel_id=1, source_target_pairs={{0,1},{1,0},{2,3},{3,2},{4,5},{5,4},{6,7},{7,6},{8,9},{9,8},{10,11... | collective-permute-start | bytes 3538952 | tf_op jit(solution)/shard_map/ppermute | solution.py:250
  37.3 27.8 %collective-permute-start.7 = (bf16[576,1024]{1,0:T(8,128)(2,1)S(1)}, bf16[576,1024]{1,0:T(8,128)(2,1)S(1)}, u32[]{:S(2)}, u32[]{:S(2)}) collective-permute-start(bf16[576,1024]{1,0:T(8,128)(2,1)S(1)} %get-tuple-element.62), channel_id=1, source_target_pairs={{0,2},{1,3},{2,0},{3,1},{4,6},{5,7},{6,4},{7,5},{8,10},{9,11},{10,... | collective-permute-start | bytes 3538952 | tf_op jit(solution)/shard_map/ppermute | solution.py:250
  37.9 21.8 %collective-permute-start.5 = (bf16[512,1024]{1,0:T(8,128)(2,1)S(1)}, bf16[512,1024]{1,0:T(8,128)(2,1)S(1)}, u32[]{:S(2)}, u32[]{:S(2)}) collective-permute-start(bf16[512,1024]{1,0:T(8,128)(2,1)S(1)} %get-tuple-element.60.refs_0_), channel_id=1, source_target_pairs={{8,16},{12,20},{16,8},{20,12},{9,17},{13,21},{17,9},{21,13},{10,18... | collective-permute-start | bytes 3145736 | tf_op jit(solution)/shard_map/ppermute | solution.py:246
  38.7 21.0 %collective-permute-start.8 = (bf16[512,1024]{1,0:T(8,128)(2,1)S(1)}, bf16[512,1024]{1,0:T(8,128)(2,1)S(1)}, u32[]{:S(2)}, u32[]{:S(2)}) collective-permute-start(bf16[512,1024]{1,0:T(8,128)(2,1)S(1)} %get-tuple-element.63.refs_4_), channel_id=1, source_target_pairs={{0,4},{4,0},{8,12},{12,8},{16,20},{20,16},{24,28},{28,24},{1,5},{5... | collective-permute-start | bytes 3145736 | tf_op jit(solution)/shard_map/ppermute | solution.py:246
  65.2 25.6 %collective-permute-start.13 = (bf16[512,1024]{1,0:T(8,128)(2,1)S(1)}, bf16[512,1024]{1,0:T(8,128)(2,1)}, u32[]{:S(2)}, u32[]{:S(2)}) collective-permute-start(bf16[512,1024]{1,0:T(8,128)(2,1)S(1)} %get-tuple-element.70), channel_id=1, source_target_pairs={{0,8},{4,12},{24,16},{28,20},{1,9},{5,13},{25,17},{29,21},{2,10},{... | collective-permute-start | bytes 3145736 | tf_op jit(solution)/shard_map/ppermute | solution.py:246
  69.1 21.7 %collective-permute-start.14 = (bf16[512,1024]{1,0:T(8,128)(2,1)S(1)}, bf16[512,1024]{1,0:T(8,128)(2,1)}, u32[]{:S(2)}, u32[]{:S(2)}) collective-permute-start(bf16[512,1024]{1,0:T(8,128)(2,1)S(1)} %get-tuple-element.65.refs_1_), channel_id=1, source_target_pairs={{8,16},{12,20},{16,8},{20,12},{9,17},{13,21},{17,9},{21,13},{10,18... | collective-permute-start | bytes 3145736 | tf_op jit(solution)/shard_map/ppermute | solution.py:246
  92.1 31.4 %collective-permute-start.19 = (bf16[512,1024]{1,0:T(8,128)(2,1)}, bf16[512,1024]{1,0:T(8,128)(2,1)S(1)}, u32[]{:S(2)}, u32[]{:S(2)}) collective-permute-start(bf16[512,1024]{1,0:T(8,128)(2,1)} %get-tuple-element.78.refs_2_), channel_id=1, source_target_pairs={{8,16},{12,20},{16,8},{20,12},{9,17},{13,21},{17,9},{21,13},{10,18... | collective-permute-start | bytes 3145736 | tf_op jit(solution)/shard_map/ppermute | solution.py:246
  92.8 30.7 %collective-permute-start.20 = (bf16[4,1024,128]{2,1,0:T(8,128)(2,1)S(1)}, bf16[4,1024,128]{2,1,0:T(8,128)(2,1)S(1)}, u32[]{:S(2)}, u32[]{:S(2)}) collective-permute-start(bf16[4,1024,128]{2,1,0:T(8,128)(2,1)S(1)} %get-tuple-element.79.refs_1_), channel_id=1, source_target_pairs={{0,8},{4,12},{8,0},{12,4},{16,24},{20,28},{24,16},{28,20},{1,9},{5... | collective-permute-start | bytes 3145736 | tf_op jit(solution)/shard_map/ppermute | solution.py:246
  124.5 19.2 %collective-permute-start.25 = (bf16[640,512]{1,0:T(8,128)(2,1)}, bf16[640,512]{1,0:T(8,128)(2,1)S(1)}, u32[]{:S(2)}, u32[]{:S(2)}) collective-permute-start(bf16[640,512]{1,0:T(8,128)(2,1)} %get-tuple-element.87), channel_id=1, source_target_pairs={{8,0},{12,4},{16,24},{20,28},{9,1},{13,5},{17,25},{21,29},{10,2},{... | collective-permute-start | bytes 1966088 | tf_op jit(solution)/shard_map/ppermute | solution.py:246
  126.0 19.9 %collective-permute-start.26 = (bf16[4,1024,128]{2,1,0:T(8,128)(2,1)S(1)}, bf16[4,1024,128]{2,1,0:T(8,128)(2,1)}, u32[]{:S(2)}, u32[]{:S(2)}) collective-permute-start(bf16[4,1024,128]{2,1,0:T(8,128)(2,1)S(1)} %get-tuple-element.90.refs_0_.refs_2_), channel_id=1, source_target_pairs={{8,16},{12,20},{16,8},{20,12},{9,17},{13,21},{17,9},{21,13},{10,18... | collective-permute-start | bytes 3145736 | tf_op jit(solution)/shard_map/ppermute | solution.py:246
  127.7 18.2 %collective-permute-start.28 = (bf16[4,1024,128]{2,1,0:T(8,128)(2,1)S(1)}, bf16[4,1024,128]{2,1,0:T(8,128)(2,1)S(1)}, u32[]{:S(2)}, u32[]{:S(2)}) collective-permute-start(bf16[4,1024,128]{2,1,0:T(8,128)(2,1)S(1)} %get-tuple-element.90.refs_0_.refs_2_), channel_id=1, source_target_pairs={{0,4},{4,0},{8,12},{12,8},{16,20},{20,16},{24,28},{28,24},{1,5},{5... | collective-permute-start | bytes 3145736 | tf_op jit(solution)/shard_map/ppermute | solution.py:246
  128.2 17.8 %collective-permute-start.29 = (bf16[4,1024,128]{2,1,0:T(8,128)(2,1)S(1)}, bf16[4,1024,128]{2,1,0:T(8,128)(2,1)S(1)}, u32[]{:S(2)}, u32[]{:S(2)}) collective-permute-start(bf16[4,1024,128]{2,1,0:T(8,128)(2,1)S(1)} %get-tuple-element.92.refs_4_.refs_6_), channel_id=1, source_target_pairs={{0,4},{4,0},{8,12},{12,8},{16,20},{20,16},{24,28},{28,24},{1,5},{5... | collective-permute-start | bytes 3145736 | tf_op jit(solution)/shard_map/ppermute | solution.py:246
  143.8 21.4 %collective-permute-start.27 = (bf16[384,1024]{1,0:T(8,128)(2,1)}, bf16[384,1024]{1,0:T(8,128)(2,1)S(1)}, u32[]{:S(2)}, u32[]{:S(2)}) collective-permute-start(bf16[384,1024]{1,0:T(8,128)(2,1)} %get-tuple-element.91), channel_id=1, source_target_pairs={{8,0},{12,4},{16,24},{20,28},{9,1},{13,5},{17,25},{21,29},{10,2},{... | collective-permute-start | bytes 2359304 | tf_op jit(solution)/shard_map/ppermute | solution.py:246
  145.2 35.0 %collective-permute-start.30 = (bf16[4,1024,128]{2,1,0:T(8,128)(2,1)S(1)}, bf16[4,1024,128]{2,1,0:T(8,128)(2,1)S(1)}, u32[]{:S(2)}, u32[]{:S(2)}) collective-permute-start(bf16[4,1024,128]{2,1,0:T(8,128)(2,1)S(1)} %get-tuple-element.92.refs_4_.refs_6_), channel_id=1, source_target_pairs={{8,16},{12,20},{16,8},{20,12},{9,17},{13,21},{17,9},{21,13},{10,18... | collective-permute-start | bytes 3145736 | tf_op jit(solution)/shard_map/ppermute | solution.py:246
  166.1 26.1 %collective-permute-start.34 = (bf16[4,1024,128]{2,1,0:T(8,128)(2,1)}, bf16[4,1024,128]{2,1,0:T(8,128)(2,1)}, u32[]{:S(2)}, u32[]{:S(2)}) collective-permute-start(bf16[4,1024,128]{2,1,0:T(8,128)(2,1)} %get-tuple-element.105.refs_2_), channel_id=1, source_target_pairs={{8,0},{12,4},{16,24},{20,28},{9,1},{13,5},{17,25},{21,29},{10,2},{... | collective-permute-start | bytes 3145736 | tf_op jit(solution)/shard_map/ppermute | solution.py:246
  167.4 31.2 %collective-permute-start.36 = (bf16[4,1024,128]{2,1,0:T(8,128)(2,1)}, bf16[4,1024,128]{2,1,0:T(8,128)(2,1)}, u32[]{:S(2)}, u32[]{:S(2)}) collective-permute-start(bf16[4,1024,128]{2,1,0:T(8,128)(2,1)} %get-tuple-element.105.refs_2_), channel_id=1, source_target_pairs={{0,4},{4,0},{8,12},{12,8},{16,20},{20,16},{24,28},{28,24},{1,5},{5... | collective-permute-start | bytes 3145736 | tf_op jit(solution)/shard_map/ppermute | solution.py:246
  194.4 26.5 %collective-permute-start.40 = (bf16[4,1024,128]{2,1,0:T(8,128)(2,1)S(1)}, bf16[4,1024,128]{2,1,0:T(8,128)(2,1)S(1)}, u32[]{:S(2)}, u32[]{:S(2)}) collective-permute-start(bf16[4,1024,128]{2,1,0:T(8,128)(2,1)S(1)} %copy-done.21), channel_id=1, source_target_pairs={{8,0},{12,4},{16,24},{20,28},{9,1},{13,5},{17,25},{21,29},{10,2},{... | collective-permute-start | bytes 3145736 | tf_op jit(solution)/shard_map/ppermute | solution.py:246
  197.0 19.2 %collective-permute-start.32 = (bf16[400,512]{1,0:T(8,128)(2,1)S(1)}, bf16[400,512]{1,0:T(8,128)(2,1)S(1)}, u32[]{:S(2)}, u32[]{:S(2)}) collective-permute-start(bf16[400,512]{1,0:T(8,128)(2,1)S(1)} %copy-done.60), channel_id=1, source_target_pairs={{0,2},{1,3},{2,0},{3,1},{4,6},{5,7},{6,4},{7,5},{8,10},{9,11},{10,... | collective-permute-start | bytes 1228808 | tf_op jit(solution)/shard_map/ppermute | solution.py:255
  199.3 27.0 %collective-permute-start.42 = (bf16[4,1024,128]{2,1,0:T(8,128)(2,1)S(1)}, bf16[4,1024,128]{2,1,0:T(8,128)(2,1)S(1)}, u32[]{:S(2)}, u32[]{:S(2)}) collective-permute-start(bf16[4,1024,128]{2,1,0:T(8,128)(2,1)S(1)} %copy-done.21), channel_id=1, source_target_pairs={{0,4},{4,0},{8,12},{12,8},{16,20},{20,16},{24,28},{28,24},{1,5},{5... | collective-permute-start | bytes 3145736 | tf_op jit(solution)/shard_map/ppermute | solution.py:246
  (85 other events, 753.7 us)
